TPU v7x, 128 devices: a whole 4x4x4 slice. The times are simulated.
128 devices in a mesh: cx: 16 (over z, x), cy: 8 (over y, core).
Axes of the slice: x: 4, y: 4, z: 4, core: 2. Of those that a mesh axis runs over, the one named last changes fastest.
Arguments:
- cell_pos: float32 [64, 32, 3, 1024], P('cx', 'cy'), may hold values from -6 to 6
- cell_drag: float32 [64, 32], P('cx', 'cy'), may hold values from 0.2 to 2
- cell_near: int32 [64, 32, 2], P('cx', 'cy'), may hold values from 0 to 2047, as said below
- analysis: bfloat16 [1024, 1024], replicated, may hold values from -0.1875 to 0.1875
- stiffness: float32 [1024], replicated, may hold values from 0.1 to 1
- synthesis: bfloat16 [1024, 1024], replicated, may hold values from -0.1875 to 0.1875
- wall_pos: float32 [1024, 3, 256], P(('cx', 'cy')), may hold values from -9 to 9
- wall_normal: float32 [1024, 3, 256], P(('cx', 'cy')), may hold values from -6 to 6
- wall_weight: float32 [1024, 256], P(('cx', 'cy')), may hold values from 0.02 to 0.2
- density: float32 [1024, 3, 256], P(('cx', 'cy')), may hold values from -6 to 6
- patch_near: int32 [1024, 4], P(('cx', 'cy')), may hold values from 0 to 1023, as said below
- cell_to_patch: int32 [1024, 2], P(('cx', 'cy')), may hold values from 0 to 2047, as said below
Outputs:
- moved_cells: float32 [64, 32, 3, 1024], P('cx', 'cy')
- density_next: float32 [1024, 3, 256], P(('cx', 'cy'))
Inputs may be any that keep to these rules, and one draw needn't show every extreme that they name: `cell_near`: each entry is the row-major index (row times 32 plus column) of a cell whose grid row and column differ from the listing cell's by at most 3 each, cyclically, and never the listing cell itself. `cell_to_patch`: for the patches of block b (patches b * 8 to b * 8 + 7), with b = i * 8 + j, each entry is the row-major index of a cell whose row lies within 3 of the rows i * 4 to i * 4 + 3 and whose column lies within 3 of the columns j * 4 to j * 4 + 3, cyclically. `patch_near`: each entry is a patch of the listing patch's block of 8 or of the two blocks beside it, cyclically, and never the listing patch itself.
All inputs are finite; a program needn't handle non-finite values.
Results may differ from a plain program's by a relative error of at most 0.0041.
Values sent between devices are 32-bit elements; how exact they have to be, the bound alone decides.
No kernel may reach another device: no remote copies, remote signals or barrier semaphores. Data moves between devices by JAX's collectives and lax.ppermute only.
A program may use at most 64 MiB of HBM per device.

v0:
```python
import functools
import math

import jax
import jax.numpy as jnp
from jax import lax
from jax.sharding import Mesh
from jax.sharding import PartitionSpec as P

HALO = 3
CX_CY = ("cx_0", "cx_1", "cy_0", "cy_1")
CX = ("cx_0", "cx_1")
CY = ("cy_0", "cy_1")


soften = 0.25
stokes_scale = 1.0 / (8.0 * math.pi)
layer_scale = 3.0 / (4.0 * math.pi)


def with_halo(value, sides, width):
    for axis, dim in sides:
        size, length = (lax.axis_size(axis), value.shape[dim])
        up = [(i, (i + 1) % size) for i in range(size)]
        down = [(j, i) for i, j in up]
        last = lax.slice_in_dim(value, length - width, length, axis=dim)
        initial = lax.slice_in_dim(value, 0, width, axis=dim)
        before = lax.ppermute(last, axis, up)
        after = lax.ppermute(initial, axis, down)
        value = jnp.concatenate([before, value, after], axis=dim)
    return value


def over_axes(value, axes):
    return functools.reduce(lax.pmax, axes, value)


def padded(value, sides, width):
    edges = {}
    for axis, dim in sides:
        size, length = (lax.axis_size(axis), value.shape[dim])
        up = [(i, (i + 1) % size) for i in range(size)]
        last = lax.slice_in_dim(value, length - width, length, axis=dim)
        initial = lax.slice_in_dim(value, 0, width, axis=dim)
        edges[dim] = (
            lax.ppermute(last, axis, up),
            lax.ppermute(initial, axis, [(b, a) for a, b in up]),
        )
    done = []
    for _, dim in sides:
        low, high = edges[dim]
        around = [(width, width) if d in done else (0, 0) for d in range(value.ndim)]
        value = jnp.concatenate([jnp.pad(low, around), value, jnp.pad(high, around)], axis=dim)
        done.append(dim)
    return value


def membrane(positions, analysis, stiffness, synthesis):
    points = positions.shape[-1]
    centred = positions - jnp.mean(positions, axis=-1, keepdims=True)
    flat = centred.reshape(-1, points).astype(jnp.bfloat16)
    coeff = jnp.dot(flat, analysis, preferred_element_type=jnp.float32)
    scaled = (coeff * stiffness[None, :]).astype(jnp.bfloat16)
    force = -jnp.dot(scaled, synthesis, preferred_element_type=jnp.float32)
    return force.reshape(positions.shape)


def stokeslet(targets, sources, forces):
    delta_x = targets[0][:, None] - sources[0][None, :]
    delta_y = targets[1][:, None] - sources[1][None, :]
    delta_z = targets[2][:, None] - sources[2][None, :]
    square = delta_x * delta_x + delta_y * delta_y + delta_z * delta_z + soften
    factor = lax.rsqrt(square) / square
    along = (
        delta_x * forces[0][None, :] + delta_y * forces[1][None, :] + delta_z * forces[2][None, :]
    )
    direct = (square + soften) * factor
    tangent = along * factor
    out_x = jnp.sum(direct * forces[0][None, :] + tangent * delta_x, axis=1)
    out_y = jnp.sum(direct * forces[1][None, :] + tangent * delta_y, axis=1)
    out_z = jnp.sum(direct * forces[2][None, :] + tangent * delta_z, axis=1)
    return stokes_scale * jnp.stack([out_x, out_y, out_z])


def double_layer(targets, sources, normals, weights, values):
    delta_x = targets[0][:, None] - sources[0][None, :]
    delta_y = targets[1][:, None] - sources[1][None, :]
    delta_z = targets[2][:, None] - sources[2][None, :]
    square = delta_x * delta_x + delta_y * delta_y + delta_z * delta_z + soften
    factor = lax.rsqrt(square) / (square * square)
    along_q = (
        delta_x * values[0][None, :] + delta_y * values[1][None, :] + delta_z * values[2][None, :]
    )
    along_n = (
        delta_x * normals[0][None, :]
        + delta_y * normals[1][None, :]
        + delta_z * normals[2][None, :]
    )
    scalar = -layer_scale * weights[None, :] * along_q * along_n * factor
    return jnp.stack(
        [
            jnp.sum(scalar * delta_x, axis=1),
            jnp.sum(scalar * delta_y, axis=1),
            jnp.sum(scalar * delta_z, axis=1),
        ]
    )


def spread_many(picked):
    leading = picked.shape[:-3]
    count = picked.shape[-3]
    moved = jnp.swapaxes(picked, -3, -2)
    return moved.reshape(leading + (3, count * picked.shape[-1]))


def local_slot(global_id, first_row, first_col, all_rows, all_cols, ext_cols):
    grid_row = global_id // all_cols
    grid_col = global_id % all_cols
    local_row = (grid_row - first_row + HALO) % all_rows
    local_col = (grid_col - first_col + HALO) % all_cols
    return local_row * ext_cols + local_col


def body(
    cell_pos,
    cell_drag,
    cell_near,
    analysis,
    stiffness,
    synthesis,
    wall_pos,
    wall_normal,
    wall_weight,
    density,
    patch_near,
    cell_to_patch,
):
    row_count = cell_pos.shape[0]
    col_count = cell_pos.shape[1]
    points = cell_pos.shape[3]
    own_force = membrane(cell_pos, analysis, stiffness, synthesis)
    stacked = jnp.concatenate([cell_pos, own_force], axis=2)
    extended = with_halo(stacked, ((CX, 0), (CY, 1)), HALO)
    ext_pos = extended[:, :, 0:3]
    ext_force = extended[:, :, 3:6]
    ext_cols = col_count + 2 * HALO
    flat_pos = ext_pos.reshape(-1, 3, points)
    flat_force = ext_force.reshape(-1, 3, points)
    all_rows = row_count * lax.axis_size(CX)
    all_cols = col_count * lax.axis_size(CY)
    first_row = lax.axis_index(CX) * row_count
    first_col = lax.axis_index(CY) * col_count
    near_slots = local_slot(cell_near, first_row, first_col, all_rows, all_cols, ext_cols)
    source_pos = spread_many(flat_pos[near_slots])
    source_force = spread_many(flat_force[near_slots])

    def one_row(pieces):
        return jax.vmap(stokeslet)(pieces[0], pieces[1], pieces[2])

    near = lax.map(one_row, (cell_pos, source_pos, source_force))
    velocity = cell_drag[:, :, None, None] * own_force + near
    speed = jnp.sqrt(jnp.sum(velocity * velocity, axis=2))
    top = over_axes(jnp.max(speed), CX_CY)
    step = 1.0 / (top + 1e-06)
    moved_cells = cell_pos + step * velocity
    patch_count = wall_pos.shape[0]
    wall_slots = local_slot(cell_to_patch, first_row, first_col, all_rows, all_cols, ext_cols)
    wall_source_pos = spread_many(flat_pos[wall_slots])
    wall_source_force = spread_many(flat_force[wall_slots])

    def wall_from_cells(pieces):
        return stokeslet(pieces[0], pieces[1], pieces[2])

    wall_velocity = lax.map(wall_from_cells, (wall_pos, wall_source_pos, wall_source_force))
    packed = jnp.concatenate([wall_pos, wall_normal, density, wall_weight[:, None, :]], axis=1)
    ext_wall = padded(packed, ((CX_CY, 0),), patch_count)
    all_patches = patch_count * lax.axis_size(CX_CY)
    block_start = lax.axis_index(CX_CY) * patch_count
    own_slots = jnp.arange(patch_count, dtype=jnp.int32) + patch_count
    other_slots = (patch_near - block_start + patch_count) % all_patches
    chosen = jnp.concatenate([own_slots[:, None], other_slots], axis=1)
    gathered = ext_wall[chosen]
    listed = gathered.shape[1]
    merged = jnp.swapaxes(gathered, 1, 2).reshape(patch_count, 10, listed * gathered.shape[-1])

    def layer_patch(pieces):
        target, sources = pieces
        return double_layer(target, sources[0:3], sources[3:6], sources[9], sources[6:9])

    layer = lax.map(layer_patch, (wall_pos, merged))
    density_next = 2.0 * layer + 2.0 * wall_velocity
    return (moved_cells, density_next)


def solution(mesh):
    torus = Mesh(mesh.devices.reshape(4, 4, 4, 2), ("cx_0", "cx_1", "cy_0", "cy_1"))
    return jax.shard_map(
        body,
        mesh=torus,
        in_specs=(
            P(CX, CY, None, None),
            P(CX, CY),
            P(CX, CY, None),
            P(),
            P(),
            P(),
            P(CX_CY, None, None),
            P(CX_CY, None, None),
            P(CX_CY, None),
            P(CX_CY, None, None),
            P(CX_CY, None),
            P(CX_CY, None),
        ),
        out_specs=(P(CX, CY, None, None), P(CX_CY, None, None)),
        check_vma=False,
    )
```

profile of v0, /device:TPU:0, one launch (start us, length us, event | category | flops | bytes accessed | tf_op | source)
XLA Modules:
  0.0 312.2 jit_solution(17841886247436861106)
XLA Ops:
  3.9 8.3 %collective-permute-start.5 = (f32[8,10,256]{2,1,0:T(8,128)S(1)}, f32[8,10,256]{2,1,0:T(8,128)S(1)}, u32[]{:S(2)}, u32[]{:S(2)}) collective-permute-start(f32[8,10,256]{2,1,0:T(8,128)S(1)} %pad_maximum_fusion.4), channel_id=1, source_target_pairs={{1,0},{2,1},{3,2},{4,3},{5,4},{6,5},{7,6},{8,7},{9,8},{10,9},{11,1... | collective-permute-start | bytes 245768 | tf_op jit(solution)/shard_map/ppermute | solution.py:47
  15.5 2.5 convolution_negate_fusion
  19.1 5.3 %collective-permute-start.1 = (f32[3,4,6,1024]{3,2,1,0:T(8,128)}, f32[3,4,6,1024]{3,2,1,0:T(8,128)}, u32[]{:S(2)}, u32[]{:S(2)}) collective-permute-start(f32[3,4,6,1024]{3,2,1,0:T(8,128)} %get-tuple-element.278), channel_id=1, source_target_pairs={{8,0},{16,8},{24,16},{32,24},{40,32},{48,40},{56,48},{64,56},{72,6... | collective-permute-start | bytes 884744 | tf_op jit(solution)/shard_map/ppermute | solution.py:29
  33.4 3.0 collective-permute-start.3
  36.4 24.2 %while.35 = (s32[]{:T(128)}, f32[8,3,256]{2,0,1:T(8,128)S(1)}, f32[8,10,1280]{2,0,1:T(8,128)}, f32[8,3,256]{2,0,1:T(8,128)S(1)}, s32[]{:T(128)}, /*index=5*/s32[...) while((s32[]{:T(128)}, f32[8,3,256]{2,0,1:T(8,128)S(1)}, ...), condition=%wide.region_16.17_spmd, body=%wide.region_12.16_spmd.sunk | while | flops 9832459 | bytes 184625 | solution.py:190
  37.5 1.8 fusion.82
  40.5 1.8 fusion.82
  60.6 2.2 pad_maximum_fusion
  62.7 2.7 fusion.69
  65.4 2.1 gather_fusion.3
  67.5 2.8 gather_fusion.4
  70.3 3.0 gather_fusion.1
  73.4 2.3 gather_fusion
  76.5 2.1 copy.154
  82.5 164.6 %while.34 = (s32[]{:T(128)}, f32[4,4,3,1024]{3,1,2,0:T(4,128)}, f32[4,4,3,1024]{3,1,2,0:T(4,128)S(1)}, f32[4,4,3,2048]{3,1,2,0:T(4,128)S(1)}, f32[4,4,3,2048]{3,1,2,0:T(4,128)S(1)}, /*index=5*/s32[]{:T(128)}) while((s32[]{:T(128)}, f32[4,4,3,1024]{3,1,2,0:T(4,128)}, f32[4,4,3,1024]{3,1,2,0:T(4,128)S(1)}, f32[4,4,3,2048]{3,1,2,0:T(4,128)S(1)}, ...), condition=%wide.region_5.6_spmd, body=%wide.region_1.5_spmd.sunk | while | flops 251682816 | bytes 1376845 | solution.py:160
  82.6 40.4 %fusion.79 = (f32[4,1024]{1,0:T(4,128)S(1)}, f32[4,1024]{1,0:T(4,128)S(1)}, f32[4,1024]{1,0:T(4,128)S(1)}) fusion(f32[4,2048]{1,0:T(4,128)S(1)} %get-tuple-element.400, f32[4,2048]{1,0:T(4,128)S(1)} %get-tuple-element.402, f32[4,1024]{1,0:T(4,128)S(1)} %get-tuple-element.403, f32[4,2048]{1,0:T(4,128)S(1)} %get-tuple-element.404, ...), kind=kLoop, calls=%fused_computation.21.clone.1 | loop fusion | flops 251645952 | bytes 294912 | tf_op jit(solution)/shard_map/while/body/eval_jaxpr/vmap()/reduce_sum | solution.py:79
  123.7 40.4 %fusion.79 = (f32[4,1024]{1,0:T(4,128)S(1)}, f32[4,1024]{1,0:T(4,128)S(1)}, f32[4,1024]{1,0:T(4,128)S(1)}) fusion(f32[4,2048]{1,0:T(4,128)S(1)} %get-tuple-element.400, f32[4,2048]{1,0:T(4,128)S(1)} %get-tuple-element.402, f32[4,1024]{1,0:T(4,128)S(1)} %get-tuple-element.403, f32[4,2048]{1,0:T(4,128)S(1)} %get-tuple-element.404, ...), kind=kLoop, calls=%fused_computation.21.clone.1 | loop fusion | flops 251645952 | bytes 294912 | tf_op jit(solution)/shard_map/while/body/eval_jaxpr/vmap()/reduce_sum | solution.py:79
  164.8 40.4 %fusion.79 = (f32[4,1024]{1,0:T(4,128)S(1)}, f32[4,1024]{1,0:T(4,128)S(1)}, f32[4,1024]{1,0:T(4,128)S(1)}) fusion(f32[4,2048]{1,0:T(4,128)S(1)} %get-tuple-element.400, f32[4,2048]{1,0:T(4,128)S(1)} %get-tuple-element.402, f32[4,1024]{1,0:T(4,128)S(1)} %get-tuple-element.403, f32[4,2048]{1,0:T(4,128)S(1)} %get-tuple-element.404, ...), kind=kLoop, calls=%fused_computation.21.clone.1 | loop fusion | flops 251645952 | bytes 294912 | tf_op jit(solution)/shard_map/while/body/eval_jaxpr/vmap()/reduce_sum | solution.py:79
  206.0 40.4 %fusion.79 = (f32[4,1024]{1,0:T(4,128)S(1)}, f32[4,1024]{1,0:T(4,128)S(1)}, f32[4,1024]{1,0:T(4,128)S(1)}) fusion(f32[4,2048]{1,0:T(4,128)S(1)} %get-tuple-element.400, f32[4,2048]{1,0:T(4,128)S(1)} %get-tuple-element.402, f32[4,1024]{1,0:T(4,128)S(1)} %get-tuple-element.403, f32[4,2048]{1,0:T(4,128)S(1)} %get-tuple-element.404, ...), kind=kLoop, calls=%fused_computation.21.clone.1 | loop fusion | flops 251645952 | bytes 294912 | tf_op jit(solution)/shard_map/while/body/eval_jaxpr/vmap()/reduce_sum | solution.py:79
  250.0 9.0 %pmax.28 = f32[]{:T(128)} all-reduce(f32[]{:T(128)} %sqrt_reduce_fusion), channel_id=1, replica_groups=mesh['cx_0'=4,'cx_1'=4,'cy_0'=4,'cy_1'=2] {'cx_0'}, use_global_device_ids=true, to_apply=%region_8.9 | all-reduce | flops 1 | bytes 8 | tf_op jit(solution)/shard_map/pmax | solution.py:35
  260.1 13.7 %pmax.29 = f32[]{:T(128)} all-reduce(f32[]{:T(128)} %pmax.28), channel_id=1, replica_groups=mesh['cx_0'=4,'cx_1'=4,'cy_0'=4,'cy_1'=2] {'cx_1'}, use_global_device_ids=true, to_apply=%region_9.10 | all-reduce | flops 1 | bytes 8 | tf_op jit(solution)/shard_map/pmax | solution.py:35
  274.0 8.4 %pmax.30 = f32[]{:T(128)} all-reduce(f32[]{:T(128)} %pmax.29), channel_id=1, replica_groups=mesh['cx_0'=4,'cx_1'=4,'cy_0'=4,'cy_1'=2] {'cy_0'}, use_global_device_ids=true, to_apply=%region_10.11 | all-reduce | flops 1 | bytes 8 | tf_op jit(solution)/shard_map/pmax | solution.py:35
  282.3 23.4 %while.36 = (s32[]{:T(128)}, f32[8,3,256]{2,0,1:T(8,128)S(1)}, f32[8,3,256]{2,0,1:T(8,128)S(1)}, f32[8,3,2048]{2,0,1:T(8,128)S(1)}, f32[8,3,2048]{2,0,1:T(8,128)S(1)}, /*index=5*/s32[]{:T(128)}, s32[]{:T(128)}, s32[]{}, s32[]{}) while((s32[]{:T(128)}, f32[8,3,256]{2,0,1:T(8,128)S(1)}, f32[8,3,256]{2,0,1:T(8,128)S(1)}, ...), condition=%wide.region_21.22_spmd, body=%wide.region_17.21_spmd.sunk | while | flops 15730180 | bytes 178321 | solution.py:174
  282.4 2.7 fusion.83
  285.3 2.7 fusion.83
  288.3 2.7 fusion.83
  291.2 2.7 fusion.83
  294.1 2.7 fusion.83
  297.0 2.7 fusion.83
  300.0 2.7 fusion.83
  302.9 2.7 fusion.83
  305.7 3.1 pmax.31
  (181 shorter events, 52.3 us)
Async XLA Ops:
  0.6 14.9 %copy-start = (bf16[1024,1024]{1,0:T(8,128)(2,1)S(1)}, bf16[1024,1024]{1,0:T(8,128)(2,1)}, u32[]{:S(2)}) copy-start(bf16[1024,1024]{1,0:T(8,128)(2,1)} %param.23) | copy-start | bytes 6291460
  3.8 21.4 %collective-permute-start.4 = (f32[8,10,256]{2,1,0:T(8,128)S(1)}, f32[8,10,256]{2,1,0:T(8,128)S(1)}, u32[]{:S(2)}, u32[]{:S(2)}) collective-permute-start(f32[8,10,256]{2,1,0:T(8,128)S(1)} %pad_maximum_fusion.4), channel_id=1, source_target_pairs={{0,1},{1,2},{2,3},{3,4},{4,5},{5,6},{6,7},{7,8},{8,9},{9,10},{10,1... | collective-permute-start | bytes 245768 | tf_op jit(solution)/shard_map/ppermute | solution.py:46
  3.9 21.3 %collective-permute-start.5 = (f32[8,10,256]{2,1,0:T(8,128)S(1)}, f32[8,10,256]{2,1,0:T(8,128)S(1)}, u32[]{:S(2)}, u32[]{:S(2)}) collective-permute-start(f32[8,10,256]{2,1,0:T(8,128)S(1)} %pad_maximum_fusion.4), channel_id=1, source_target_pairs={{1,0},{2,1},{3,2},{4,3},{5,4},{6,5},{7,6},{8,7},{9,8},{10,9},{11,1... | collective-permute-start | bytes 245768 | tf_op jit(solution)/shard_map/ppermute | solution.py:47
  15.5 9.0 %copy-start.6 = (s32[8,2]{0,1:T(2,128)S(1)}, s32[8,2]{0,1:T(2,128)}, u32[]{:S(2)}) copy-start(s32[8,2]{0,1:T(2,128)} %param.29) | copy-start | bytes 196
  15.5 9.2 %copy-start.5 = (s32[8,4]{0,1:T(4,128)S(1)}, s32[8,4]{0,1:T(4,128)}, u32[]{:S(2)}) copy-start(s32[8,4]{0,1:T(4,128)} %param.28) | copy-start | bytes 388
  15.5 9.4 %copy-start.4 = (s32[4,4,2]{1,2,0:T(2,128)S(1)}, s32[4,4,2]{1,2,0:T(2,128)}, u32[]{:S(2)}) copy-start(s32[4,4,2]{1,2,0:T(2,128)} %param.20) | copy-start | bytes 388
  19.1 11.4 %collective-permute-start = (f32[3,4,6,1024]{3,2,1,0:T(8,128)}, f32[3,4,6,1024]{3,2,1,0:T(8,128)}, u32[]{:S(2)}, u32[]{:S(2)}) collective-permute-start(f32[3,4,6,1024]{3,2,1,0:T(8,128)} %get-tuple-element.277), channel_id=1, source_target_pairs={{0,8},{8,16},{16,24},{24,32},{32,40},{40,48},{48,56},{56,64},{64,7... | collective-permute-start | bytes 884744 | tf_op jit(solution)/shard_map/ppermute | solution.py:28
  19.1 11.4 %collective-permute-start.1 = (f32[3,4,6,1024]{3,2,1,0:T(8,128)}, f32[3,4,6,1024]{3,2,1,0:T(8,128)}, u32[]{:S(2)}, u32[]{:S(2)}) collective-permute-start(f32[3,4,6,1024]{3,2,1,0:T(8,128)} %get-tuple-element.278), channel_id=1, source_target_pairs={{8,0},{16,8},{24,16},{32,24},{40,32},{48,40},{56,48},{64,56},{72,6... | collective-permute-start | bytes 884744 | tf_op jit(solution)/shard_map/ppermute | solution.py:29
  31.9 4.5 %copy-start.2 = (f32[8,3,256]{2,0,1:T(8,128)S(1)}, f32[8,3,256]{2,0,1:T(8,128)}, u32[]{:S(2)}) copy-start(f32[8,3,256]{2,0,1:T(8,128)} %param.24) | copy-start | bytes 73732
  33.4 27.2 %collective-permute-start.2 = (f32[10,3,6,1024]{3,2,1,0:T(8,128)}, f32[10,3,6,1024]{3,2,1,0:T(8,128)}, u32[]{:S(2)}, u32[]{:S(2)}) collective-permute-start(f32[10,3,6,1024]{3,2,1,0:T(8,128)} %get-tuple-element.275), channel_id=1, source_target_pairs={{0,1},{1,2},{2,3},{3,4},{4,5},{5,6},{6,7},{7,0},{8,9},{9,10},{10,1... | collective-permute-start | bytes 2211848 | tf_op jit(solution)/shard_map/ppermute | solution.py:28
  33.4 27.2 %collective-permute-start.3 = (f32[10,3,6,1024]{3,2,1,0:T(8,128)}, f32[10,3,6,1024]{3,2,1,0:T(8,128)}, u32[]{:S(2)}, u32[]{:S(2)}) collective-permute-start(f32[10,3,6,1024]{3,2,1,0:T(8,128)} %get-tuple-element.276), channel_id=1, source_target_pairs={{1,0},{2,1},{3,2},{4,3},{5,4},{6,5},{7,6},{0,7},{9,8},{10,9},{11,1... | collective-permute-start | bytes 2211848 | tf_op jit(solution)/shard_map/ppermute | solution.py:29
  75.7 6.8 %copy-start.1 = (f32[4,4,3,1024]{3,1,2,0:T(4,128)S(1)}, f32[4,4,3,1024]{3,1,2,0:T(4,128)}, u32[]{:S(2)}) copy-start(f32[4,4,3,1024]{3,1,2,0:T(4,128)} %param.18) | copy-start | bytes 589828
  82.4 164.6 %copy-start.3 = (f32[4,4]{1,0:T(4,128)S(1)}, f32[4,4]{1,0:T(4,128)}, u32[]{:S(2)}) copy-start(f32[4,4]{1,0:T(4,128)} %param.19) | copy-start | bytes 196
where the time goes:
time: 315 us; the launch traced here: 312 us
  other arithmetic  220 us (70%)
  local copies, waits for them, and re-layouts  34.9 us (11%)
  blocking collectives  34.1 us (11%)
  starting transfers between devices  16.7 us (5%)
    reduce_sum x12, other arithmetic, stokeslet(): out_x = jnp.sum(direct * forces[0][None, :] + tangent * delta_x, axis=1)  184 us
    pmax x4, blocking collectives, over_axes(): return functools.reduce(lax.pmax, axes, value)  34.1 us
    reduce_sum x8, other arithmetic, double_layer(): jnp.sum(scalar * delta_x, axis=1)  14.1 us
    mul x8, other arithmetic, double_layer(): scalar = -layer_scale * weights[None, :] * along_q * along_n * factor  9 us
    ppermute x2, starting transfers between devices, with_halo(): after = lax.ppermute(initial, axis, down)  8.3 us
    ppermute x1, starting transfers between devices, padded(): lax.ppermute(initial, axis, [(b, a) for a, b in up])  8.27 us
  transfers between devices with their start and end apart: 6, of which 1 were waited for; matrix products, arithmetic and copies ran while one was open for 11% of the time, Pallas kernels for 0%

commit v1 on v0

v1 whole, which is shorter than its diff:
```python
import math

import jax
import jax.numpy as jnp
from jax import lax
from jax.experimental import pallas as pl
from jax.experimental.pallas import tpu as pltpu
from jax.sharding import PartitionSpec as P

HALO = 3
AXES = ("cx", "cy")
SOFT = 0.25
STOKES_SCALE = 1.0 / (8.0 * math.pi)
LAYER_SCALE = 3.0 / (4.0 * math.pi)
F32 = jnp.float32
BF16 = jnp.bfloat16
LANES = 128

GROUPS = ((0, 0), (0, 1), (1, 0), (0, 2), (2, 0), (1, 1), (1, 2), (2, 1))
STOKES_ROWS = 24
LAYER_ROWS = 32


def parts(v):
    high = v.astype(BF16)
    rest = v - high.astype(F32)
    middle = rest.astype(BF16)
    low = (rest - middle.astype(F32)).astype(BF16)
    return high, middle, low


def target_rows(raw):
    split = [p.astype(F32) for p in parts(raw)]
    return jnp.concatenate([split[a] for a, _ in GROUPS], axis=0).astype(BF16)


def source_rows(raw):
    split = [p.astype(F32) for p in parts(raw)]
    stacked = jnp.concatenate([split[b] for _, b in GROUPS], axis=0)
    return jnp.transpose(stacked).astype(BF16)


def feature_rows(raw):
    return jnp.concatenate(parts(raw), axis=0)


def put_rows(ref, first, count, stride, value):
    for tile in range(ref.shape[0]):
        ref[tile, pl.ds(first, count, stride=stride), :] = value[
            :, tile * LANES : (tile + 1) * LANES
        ]


def get_rows(ref, first, count):
    return jnp.concatenate(
        [ref[tile, pl.ds(first, count), :] for tile in range(ref.shape[0])], axis=1
    )


def stokes_raw(ref, first, pos, force):
    square = pos[0] * pos[0] + pos[1] * pos[1] + pos[2] * pos[2]
    along = pos[0] * force[0] + pos[1] * force[1] + pos[2] * force[2]
    rows = [-2.0 * pos[0], -2.0 * pos[1], -2.0 * pos[2], square, jnp.ones_like(square)]
    rows += [jnp.zeros_like(square)] * 3
    rows += [force[0], force[1], force[2]]
    rows += [pos[j] * force[i] for j in range(3) for i in range(3)]
    rows += [square * force[i] + pos[i] * along for i in range(3)]
    rows += [jnp.zeros_like(square)]
    for k, row in enumerate(rows):
        put_rows(ref, first + k, 8, STOKES_ROWS, row)


def target_raw(ref, first, pos):
    square = pos[0] * pos[0] + pos[1] * pos[1] + pos[2] * pos[2] + SOFT
    rows = [pos[0], pos[1], pos[2], jnp.ones_like(square), square]
    rows += [jnp.zeros_like(square)] * 3
    for k, row in enumerate(rows):
        put_rows(ref, first + k, 8, 8, row)


def stokes_moments(raw_ref, slots, target):
    total = None
    for slot in slots:
        base = pl.multiple_of(slot * STOKES_ROWS, 8)
        left = source_rows(get_rows(raw_ref, base, 8))
        square = jnp.dot(left, target, preferred_element_type=F32)
        root = lax.rsqrt(jnp.maximum(square, SOFT))
        factor = (root * root * root).astype(BF16)
        features = feature_rows(get_rows(raw_ref, base + 8, 16))
        part = jnp.dot(features, factor, preferred_element_type=F32)
        total = part if total is None else total + part
    return total[0:16] + total[16:32] + total[32:48]


def stokes_finish(pos, moments):
    m0 = moments[0:3]
    m1 = [[moments[3 + 3 * j + i] for i in range(3)] for j in range(3)]
    m2 = moments[12:15]
    square = pos[0] * pos[0] + pos[1] * pos[1] + pos[2] * pos[2] + 2.0 * SOFT
    along = pos[0] * m0[0] + pos[1] * m0[1] + pos[2] * m0[2]
    along = along - (m1[0][0] + m1[1][1] + m1[2][2])
    out = []
    for i in range(3):
        cross = sum(pos[j] * (2.0 * m1[j][i] + m1[i][j]) for j in range(3))
        out.append(square * m0[i] + m2[i] + pos[i] * along - cross)
    return out


def near_kernel(
    near_ref,
    wall_ref,
    middle_ref,
    left_ref,
    right_ref,
    drag_ref,
    analysis_ref,
    stiffness_ref,
    synthesis_ref,
    velocity_ref,
    top_ref,
    wall_raw_ref,
    ext_ref,
    pos_ref,
    raw_ref,
    target_ref,
    moment_ref,
):
    rows = middle_ref.shape[0] - 2 * HALO
    cols = middle_ref.shape[2]
    points = middle_ref.shape[3]
    own = rows * cols
    near = near_ref.shape[0]
    wall = wall_ref.shape[0]
    slots = own + near + wall
    ext_ref[:, :, 0:HALO, :] = left_ref[...]
    ext_ref[:, :, HALO : HALO + cols, :] = middle_ref[...]
    ext_ref[:, :, HALO + cols :, :] = right_ref[...]
    for r in range(rows):
        for d in range(3):
            pos_ref[d, r * cols : (r + 1) * cols, :] = middle_ref[HALO + r, d]
    for i in range(near + wall):
        code = near_ref[i] if i < near else wall_ref[i - near]
        row = code // 16
        col = code % 16
        for d in range(3):
            pos_ref[d, own + i : own + i + 1, :] = ext_ref[row, d, pl.ds(col, 1), :]
    everything = [pos_ref[d] for d in range(3)]
    centred = [v - jnp.sum(v, axis=1, keepdims=True) * (1.0 / points) for v in everything]
    flat = jnp.concatenate(centred, axis=0).astype(BF16)
    coeff = jnp.dot(flat, analysis_ref[...], preferred_element_type=F32)
    scaled = (coeff * stiffness_ref[...]).astype(BF16)
    force = -jnp.dot(scaled, synthesis_ref[...], preferred_element_type=F32)
    forces = [force[d * slots : (d + 1) * slots] for d in range(3)]
    for g in range((near + wall) // 8):
        a = own + 8 * g
        into, base = (raw_ref, 8 * g) if 8 * g < near else (wall_raw_ref, 8 * g - near)
        stokes_raw(
            into,
            base * STOKES_ROWS,
            [v[a : a + 8] for v in everything],
            [v[a : a + 8] for v in forces],
        )
    for g in range(own // 8):
        target_raw(target_ref, 64 * g, [v[8 * g : 8 * g + 8] for v in everything])

    def cell(c, carry):
        target = target_rows(get_rows(target_ref, pl.multiple_of(c * 8, 8), 8))
        per = near // own
        moments = stokes_moments(raw_ref, [c * per + k for k in range(per)], target)
        put_rows(moment_ref, c, 16, own, moments)
        return carry

    lax.fori_loop(0, own, cell, 0)
    moments = [get_rows(moment_ref, k * own, own) for k in range(15)]
    own_pos = [v[0:own] for v in everything]
    sums = stokes_finish(own_pos, moments)
    speed = jnp.zeros_like(sums[0])
    for d in range(3):
        velocity = drag_ref[...] * forces[d][0:own] + STOKES_SCALE * sums[d]
        speed = speed + velocity * velocity
        for r in range(rows):
            velocity_ref[r, d] = velocity[r * cols : (r + 1) * cols]
    top_ref[...] = jnp.sqrt(jnp.max(speed, axis=(0, 1), keepdims=True))


def near_part(near_code, wall_code, middle, left, right, drag, analysis, stiffness, synthesis):
    rows, _, cols, points = middle.shape
    rows = rows - 2 * HALO
    own = rows * cols
    near, wall = near_code.shape[0], wall_code.shape[0]
    slots = own + near + wall
    tiles = points // LANES
    in_vmem = pl.BlockSpec(memory_space=pltpu.VMEM)
    in_smem = pl.BlockSpec(memory_space=pltpu.SMEM)
    pairs = own * points * (near // own) * points
    return pl.pallas_call(
        near_kernel,
        in_specs=[in_smem] * 2 + [in_vmem] * 7,
        out_specs=[in_vmem] * 3,
        out_shape=[
            jax.ShapeDtypeStruct((rows, 3, cols, points), F32),
            jax.ShapeDtypeStruct((1, 1), F32),
            jax.ShapeDtypeStruct((tiles, wall * STOKES_ROWS, LANES), F32),
        ],
        scratch_shapes=[
            pltpu.VMEM((rows + 2 * HALO, 3, cols + 2 * HALO, points), F32),
            pltpu.VMEM((3, slots, points), F32),
            pltpu.VMEM((tiles, near * STOKES_ROWS, LANES), F32),
            pltpu.VMEM((tiles, own * 8, LANES), F32),
            pltpu.VMEM((tiles, own * 16, LANES), F32),
        ],
        compiler_params=pltpu.CompilerParams(vmem_limit_bytes=50 * 2**20),
        cost_estimate=pl.CostEstimate(
            flops=1000 * pairs, bytes_accessed=8 * 2**20, transcendentals=pairs
        ),
        name="near",
    )(near_code, wall_code, middle, left, right, drag, analysis, stiffness, synthesis)


def wall_kernel(raw_ref, pos_ref, layer_ref, out_ref, target_ref, moment_ref):
    patches = pos_ref.shape[1]
    per = raw_ref.shape[1] // STOKES_ROWS // patches
    pos = [pos_ref[d] for d in range(3)]
    target_raw(target_ref, 0, pos)

    def patch(p, carry):
        target = target_rows(get_rows(target_ref, pl.multiple_of(p * 8, 8), 8))
        moments = stokes_moments(raw_ref, [p * per + k for k in range(per)], target)
        put_rows(moment_ref, p, 16, patches, moments)
        return carry

    lax.fori_loop(0, patches, patch, 0)
    sums = stokes_finish(pos, [get_rows(moment_ref, k * patches, patches) for k in range(15)])
    for d in range(3):
        out_ref[d] = layer_ref[d] + (2.0 * STOKES_SCALE) * sums[d]


def wall_part(raw, pos, layer):
    _, patches, points = pos.shape
    tiles = points // LANES
    in_vmem = pl.BlockSpec(memory_space=pltpu.VMEM)
    pairs = raw.shape[0] * raw.shape[1] // STOKES_ROWS * LANES * points
    return pl.pallas_call(
        wall_kernel,
        in_specs=[in_vmem] * 3,
        out_specs=in_vmem,
        out_shape=jax.ShapeDtypeStruct(pos.shape, F32),
        scratch_shapes=[
            pltpu.VMEM((tiles, patches * 8, LANES), F32),
            pltpu.VMEM((tiles, patches * 16, LANES), F32),
        ],
        compiler_params=pltpu.CompilerParams(vmem_limit_bytes=24 * 2**20),
        cost_estimate=pl.CostEstimate(
            flops=1000 * pairs, bytes_accessed=2 * 2**20, transcendentals=pairs
        ),
        name="wall",
    )(raw, pos, layer)


def layer_kernel(listed_ref, own_ref, before_ref, after_ref, out_ref, raw_ref, target_ref, left_ref, feature_ref, moment_ref):
    patches = own_ref.shape[1]
    for block, ref in enumerate((before_ref, own_ref, after_ref)):
        y = [ref[d] for d in range(3)]
        normal = [ref[3 + d] for d in range(3)]
        weight = ref[9]
        value = [ref[6 + d] * weight for d in range(3)]
        square = y[0] * y[0] + y[1] * y[1] + y[2] * y[2]
        one, zero = jnp.ones_like(square), jnp.zeros_like(square)
        rows = [-2.0 * y[0], -2.0 * y[1], -2.0 * y[2], square, one, zero, zero, zero]
        for v in (value, normal):
            rows += [v[0], v[1], v[2], -(y[0] * v[0] + y[1] * v[1] + y[2] * v[2])]
            rows += [zero] * 4
        rows += [y[0], y[1], y[2], one, zero, zero, zero, zero]
        for k, row in enumerate(rows):
            put_rows(raw_ref, block * patches * LAYER_ROWS + k, patches, LAYER_ROWS, row)
    pos = [own_ref[d] for d in range(3)]
    target_raw(target_ref, 0, pos)

    def prepare(s, carry):
        raw = get_rows(raw_ref, pl.multiple_of(s * LAYER_ROWS, 8), LAYER_ROWS)
        for k in range(3):
            left_ref[s, k] = source_rows(raw[8 * k : 8 * k + 8])
        split = [p.astype(F32) for p in parts(raw[24:32])]
        split.append(jnp.zeros_like(split[0]))
        feature_ref[s] = jnp.concatenate(split, axis=0).astype(BF16)
        return carry

    lax.fori_loop(0, 3 * patches, prepare, 0)
    listed = listed_ref.shape[1]

    def patch(p, carry):
        target = target_rows(get_rows(target_ref, pl.multiple_of(p * 8, 8), 8))
        total = None
        for k in range(listed + 1):
            s = patches + p if k == 0 else listed_ref[p, k - 1]
            square = jnp.dot(left_ref[s, 0], target, preferred_element_type=F32)
            along_q = jnp.dot(left_ref[s, 1], target, preferred_element_type=F32)
            along_n = jnp.dot(left_ref[s, 2], target, preferred_element_type=F32)
            root = lax.rsqrt(jnp.maximum(square, SOFT))
            double = root * root
            scalar = (along_q * along_n * (double * double * root)).astype(BF16)
            part = jnp.dot(feature_ref[s], scalar, preferred_element_type=F32)
            total = part if total is None else total + part
        moments = total[0:8] + total[8:16] + total[16:24]
        put_rows(moment_ref, p, 8, patches, moments)
        return carry

    lax.fori_loop(0, patches, patch, 0)
    moments = [get_rows(moment_ref, k * patches, patches) for k in range(4)]
    for d in range(3):
        out_ref[d] = (-2.0 * LAYER_SCALE) * (pos[d] * moments[3] - moments[d])


def layer_part(listed, own, before, after):
    _, patches, points = own.shape
    tiles = points // LANES
    in_vmem = pl.BlockSpec(memory_space=pltpu.VMEM)
    pairs = patches * points * (listed.shape[1] + 1) * points
    return pl.pallas_call(
        layer_kernel,
        in_specs=[pl.BlockSpec(memory_space=pltpu.SMEM)] + [in_vmem] * 3,
        out_specs=in_vmem,
        out_shape=jax.ShapeDtypeStruct((3, patches, points), F32),
        scratch_shapes=[
            pltpu.VMEM((tiles, 3 * patches * LAYER_ROWS, LANES), F32),
            pltpu.VMEM((tiles, patches * 8, LANES), F32),
            pltpu.VMEM((3 * patches, 3, points, 64), BF16),
            pltpu.VMEM((3 * patches, 32, points), BF16),
            pltpu.VMEM((tiles, patches * 8, LANES), F32),
        ],
        compiler_params=pltpu.CompilerParams(vmem_limit_bytes=24 * 2**20),
        cost_estimate=pl.CostEstimate(
            flops=1000 * pairs, bytes_accessed=2**20, transcendentals=pairs
        ),
        name="layer",
    )(listed, own, before, after)


def neighbours(low, high, axis):
    size = lax.axis_size(axis)
    up = [(i, (i + 1) % size) for i in range(size)]
    down = [(b, a) for a, b in up]
    return lax.ppermute(high, axis, up), lax.ppermute(low, axis, down)


def body(
    cell_pos,
    cell_drag,
    cell_near,
    analysis,
    stiffness,
    synthesis,
    wall_pos,
    wall_normal,
    wall_weight,
    density,
    patch_near,
    cell_to_patch,
):
    rows, cols = cell_pos.shape[:2]
    all_rows = rows * lax.axis_size("cx")
    all_cols = cols * lax.axis_size("cy")
    first_row = lax.axis_index("cx") * rows
    first_col = lax.axis_index("cy") * cols

    pos = jnp.transpose(cell_pos, (0, 2, 1, 3))
    walls = [jnp.transpose(v, (1, 0, 2)) for v in (wall_pos, wall_normal, density)]
    packed = jnp.concatenate(walls + [wall_weight[None]], axis=0)

    below, above = neighbours(pos[:HALO], pos[rows - HALO :], "cx")
    wall_below, wall_above = neighbours(packed, packed, AXES)
    middle = jnp.concatenate([below, pos, above], axis=0)
    left, right = neighbours(middle[:, :, :HALO], middle[:, :, cols - HALO :], "cy")

    patches = wall_pos.shape[0]
    all_patches = patches * lax.axis_size(AXES)
    start = lax.axis_index(AXES) * patches
    listed = (patch_near - start + patches) % all_patches
    layer = layer_part(listed, packed, wall_below, wall_above)

    def code(cell):
        row = (cell // all_cols - first_row + HALO) % all_rows
        col = (cell % all_cols - first_col + HALO) % all_cols
        return (row * 16 + col).reshape(-1)

    velocity, top, wall_raw = near_part(
        code(cell_near),
        code(cell_to_patch),
        middle,
        left,
        right,
        cell_drag.reshape(-1, 1),
        analysis,
        stiffness[None, :],
        synthesis,
    )
    top = lax.pmax(top, AXES)
    density_next = wall_part(wall_raw, walls[0], layer)
    step = 1.0 / (top[0, 0] + 1e-06)
    moved = pos + step * velocity
    return jnp.transpose(moved, (0, 2, 1, 3)), jnp.transpose(density_next, (1, 0, 2))


def solution(mesh):
    patch = P(AXES, None, None)
    return jax.shard_map(
        body,
        mesh=mesh,
        in_specs=(
            P("cx", "cy", None, None),
            P("cx", "cy"),
            P("cx", "cy", None),
            P(),
            P(),
            P(),
            patch,
            patch,
            P(AXES, None),
            patch,
            P(AXES, None),
            P(AXES, None),
        ),
        out_specs=(P("cx", "cy", None, None), patch),
        check_vma=False,
    )
```

time: 315 us -> 153 us (0.49)
  other arithmetic: 220 us -> 3.34 us
  Pallas kernels: 0 us -> 61.6 us
  local copies, waits for them, and re-layouts: 34.9 us -> 2.49 us
  blocking collectives: 34.1 us -> 65.1 us
    reduce_sum x22 -> x0, other arithmetic: 200 us -> none  [the longest x12 184 us: stokeslet(): out_x = jnp.sum(direct * forces[0][None, :] + tangent * delta_x, axis=1)]
    pallas_call x0 -> x3, Pallas kernels: none -> 61.6 us  [the longest x1 39.9 us: near_part(): pl.pallas_call(near_kernel, in_specs=[in_smem] * 2 + [in_vmem] * 7, out_s...]
    pmax x4 -> x1, blocking collectives: 34.1 us -> 65.1 us  [body(): top = lax.pmax(top, AXES)]
    gather x8 -> x0, local copies, waits for them, and re-layouts: 15 us -> none  [the longest x2 3.91 us: body(): wall_source_force = spread_many(flat_force[wall_slots])]
    mul x16 -> x0, other arithmetic: 9.1 us -> none  [the longest x8 9 us: double_layer(): scalar = -layer_scale * weights[None, :] * along_q * along_n * factor]
    reshape x6 -> x3, local copies, waits for them, and re-layouts: 5.05 us -> 0.25 us  [the longest x2 0.17 us: code(): return (row * 16 + col).reshape(-1)]
    unnamed x19 -> x11, local copies, waits for them, and re-layouts: 4.33 us -> 0.78 us
    slice x26 -> x2, local copies, waits for them, and re-layouts: 4.73 us -> 1.27 us  [the longest x1 1 us: body(): below, above = neighbours(pos[:HALO], pos[rows - HALO:], 'cx')]
  transfers between devices with their start and end apart: 6 -> 6, of which waited for: 1 -> 1; matrix products, arithmetic and copies ran while one was open for 11% -> 3% of each run, Pallas kernels for 0% -> 9%
where the time goes in v1:
time: 153 us; the launch traced here: 152 us
  blocking collectives  65.1 us (43%)
  Pallas kernels  61.6 us (40%)
  starting transfers between devices  16.7 us (11%)
  other arithmetic  3.34 us (2%)
  local copies, waits for them, and re-layouts  2.49 us (2%)
  waiting for transfers between devices  1.64 us (1%)
    pmax x1, blocking collectives, body(): top = lax.pmax(top, AXES)  65.1 us
    pallas_call x1, Pallas kernels, near_part(): pl.pallas_call(near_kernel, in_specs=[in_smem] * 2 + [in_vmem] * 7, out_s...  39.9 us
    ppermute x6, starting transfers between devices, neighbours(): return (lax.ppermute(high, axis, up), lax.ppermute(low, axis, down))  16.7 us
    pallas_call x1, Pallas kernels, layer_part(): pl.pallas_call(layer_kernel, in_specs=[pl.BlockSpec(memory_space=pltpu.SM...  13.9 us
    pallas_call x1, Pallas kernels, wall_part(): pl.pallas_call(wall_kernel, in_specs=[in_vmem] * 3, out_specs=in_vmem, ou...  7.69 us
  transfers between devices with their start and end apart: 6, of which 1 were waited for; matrix products, arithmetic and copies ran while one was open for 3% of the time, Pallas kernels for 9%

profile of v1, /device:TPU:0, one launch (start us, length us, event | category | flops | bytes accessed | tf_op | source)
XLA Modules:
  0.0 152.3 jit_solution(1441342506888841070)
XLA Ops:
  0.6 0.0 copy-start.4
  0.7 0.8 pad_maximum_fusion.1.own_ref
  1.5 0.0 collective-permute-start.4
  1.5 8.3 %collective-permute-start.5 = (f32[10,8,256]{2,1,0:T(8,128)S(1)}, f32[10,8,256]{2,1,0:T(8,128)S(1)}, u32[]{:S(2)}, u32[]{:S(2)}) collective-permute-start(f32[10,8,256]{2,1,0:T(8,128)S(1)} %pad_maximum_fusion.1.own_ref), channel_id=1, source_target_pairs={{1,0},{2,1},{3,2},{4,3},{5,4},{6,5},{7,6},{8,7},{9,8},{10,9},{11,1... | collective-permute-start | bytes 245768 | tf_op jit(solution)/shard_map/ppermute | solution.py:343
  9.8 1.0 fusion.12
  10.8 0.1 collective-permute-start
  10.9 5.3 %collective-permute-start.1 = (f32[3,3,4,1024]{3,2,1,0:T(4,128)S(1)}, f32[3,3,4,1024]{3,2,1,0:T(4,128)S(1)}, u32[]{:S(2)}, u32[]{:S(2)}) collective-permute-start(f32[3,3,4,1024]{3,2,1,0:T(4,128)S(1)} %get-tuple-element.11), channel_id=1, source_target_pairs={{8,0},{16,8},{24,16},{32,24},{40,32},{48,40},{56,48},{64,56},{72,6... | collective-permute-start | bytes 442376 | tf_op jit(solution)/shard_map/ppermute | solution.py:343
  16.2 0.8 copy.21
  17.0 0.7 fusion
  17.7 1.6 %collective-permute-done = f32[3,3,4,1024]{3,2,1,0:T(4,128)S(1)} collective-permute-done((f32[3,3,4,1024]{3,2,1,0:T(4,128)S(1)}, f32[3,3,4,1024]{3,2,1,0:T(4,128)S(1)}, u32[]{:S(2)}, u32[]{:S(2)}) %collective-permute-start) | collective-permute-done | bytes 147488 | tf_op jit(solution)/shard_map/ppermute | solution.py:343
  19.3 0.0 collective-permute-done.1
  19.3 1.0 pad_maximum_fusion.middle_ref
  20.4 0.3 fusion.11
  20.6 0.0 collective-permute-start.2
  20.7 2.9 %collective-permute-start.3 = (f32[10,3,3,1024]{3,2,1,0:T(4,128)S(1)}, f32[10,3,3,1024]{3,2,1,0:T(4,128)S(1)}, u32[]{:S(2)}, u32[]{:S(2)}) collective-permute-start(f32[10,3,3,1024]{3,2,1,0:T(4,128)S(1)} %get-tuple-element.8), channel_id=1, source_target_pairs={{1,0},{2,1},{3,2},{4,3},{5,4},{6,5},{7,6},{0,7},{9,8},{10,9},{11,1... | collective-permute-start | bytes 1105928 | tf_op jit(solution)/shard_map/ppermute | solution.py:343
  23.6 0.1 copy.18
  23.7 0.1 reshape.17.near_ref
  23.8 0.1 copy.19
  23.9 0.1 reshape.18.wall_ref
  24.0 0.1 reshape.20.drag_ref
  24.1 0.0 collective-permute-done.4.before_ref
  24.1 0.0 collective-permute-done.5.after_ref
  24.1 13.9 %layer.1.layer_ref = f32[3,8,256]{2,1,0:T(8,128)S(1)} custom-call(s32[8,4]{1,0:T(8,128)S(1)} %add_select_fusion.listed_ref, f32[10,8,256]{2,1,0:T(8,128)S(1)} %pad_maximum_fusion.1.own_ref, f32[10,8,256]{2,1,0:T(8,128)S(1)} %collective-permute-done.4.before_ref, f32[10,8,256]{2,1,0:T(8,128)S(1)} %collective-permute-done.5.after_ref), custom_call_target="tpu_custom_call" | custom-call | flops 2621440000 | bytes 1048576 | tf_op jit(solution)/shard_map/layer/pallas_call | solution.py:319
  38.0 0.0 collective-permute-done.2.left_ref
  38.1 0.0 collective-permute-done.3.right_ref
  38.1 0.0 copy-start.2
  38.1 0.0 copy-start
  38.1 39.9 %near.1 = (f32[4,3,4,1024]{3,2,1,0:T(4,128)S(1)}, f32[1,1]{1,0:T(1,128)}, f32[8,384,128]{2,1,0:T(8,128)S(1)}) custom-call(s32[32]{0:T(128)S(1)} %reshape.17.near_ref, s32[16]{0:T(128)S(1)} %reshape.18.wall_ref, f32[10,3,4,1024]{3,2,1,0:T(4,128)S(1)} %pad_maximum_fusion.middle_ref, f32[10,3,3,1024]{3,2,1,0:T(4,128)S(1)} %collective-permute-done.2.left_ref, ...), custom_call_target="tpu_custom_call" | custom-call | flops 33554432000 | bytes 8388608 | tf_op jit(solution)/shard_map/near/pallas_call | solution.py:196
  78.0 65.1 %pmax.7 = f32[1,1]{1,0:T(1,128)} all-reduce(f32[1,1]{1,0:T(1,128)} %get-tuple-element.5), channel_id=1, replica_groups=mesh['cx'=16,'cy'=8] {'cx','cy'}, use_global_device_ids=true, to_apply=%region_0.1 | all-reduce | flops 1 | bytes 8 | tf_op jit(solution)/shard_map/pmax | solution.py:397
  143.8 0.0 copy-done.2
  143.9 0.7 add_bitcast_fusion
  144.6 7.7 %wall.1 = f32[3,8,256]{2,1,0:T(8,128)} custom-call(f32[8,384,128]{2,1,0:T(8,128)S(1)} %get-tuple-element.7.raw_ref, f32[3,8,256]{2,1,0:T(8,128)S(1)} %bitcast.12, f32[3,8,256]{2,1,0:T(8,128)S(1)} %layer.1.layer_ref), custom_call_target="tpu_custom_call" | custom-call | flops 4194304000 | bytes 2097152 | tf_op jit(solution)/shard_map/wall/pallas_call | solution.py:243
  (8 shorter events, 0.0 us)
Async XLA Ops:
  0.6 23.0 %copy-start.4 = (s32[8,2]{0,1:T(2,128)S(1)}, s32[8,2]{0,1:T(2,128)}, u32[]{:S(2)}) copy-start(s32[8,2]{0,1:T(2,128)} %param.23) | copy-start | bytes 196
  0.6 23.4 %copy-start.3 = (f32[4,4]{1,0:T(4,128)S(1)}, f32[4,4]{1,0:T(4,128)}, u32[]{:S(2)}) copy-start(f32[4,4]{1,0:T(4,128)} %param.13) | copy-start | bytes 196
  1.5 22.6 %collective-permute-start.4 = (f32[10,8,256]{2,1,0:T(8,128)S(1)}, f32[10,8,256]{2,1,0:T(8,128)S(1)}, u32[]{:S(2)}, u32[]{:S(2)}) collective-permute-start(f32[10,8,256]{2,1,0:T(8,128)S(1)} %pad_maximum_fusion.1.own_ref), channel_id=1, source_target_pairs={{0,1},{1,2},{2,3},{3,4},{4,5},{5,6},{6,7},{7,8},{8,9},{9,10},{10,1... | collective-permute-start | bytes 245768 | tf_op jit(solution)/shard_map/ppermute | solution.py:343
  1.5 22.6 %collective-permute-start.5 = (f32[10,8,256]{2,1,0:T(8,128)S(1)}, f32[10,8,256]{2,1,0:T(8,128)S(1)}, u32[]{:S(2)}, u32[]{:S(2)}) collective-permute-start(f32[10,8,256]{2,1,0:T(8,128)S(1)} %pad_maximum_fusion.1.own_ref), channel_id=1, source_target_pairs={{1,0},{2,1},{3,2},{4,3},{5,4},{6,5},{7,6},{8,7},{9,8},{10,9},{11,1... | collective-permute-start | bytes 245768 | tf_op jit(solution)/shard_map/ppermute | solution.py:343
  10.8 8.5 %collective-permute-start = (f32[3,3,4,1024]{3,2,1,0:T(4,128)S(1)}, f32[3,3,4,1024]{3,2,1,0:T(4,128)S(1)}, u32[]{:S(2)}, u32[]{:S(2)}) collective-permute-start(f32[3,3,4,1024]{3,2,1,0:T(4,128)S(1)} %get-tuple-element.10), channel_id=1, source_target_pairs={{0,8},{8,16},{16,24},{24,32},{32,40},{40,48},{48,56},{56,64},{64,7... | collective-permute-start | bytes 442376 | tf_op jit(solution)/shard_map/ppermute | solution.py:343
  10.9 8.5 %collective-permute-start.1 = (f32[3,3,4,1024]{3,2,1,0:T(4,128)S(1)}, f32[3,3,4,1024]{3,2,1,0:T(4,128)S(1)}, u32[]{:S(2)}, u32[]{:S(2)}) collective-permute-start(f32[3,3,4,1024]{3,2,1,0:T(4,128)S(1)} %get-tuple-element.11), channel_id=1, source_target_pairs={{8,0},{16,8},{24,16},{32,24},{40,32},{48,40},{56,48},{64,56},{72,6... | collective-permute-start | bytes 442376 | tf_op jit(solution)/shard_map/ppermute | solution.py:343
  20.6 17.4 %collective-permute-start.2 = (f32[10,3,3,1024]{3,2,1,0:T(4,128)S(1)}, f32[10,3,3,1024]{3,2,1,0:T(4,128)S(1)}, u32[]{:S(2)}, u32[]{:S(2)}) collective-permute-start(f32[10,3,3,1024]{3,2,1,0:T(4,128)S(1)} %get-tuple-element.9), channel_id=1, source_target_pairs={{0,1},{1,2},{2,3},{3,4},{4,5},{5,6},{6,7},{7,0},{8,9},{9,10},{10,1... | collective-permute-start | bytes 1105928 | tf_op jit(solution)/shard_map/ppermute | solution.py:343
  20.7 17.4 %collective-permute-start.3 = (f32[10,3,3,1024]{3,2,1,0:T(4,128)S(1)}, f32[10,3,3,1024]{3,2,1,0:T(4,128)S(1)}, u32[]{:S(2)}, u32[]{:S(2)}) collective-permute-start(f32[10,3,3,1024]{3,2,1,0:T(4,128)S(1)} %get-tuple-element.8), channel_id=1, source_target_pairs={{1,0},{2,1},{3,2},{4,3},{5,4},{6,5},{7,6},{0,7},{9,8},{10,9},{11,1... | collective-permute-start | bytes 1105928 | tf_op jit(solution)/shard_map/ppermute | solution.py:343
  24.1 14.0 %copy-start.1 = (f32[1024]{0:T(1024)S(1)}, f32[1024]{0:T(1024)}, u32[]{:S(2)}) copy-start(f32[1024]{0:T(1024)} %param.16) | copy-start | bytes 12292
  38.1 105.8 %copy-start.2 = (f32[4,4,3,1024]{3,1,2,0:T(4,128)S(1)}, f32[4,4,3,1024]{3,1,2,0:T(4,128)}, u32[]{:S(2)}) copy-start(f32[4,4,3,1024]{3,1,2,0:T(4,128)} %param.12) | copy-start | bytes 589828
  38.1 106.5 %copy-start = (f32[8,3,256]{2,0,1:T(8,128)S(1)}, f32[8,3,256]{2,0,1:T(8,128)}, u32[]{:S(2)}) copy-start(f32[8,3,256]{2,0,1:T(8,128)} %param.18) | copy-start | bytes 73732

commit v2 on v1

--- a/solution.py
+++ b/solution.py
@@ -1,3 +1,4 @@
+import functools
 import math
 
 import jax
@@ -36,8 +37,11 @@
 
 def source_rows(raw):
     split = [p.astype(F32) for p in parts(raw)]
-    stacked = jnp.concatenate([split[b] for _, b in GROUPS], axis=0)
-    return jnp.transpose(stacked).astype(BF16)
+    return jnp.concatenate([split[b] for _, b in GROUPS], axis=0).astype(BF16)
+
+
+def product(left, right):
+    return lax.dot_general(left, right, (((0,), (0,)), ((), ())), preferred_element_type=F32)
 
 
 def feature_rows(raw):
@@ -83,7 +87,7 @@
     for slot in slots:
         base = pl.multiple_of(slot * STOKES_ROWS, 8)
         left = source_rows(get_rows(raw_ref, base, 8))
-        square = jnp.dot(left, target, preferred_element_type=F32)
+        square = product(left, target)
         root = lax.rsqrt(jnp.maximum(square, SOFT))
         factor = (root * root * root).astype(BF16)
         features = feature_rows(get_rows(raw_ref, base + 8, 16))
@@ -109,7 +113,9 @@
 def near_kernel(
     near_ref,
     wall_ref,
-    middle_ref,
+    below_ref,
+    own_ref,
+    above_ref,
     left_ref,
     right_ref,
     drag_ref,
@@ -125,19 +131,20 @@
     target_ref,
     moment_ref,
 ):
-    rows = middle_ref.shape[0] - 2 * HALO
-    cols = middle_ref.shape[2]
-    points = middle_ref.shape[3]
+    rows, _, cols, points = own_ref.shape
     own = rows * cols
     near = near_ref.shape[0]
     wall = wall_ref.shape[0]
     slots = own + near + wall
     ext_ref[:, :, 0:HALO, :] = left_ref[...]
-    ext_ref[:, :, HALO : HALO + cols, :] = middle_ref[...]
+    inner = slice(HALO, HALO + cols)
+    ext_ref[0:HALO, :, inner, :] = below_ref[rows - HALO :]
+    ext_ref[HALO : HALO + rows, :, inner, :] = own_ref[...]
+    ext_ref[HALO + rows :, :, inner, :] = above_ref[0:HALO]
     ext_ref[:, :, HALO + cols :, :] = right_ref[...]
     for r in range(rows):
         for d in range(3):
-            pos_ref[d, r * cols : (r + 1) * cols, :] = middle_ref[HALO + r, d]
+            pos_ref[d, r * cols : (r + 1) * cols, :] = own_ref[r, d]
     for i in range(near + wall):
         code = near_ref[i] if i < near else wall_ref[i - near]
         row = code // 16
@@ -180,12 +187,12 @@
         speed = speed + velocity * velocity
         for r in range(rows):
             velocity_ref[r, d] = velocity[r * cols : (r + 1) * cols]
-    top_ref[...] = jnp.sqrt(jnp.max(speed, axis=(0, 1), keepdims=True))
-
-
-def near_part(near_code, wall_code, middle, left, right, drag, analysis, stiffness, synthesis):
-    rows, _, cols, points = middle.shape
-    rows = rows - 2 * HALO
+    top = jnp.sqrt(jnp.max(speed, axis=(0, 1), keepdims=True))
+    top_ref[...] = jnp.broadcast_to(top, top_ref.shape)
+
+
+def near_part(near_code, wall_code, below, pos, above, left, right, drag, tables):
+    rows, _, cols, points = pos.shape
     own = rows * cols
     near, wall = near_code.shape[0], wall_code.shape[0]
     slots = own + near + wall
@@ -195,11 +202,11 @@
     pairs = own * points * (near // own) * points
     return pl.pallas_call(
         near_kernel,
-        in_specs=[in_smem] * 2 + [in_vmem] * 7,
+        in_specs=[in_smem] * 2 + [in_vmem] * 9,
         out_specs=[in_vmem] * 3,
         out_shape=[
             jax.ShapeDtypeStruct((rows, 3, cols, points), F32),
-            jax.ShapeDtypeStruct((1, 1), F32),
+            jax.ShapeDtypeStruct((8, LANES), F32),
             jax.ShapeDtypeStruct((tiles, wall * STOKES_ROWS, LANES), F32),
         ],
         scratch_shapes=[
@@ -214,18 +221,17 @@
             flops=1000 * pairs, bytes_accessed=8 * 2**20, transcendentals=pairs
         ),
         name="near",
-    )(near_code, wall_code, middle, left, right, drag, analysis, stiffness, synthesis)
-
-
-def wall_kernel(raw_ref, pos_ref, layer_ref, out_ref, target_ref, moment_ref):
+    )(near_code, wall_code, below, pos, above, left, right, drag, *tables)
+
+
+def wall_kernel(stage, per, raw_ref, pos_ref, layer_ref, out_ref, target_ref, moment_ref):
     patches = pos_ref.shape[1]
-    per = raw_ref.shape[1] // STOKES_ROWS // patches
     pos = [pos_ref[d] for d in range(3)]
     target_raw(target_ref, 0, pos)
 
     def patch(p, carry):
         target = target_rows(get_rows(target_ref, pl.multiple_of(p * 8, 8), 8))
-        moments = stokes_moments(raw_ref, [p * per + k for k in range(per)], target)
+        moments = stokes_moments(raw_ref, [p * per + stage], target)
         put_rows(moment_ref, p, 16, patches, moments)
         return carry
 
@@ -235,13 +241,13 @@
         out_ref[d] = layer_ref[d] + (2.0 * STOKES_SCALE) * sums[d]
 
 
-def wall_part(raw, pos, layer):
+def wall_part(stage, per, raw, pos, layer):
     _, patches, points = pos.shape
     tiles = points // LANES
     in_vmem = pl.BlockSpec(memory_space=pltpu.VMEM)
-    pairs = raw.shape[0] * raw.shape[1] // STOKES_ROWS * LANES * points
+    pairs = patches * raw.shape[0] * LANES * points
     return pl.pallas_call(
-        wall_kernel,
+        functools.partial(wall_kernel, stage, per),
         in_specs=[in_vmem] * 3,
         out_specs=in_vmem,
         out_shape=jax.ShapeDtypeStruct(pos.shape, F32),
@@ -253,7 +259,7 @@
         cost_estimate=pl.CostEstimate(
             flops=1000 * pairs, bytes_accessed=2 * 2**20, transcendentals=pairs
         ),
-        name="wall",
+        name=f"wall_{stage}",
     )(raw, pos, layer)
 
 
@@ -293,9 +299,9 @@
         total = None
         for k in range(listed + 1):
             s = patches + p if k == 0 else listed_ref[p, k - 1]
-            square = jnp.dot(left_ref[s, 0], target, preferred_element_type=F32)
-            along_q = jnp.dot(left_ref[s, 1], target, preferred_element_type=F32)
-            along_n = jnp.dot(left_ref[s, 2], target, preferred_element_type=F32)
+            square = product(left_ref[s, 0], target)
+            along_q = product(left_ref[s, 1], target)
+            along_n = product(left_ref[s, 2], target)
             root = lax.rsqrt(jnp.maximum(square, SOFT))
             double = root * root
             scalar = (along_q * along_n * (double * double * root)).astype(BF16)
@@ -324,7 +330,7 @@
         scratch_shapes=[
             pltpu.VMEM((tiles, 3 * patches * LAYER_ROWS, LANES), F32),
             pltpu.VMEM((tiles, patches * 8, LANES), F32),
-            pltpu.VMEM((3 * patches, 3, points, 64), BF16),
+            pltpu.VMEM((3 * patches, 3, 64, points), BF16),
             pltpu.VMEM((3 * patches, 32, points), BF16),
             pltpu.VMEM((tiles, patches * 8, LANES), F32),
         ],
@@ -341,6 +347,31 @@
     up = [(i, (i + 1) % size) for i in range(size)]
     down = [(b, a) for a, b in up]
     return lax.ppermute(high, axis, up), lax.ppermute(low, axis, down)
+
+
+def rotations(outer, inner, along_outer):
+    size = outer if along_outer else inner
+    for turn in range(1, size):
+        yield [
+            (
+                a * inner + b,
+                (a + turn) % outer * inner + b if along_outer else a * inner + (b + turn) % inner,
+            )
+            for a in range(outer)
+            for b in range(inner)
+        ]
+
+
+def over_all(value):
+    for axis, inner in (("cy", 2), ("cx", 4)):
+        outer = lax.axis_size(axis) // inner
+        for along_outer in (False, True):
+            came = [
+                lax.ppermute(value, axis, pairs)
+                for pairs in rotations(outer, inner, along_outer)
+            ]
+            value = functools.reduce(jnp.maximum, came, value)
+    return value
 
 
 def body(
@@ -367,10 +398,12 @@
     walls = [jnp.transpose(v, (1, 0, 2)) for v in (wall_pos, wall_normal, density)]
     packed = jnp.concatenate(walls + [wall_weight[None]], axis=0)
 
-    below, above = neighbours(pos[:HALO], pos[rows - HALO :], "cx")
+    below, above = neighbours(pos, pos, "cx")
     wall_below, wall_above = neighbours(packed, packed, AXES)
-    middle = jnp.concatenate([below, pos, above], axis=0)
-    left, right = neighbours(middle[:, :, :HALO], middle[:, :, cols - HALO :], "cy")
+    strips = [v[:, :, c : c + HALO] for c in (0, cols - HALO) for v in (below[rows - HALO :], pos, above[:HALO])]
+    left, right = neighbours(
+        jnp.concatenate(strips[:3], axis=0), jnp.concatenate(strips[3:], axis=0), "cy"
+    )
 
     patches = wall_pos.shape[0]
     all_patches = patches * lax.axis_size(AXES)
@@ -386,16 +419,19 @@
     velocity, top, wall_raw = near_part(
         code(cell_near),
         code(cell_to_patch),
-        middle,
+        below,
+        pos,
+        above,
         left,
         right,
         cell_drag.reshape(-1, 1),
-        analysis,
-        stiffness[None, :],
-        synthesis,
+        (analysis, stiffness[None, :], synthesis),
     )
-    top = lax.pmax(top, AXES)
-    density_next = wall_part(wall_raw, walls[0], layer)
+    top = over_all(top)
+    density_next = layer
+    per = cell_to_patch.shape[1]
+    for stage in range(per):
+        density_next = wall_part(stage, per, wall_raw, walls[0], density_next)
     step = 1.0 / (top[0, 0] + 1e-06)
     moved = pos + step * velocity
     return jnp.transpose(moved, (0, 2, 1, 3)), jnp.transpose(density_next, (1, 0, 2))

time: 153 us -> 102 us (0.67)
  blocking collectives: 65.1 us -> 0 us
  starting transfers between devices: 16.7 us -> 29 us
  waiting for transfers between devices: 1.64 us -> 7.86 us
  Pallas kernels: 61.6 us -> 59.2 us
    pmax x1 -> x0, blocking collectives: 65.1 us -> none  [body(): top = lax.pmax(top, AXES)]
    ppermute x0 -> x10, starting transfers between devices: none -> 12.4 us  [over_all(): lax.ppermute(value, axis, pairs)]
    ppermute x6, waiting for transfers between devices: 1.64 us -> 6.43 us  [neighbours(): return (lax.ppermute(high, axis, up), lax.ppermute(low, axis, down))]
    pallas_call x1, Pallas kernels: 13.9 us -> 11.5 us  [layer_part(): pl.pallas_call(layer_kernel, in_specs=[pl.BlockSpec(memory_space=pltpu.SM...]
    pallas_call x2 -> x3, Pallas kernels: 47.6 us -> 47.8 us  [the longest x1 38.2 us: near_part(): pl.pallas_call(near_kernel, in_specs=[in_smem] * 2 + [in_vmem] * 9, out_s...]
  transfers between devices with their start and end apart: 6 -> 16, of which waited for: 1 -> 4; matrix products, arithmetic and copies ran while one was open for 3% -> 3% of each run, Pallas kernels for 9% -> 58%
where the time goes in v2:
time: 102 us
  Pallas kernels  59.2 us (58%)
  starting transfers between devices  29 us (28%)
  waiting for transfers between devices  7.86 us (8%)
  local copies, waits for them, and re-layouts  2.28 us (2%)
  other arithmetic  1.91 us (2%)
  between operations  1.54 us (2%)
    pallas_call x1, Pallas kernels, near_part(): pl.pallas_call(near_kernel, in_specs=[in_smem] * 2 + [in_vmem] * 9, out_s...  38.2 us
    ppermute x6, starting transfers between devices, neighbours(): return (lax.ppermute(high, axis, up), lax.ppermute(low, axis, down))  16.6 us
    ppermute x10, starting transfers between devices, over_all(): lax.ppermute(value, axis, pairs)  12.4 us
    pallas_call x1, Pallas kernels, layer_part(): pl.pallas_call(layer_kernel, in_specs=[pl.BlockSpec(memory_space=pltpu.SM...  11.5 us
    pallas_call x2, Pallas kernels, wall_part(): pl.pallas_call(functools.partial(wall_kernel, stage, per), in_specs=[in_v...  9.56 us
    ppermute x6, waiting for transfers between devices, neighbours(): return (lax.ppermute(high, axis, up), lax.ppermute(low, axis, down))  6.43 us
  transfers between devices with their start and end apart: 16, of which 4 were waited for; matrix products, arithmetic and copies ran while one was open for 3% of the time, Pallas kernels for 58%

profile of v2, /device:TPU:0, one launch (start us, length us, event | category | flops | bytes accessed | tf_op | source)
XLA Modules:
  0.0 101.8 jit_solution(15894285726741530240)
XLA Ops:
  0.7 6.4 %collective-permute-start.1 = (f32[4,3,4,1024]{3,2,1,0:T(4,128)}, f32[4,3,4,1024]{3,2,1,0:T(4,128)S(1)}, u32[]{:S(2)}, u32[]{:S(2)}) collective-permute-start(f32[4,3,4,1024]{3,2,1,0:T(4,128)} %bitcast.11), channel_id=1, source_target_pairs={{8,0},{16,8},{24,16},{32,24},{40,32},{48,40},{56,48},{64,56},{72,6... | collective-permute-start | bytes 589832 | tf_op jit(solution)/shard_map/ppermute | solution.py:349
  7.1 0.8 pad_maximum_fusion.2.own_ref
  7.9 7.2 %collective-permute-start.15 = (f32[10,8,256]{2,1,0:T(8,128)S(1)}, f32[10,8,256]{2,1,0:T(8,128)S(1)}, u32[]{:S(2)}, u32[]{:S(2)}) collective-permute-start(f32[10,8,256]{2,1,0:T(8,128)S(1)} %pad_maximum_fusion.2.own_ref), channel_id=1, source_target_pairs={{1,0},{2,1},{3,2},{4,3},{5,4},{6,5},{7,6},{8,7},{9,8},{10,9},{11,1... | collective-permute-start | bytes 245768 | tf_op jit(solution)/shard_map/ppermute | solution.py:349
  15.1 1.1 %fusion.12 = (f32[4,3,3,1024]{3,2,1,0:T(4,128)S(1)}, f32[4,3,3,1024]{3,2,1,0:T(4,128)S(1)}) fusion(f32[4,3,4,1024]{3,2,1,0:T(4,128)} %bitcast.13), kind=kLoop, calls=%fused_computation.44 | loop fusion | bytes 589824 | tf_op jit(solution)/shard_map/slice | solution.py:403
  16.2 0.1 fusion.13
  16.3 0.7 collective-permute-done.below_ref
  17.0 0.1 pad_maximum_fusion
  17.2 0.1 pad_maximum_fusion.1
  17.3 3.0 %collective-permute-start.3 = (f32[10,3,3,1024]{3,2,1,0:T(4,128)S(1)}, f32[10,3,3,1024]{3,2,1,0:T(4,128)S(1)}, u32[]{:S(2)}, u32[]{:S(2)}) collective-permute-start(f32[10,3,3,1024]{3,2,1,0:T(4,128)S(1)} %pad_maximum_fusion.1), channel_id=1, source_target_pairs={{1,0},{2,1},{3,2},{4,3},{5,4},{6,5},{7,6},{0,7},{9,8},{10,9},{11,1... | collective-permute-start | bytes 1105928 | tf_op jit(solution)/shard_map/ppermute | solution.py:349
  20.3 0.1 copy.18
  20.4 0.1 reshape.17.near_ref
  20.6 0.1 copy.19
  20.6 0.1 reshape.18.wall_ref
  20.7 0.1 reshape.20.drag_ref
  20.8 0.1 copy.21
  20.9 5.8 %collective-permute-done.2.left_ref = f32[10,3,3,1024]{3,2,1,0:T(4,128)S(1)} collective-permute-done((f32[10,3,3,1024]{3,2,1,0:T(4,128)S(1)}, f32[10,3,3,1024]{3,2,1,0:T(4,128)S(1)}, u32[]{:S(2)}, u32[]{:S(2)}) %collective-permute-start.2) | collective-permute-done | bytes 368672 | tf_op jit(solution)/shard_map/ppermute | solution.py:349
  26.6 38.2 %near.1 = (f32[4,3,4,1024]{3,2,1,0:T(4,128)S(1)}, f32[8,128]{1,0:T(8,128)S(1)}, f32[8,384,128]{2,1,0:T(8,128)S(1)}) custom-call(s32[32]{0:T(128)S(1)} %reshape.17.near_ref, s32[16]{0:T(128)S(1)} %reshape.18.wall_ref, f32[4,3,4,1024]{3,2,1,0:T(4,128)S(1)} %collective-permute-done.below_ref, f32[4,3,4,1024]{3,2,1,0:T(4,128)S(1)} %bitcast.14, ...), custom_call_target="tpu_custom_call" | custom-call | flops 33554432000 | bytes 8388608 | tf_op jit(solution)/shard_map/near/pallas_call | solution.py:203
  64.8 0.7 collective-permute-start.4
  65.6 0.8 collective-permute-done.4
  66.4 1.6 %collective-permute-start.5 = (f32[8,128]{1,0:T(8,128)S(1)}, f32[8,128]{1,0:T(8,128)S(1)}, u32[]{:S(2)}, u32[]{:S(2)}) collective-permute-start(f32[8,128]{1,0:T(8,128)S(1)} %max.30), channel_id=1, source_target_pairs={{0,2},{1,3},{2,4},{3,5},{4,6},{5,7},{6,0},{7,1},{8,10},{9,11},{10,... | collective-permute-start | bytes 12296 | tf_op jit(solution)/shard_map/ppermute | solution.py:370
  67.9 2.8 %collective-permute-start.6 = (f32[8,128]{1,0:T(8,128)S(1)}, f32[8,128]{1,0:T(8,128)S(1)}, u32[]{:S(2)}, u32[]{:S(2)}) collective-permute-start(f32[8,128]{1,0:T(8,128)S(1)} %max.30), channel_id=1, source_target_pairs={{0,4},{1,5},{2,6},{3,7},{4,0},{5,1},{6,2},{7,3},{8,12},{9,13},{10,... | collective-permute-start | bytes 12296 | tf_op jit(solution)/shard_map/ppermute | solution.py:370
  70.7 2.1 %collective-permute-start.7 = (f32[8,128]{1,0:T(8,128)S(1)}, f32[8,128]{1,0:T(8,128)S(1)}, u32[]{:S(2)}, u32[]{:S(2)}) collective-permute-start(f32[8,128]{1,0:T(8,128)S(1)} %max.30), channel_id=1, source_target_pairs={{0,6},{1,7},{2,0},{3,1},{4,2},{5,3},{6,4},{7,5},{8,14},{9,15},{10,... | collective-permute-start | bytes 12296 | tf_op jit(solution)/shard_map/ppermute | solution.py:370
  72.8 11.5 %layer.1.layer_ref = f32[3,8,256]{2,1,0:T(8,128)S(1)} custom-call(s32[8,4]{1,0:T(8,128)S(1)} %add_select_fusion.listed_ref, f32[10,8,256]{2,1,0:T(8,128)S(1)} %pad_maximum_fusion.2.own_ref, f32[10,8,256]{2,1,0:T(8,128)S(1)} %collective-permute-done.14.before_ref, f32[10,8,256]{2,1,0:T(8,128)S(1)} %collective-permute-done.15.after_ref), custom_call_target="tpu_custom_call" | custom-call | flops 2621440000 | bytes 1048576 | tf_op jit(solution)/shard_map/layer/pallas_call | solution.py:325
  84.3 0.1 collective-permute-start.10
  84.4 2.0 %collective-permute-start.8 = (f32[8,128]{1,0:T(8,128)S(1)}, f32[8,128]{1,0:T(8,128)S(1)}, u32[]{:S(2)}, u32[]{:S(2)}) collective-permute-start(f32[8,128]{1,0:T(8,128)S(1)} %maximum_maximum_fusion.2), channel_id=1, source_target_pairs={{0,8},{8,16},{16,24},{24,0},{32,40},{40,48},{48,56},{56,32},{64,72... | collective-permute-start | bytes 12296 | tf_op jit(solution)/shard_map/ppermute | solution.py:370
  86.4 4.5 %wall_0.1.layer_ref = f32[3,8,256]{2,1,0:T(8,128)S(1)} custom-call(f32[8,384,128]{2,1,0:T(8,128)S(1)} %get-tuple-element.7.raw_ref, f32[3,8,256]{2,1,0:T(8,128)S(1)} %bitcast.16, f32[3,8,256]{2,1,0:T(8,128)S(1)} %layer.1.layer_ref), custom_call_target="tpu_custom_call" | custom-call | flops 2097152000 | bytes 2097152 | tf_op jit(solution)/shard_map/wall_0/pallas_call | solution.py:249
  90.9 0.6 collective-permute-done.9
  91.5 0.7 collective-permute-start.12
  92.2 2.6 %collective-permute-start.13 = (f32[8,128]{1,0:T(8,128)S(1)}, f32[8,128]{1,0:T(8,128)S(1)}, u32[]{:S(2)}, u32[]{:S(2)}) collective-permute-start(f32[8,128]{1,0:T(8,128)S(1)} %maximum_maximum_fusion.1), channel_id=1, source_target_pairs={{0,96},{8,104},{16,112},{24,120},{32,0},{40,8},{48,16},{56,24},{64... | collective-permute-start | bytes 12296 | tf_op jit(solution)/shard_map/ppermute | solution.py:370
  94.8 5.1 %wall_1.1 = f32[3,8,256]{2,1,0:T(8,128)} custom-call(f32[8,384,128]{2,1,0:T(8,128)S(1)} %get-tuple-element.7.raw_ref, f32[3,8,256]{2,1,0:T(8,128)S(1)} %bitcast.17, f32[3,8,256]{2,1,0:T(8,128)S(1)} %wall_0.1.layer_ref), custom_call_target="tpu_custom_call" | custom-call | flops 2097152000 | bytes 2097152 | tf_op jit(solution)/shard_map/wall_1/pallas_call | solution.py:249
  99.9 0.5 slice.35
  101.1 0.7 add_bitcast_fusion
  (39 shorter events, 0.3 us)
Async XLA Ops:
  0.6 19.6 %copy-start.3 = (s32[4,4,2]{1,2,0:T(2,128)S(1)}, s32[4,4,2]{1,2,0:T(2,128)}, u32[]{:S(2)}) copy-start(s32[4,4,2]{1,2,0:T(2,128)} %param.14) | copy-start | bytes 388
  0.6 19.9 %copy-start.6 = (s32[8,2]{0,1:T(2,128)S(1)}, s32[8,2]{0,1:T(2,128)}, u32[]{:S(2)}) copy-start(s32[8,2]{0,1:T(2,128)} %param.23) | copy-start | bytes 196
  0.7 20.1 %copy-start.4 = (f32[4,4]{1,0:T(4,128)S(1)}, f32[4,4]{1,0:T(4,128)}, u32[]{:S(2)}) copy-start(f32[4,4]{1,0:T(4,128)} %param.13) | copy-start | bytes 196
  0.7 20.1 %copy-start.5 = (s32[8,4]{0,1:T(4,128)S(1)}, s32[8,4]{0,1:T(4,128)}, u32[]{:S(2)}) copy-start(s32[8,4]{0,1:T(4,128)} %param.22) | copy-start | bytes 388
  0.7 15.5 %collective-permute-start.1 = (f32[4,3,4,1024]{3,2,1,0:T(4,128)}, f32[4,3,4,1024]{3,2,1,0:T(4,128)S(1)}, u32[]{:S(2)}, u32[]{:S(2)}) collective-permute-start(f32[4,3,4,1024]{3,2,1,0:T(4,128)} %bitcast.11), channel_id=1, source_target_pairs={{8,0},{16,8},{24,16},{32,24},{40,32},{48,40},{56,48},{64,56},{72,6... | collective-permute-start | bytes 589832 | tf_op jit(solution)/shard_map/ppermute | solution.py:349
  7.1 9.9 %collective-permute-start = (f32[4,3,4,1024]{3,2,1,0:T(4,128)}, f32[4,3,4,1024]{3,2,1,0:T(4,128)S(1)}, u32[]{:S(2)}, u32[]{:S(2)}) collective-permute-start(f32[4,3,4,1024]{3,2,1,0:T(4,128)} %bitcast.12), channel_id=1, source_target_pairs={{0,8},{8,16},{16,24},{24,32},{32,40},{40,48},{48,56},{56,64},{64,7... | collective-permute-start | bytes 589832 | tf_op jit(solution)/shard_map/ppermute | solution.py:349
  7.1 19.6 %copy-start = (f32[4,4,3,1024]{3,1,2,0:T(4,128)S(1)}, f32[4,4,3,1024]{3,1,2,0:T(4,128)}, u32[]{:S(2)}) copy-start(f32[4,4,3,1024]{3,1,2,0:T(4,128)} %param.12) | copy-start | bytes 589828
  7.1 19.6 %copy-start.2 = (f32[1024]{0:T(1024)S(1)}, f32[1024]{0:T(1024)}, u32[]{:S(2)}) copy-start(f32[1024]{0:T(1024)} %param.16) | copy-start | bytes 12292
  7.9 64.9 %collective-permute-start.14 = (f32[10,8,256]{2,1,0:T(8,128)S(1)}, f32[10,8,256]{2,1,0:T(8,128)S(1)}, u32[]{:S(2)}, u32[]{:S(2)}) collective-permute-start(f32[10,8,256]{2,1,0:T(8,128)S(1)} %pad_maximum_fusion.2.own_ref), channel_id=1, source_target_pairs={{0,1},{1,2},{2,3},{3,4},{4,5},{5,6},{6,7},{7,8},{8,9},{9,10},{10,1... | collective-permute-start | bytes 245768 | tf_op jit(solution)/shard_map/ppermute | solution.py:349
  7.9 64.8 %collective-permute-start.15 = (f32[10,8,256]{2,1,0:T(8,128)S(1)}, f32[10,8,256]{2,1,0:T(8,128)S(1)}, u32[]{:S(2)}, u32[]{:S(2)}) collective-permute-start(f32[10,8,256]{2,1,0:T(8,128)S(1)} %pad_maximum_fusion.2.own_ref), channel_id=1, source_target_pairs={{1,0},{2,1},{3,2},{4,3},{5,4},{6,5},{7,6},{8,7},{9,8},{10,9},{11,1... | collective-permute-start | bytes 245768 | tf_op jit(solution)/shard_map/ppermute | solution.py:349
  17.2 9.5 %collective-permute-start.2 = (f32[10,3,3,1024]{3,2,1,0:T(4,128)S(1)}, f32[10,3,3,1024]{3,2,1,0:T(4,128)S(1)}, u32[]{:S(2)}, u32[]{:S(2)}) collective-permute-start(f32[10,3,3,1024]{3,2,1,0:T(4,128)S(1)} %pad_maximum_fusion), channel_id=1, source_target_pairs={{0,1},{1,2},{2,3},{3,4},{4,5},{5,6},{6,7},{7,0},{8,9},{9,10},{10,1... | collective-permute-start | bytes 1105928 | tf_op jit(solution)/shard_map/ppermute | solution.py:349
  17.3 9.3 %collective-permute-start.3 = (f32[10,3,3,1024]{3,2,1,0:T(4,128)S(1)}, f32[10,3,3,1024]{3,2,1,0:T(4,128)S(1)}, u32[]{:S(2)}, u32[]{:S(2)}) collective-permute-start(f32[10,3,3,1024]{3,2,1,0:T(4,128)S(1)} %pad_maximum_fusion.1), channel_id=1, source_target_pairs={{1,0},{2,1},{3,2},{4,3},{5,4},{6,5},{7,6},{0,7},{9,8},{10,9},{11,1... | collective-permute-start | bytes 1105928 | tf_op jit(solution)/shard_map/ppermute | solution.py:349
  64.8 1.5 %collective-permute-start.4 = (f32[8,128]{1,0:T(8,128)S(1)}, f32[8,128]{1,0:T(8,128)S(1)}, u32[]{:S(2)}, u32[]{:S(2)}) collective-permute-start(f32[8,128]{1,0:T(8,128)S(1)} %get-tuple-element.5), channel_id=1, source_target_pairs={{0,1},{1,0},{2,3},{3,2},{4,5},{5,4},{6,7},{7,6},{8,9},{9,8},{10,11... | collective-permute-start | bytes 12296 | tf_op jit(solution)/shard_map/ppermute | solution.py:370
  66.4 20.0 %copy-start.1 = (f32[8,3,256]{2,0,1:T(8,128)S(1)}, f32[8,3,256]{2,0,1:T(8,128)}, u32[]{:S(2)}) copy-start(f32[8,3,256]{2,0,1:T(8,128)} %param.18) | copy-start | bytes 73732
  66.4 17.9 %collective-permute-start.5 = (f32[8,128]{1,0:T(8,128)S(1)}, f32[8,128]{1,0:T(8,128)S(1)}, u32[]{:S(2)}, u32[]{:S(2)}) collective-permute-start(f32[8,128]{1,0:T(8,128)S(1)} %max.30), channel_id=1, source_target_pairs={{0,2},{1,3},{2,4},{3,5},{4,6},{5,7},{6,0},{7,1},{8,10},{9,11},{10,... | collective-permute-start | bytes 12296 | tf_op jit(solution)/shard_map/ppermute | solution.py:370
  67.9 16.3 %collective-permute-start.6 = (f32[8,128]{1,0:T(8,128)S(1)}, f32[8,128]{1,0:T(8,128)S(1)}, u32[]{:S(2)}, u32[]{:S(2)}) collective-permute-start(f32[8,128]{1,0:T(8,128)S(1)} %max.30), channel_id=1, source_target_pairs={{0,4},{1,5},{2,6},{3,7},{4,0},{5,1},{6,2},{7,3},{8,12},{9,13},{10,... | collective-permute-start | bytes 12296 | tf_op jit(solution)/shard_map/ppermute | solution.py:370
  70.7 13.6 %collective-permute-start.7 = (f32[8,128]{1,0:T(8,128)S(1)}, f32[8,128]{1,0:T(8,128)S(1)}, u32[]{:S(2)}, u32[]{:S(2)}) collective-permute-start(f32[8,128]{1,0:T(8,128)S(1)} %max.30), channel_id=1, source_target_pairs={{0,6},{1,7},{2,0},{3,1},{4,2},{5,3},{6,4},{7,5},{8,14},{9,15},{10,... | collective-permute-start | bytes 12296 | tf_op jit(solution)/shard_map/ppermute | solution.py:370
  84.3 6.6 %collective-permute-start.10 = (f32[8,128]{1,0:T(8,128)S(1)}, f32[8,128]{1,0:T(8,128)S(1)}, u32[]{:S(2)}, u32[]{:S(2)}) collective-permute-start(f32[8,128]{1,0:T(8,128)S(1)} %maximum_maximum_fusion.2), channel_id=1, source_target_pairs={{0,24},{8,0},{16,8},{24,16},{32,56},{40,32},{48,40},{56,48},{64,88... | collective-permute-start | bytes 12296 | tf_op jit(solution)/shard_map/ppermute | solution.py:370
  84.4 6.5 %collective-permute-start.8 = (f32[8,128]{1,0:T(8,128)S(1)}, f32[8,128]{1,0:T(8,128)S(1)}, u32[]{:S(2)}, u32[]{:S(2)}) collective-permute-start(f32[8,128]{1,0:T(8,128)S(1)} %maximum_maximum_fusion.2), channel_id=1, source_target_pairs={{0,8},{8,16},{16,24},{24,0},{32,40},{40,48},{48,56},{56,32},{64,72... | collective-permute-start | bytes 12296 | tf_op jit(solution)/shard_map/ppermute | solution.py:370
  86.4 5.1 %collective-permute-start.9 = (f32[8,128]{1,0:T(8,128)S(1)}, f32[8,128]{1,0:T(8,128)S(1)}, u32[]{:S(2)}, u32[]{:S(2)}) collective-permute-start(f32[8,128]{1,0:T(8,128)S(1)} %maximum_maximum_fusion.2), channel_id=1, source_target_pairs={{0,16},{8,24},{16,0},{24,8},{32,48},{40,56},{48,32},{56,40},{64,80... | collective-permute-start | bytes 12296 | tf_op jit(solution)/shard_map/ppermute | solution.py:370
  91.5 8.3 %collective-permute-start.11 = (f32[8,128]{1,0:T(8,128)S(1)}, f32[8,128]{1,0:T(8,128)S(1)}, u32[]{:S(2)}, u32[]{:S(2)}) collective-permute-start(f32[8,128]{1,0:T(8,128)S(1)} %maximum_maximum_fusion.1), channel_id=1, source_target_pairs={{0,32},{8,40},{16,48},{24,56},{32,64},{40,72},{48,80},{56,88},{64,... | collective-permute-start | bytes 12296 | tf_op jit(solution)/shard_map/ppermute | solution.py:370
  91.5 8.3 %collective-permute-start.12 = (f32[8,128]{1,0:T(8,128)S(1)}, f32[8,128]{1,0:T(8,128)S(1)}, u32[]{:S(2)}, u32[]{:S(2)}) collective-permute-start(f32[8,128]{1,0:T(8,128)S(1)} %maximum_maximum_fusion.1), channel_id=1, source_target_pairs={{0,64},{8,72},{16,80},{24,88},{32,96},{40,104},{48,112},{56,120},{... | collective-permute-start | bytes 12296 | tf_op jit(solution)/shard_map/ppermute | solution.py:370
  92.2 7.7 %collective-permute-start.13 = (f32[8,128]{1,0:T(8,128)S(1)}, f32[8,128]{1,0:T(8,128)S(1)}, u32[]{:S(2)}, u32[]{:S(2)}) collective-permute-start(f32[8,128]{1,0:T(8,128)S(1)} %maximum_maximum_fusion.1), channel_id=1, source_target_pairs={{0,96},{8,104},{16,112},{24,120},{32,0},{40,8},{48,16},{56,24},{64... | collective-permute-start | bytes 12296 | tf_op jit(solution)/shard_map/ppermute | solution.py:370

commit v3 on v2

--- a/solution.py
+++ b/solution.py
@@ -9,6 +9,7 @@
 from jax.sharding import PartitionSpec as P
 
 HALO = 3
+FIRST = 2
 AXES = ("cx", "cy")
 SOFT = 0.25
 STOKES_SCALE = 1.0 / (8.0 * math.pi)
@@ -20,6 +21,7 @@
 GROUPS = ((0, 0), (0, 1), (1, 0), (0, 2), (2, 0), (1, 1), (1, 2), (2, 1))
 STOKES_ROWS = 24
 LAYER_ROWS = 32
+TARGET_ROWS = 24
 
 
 def parts(v):
@@ -74,12 +76,12 @@
         put_rows(ref, first + k, 8, STOKES_ROWS, row)
 
 
-def target_raw(ref, first, pos):
+def target_raw(ref, first, pos, stride=8):
     square = pos[0] * pos[0] + pos[1] * pos[1] + pos[2] * pos[2] + SOFT
     rows = [pos[0], pos[1], pos[2], jnp.ones_like(square), square]
     rows += [jnp.zeros_like(square)] * 3
     for k, row in enumerate(rows):
-        put_rows(ref, first + k, 8, 8, row)
+        put_rows(ref, first + k, 8, stride, row)
 
 
 def stokes_moments(raw_ref, slots, target):
@@ -130,7 +132,16 @@
     raw_ref,
     target_ref,
     moment_ref,
+    first_ref,
+    second_ref,
+    sems,
 ):
+    tables = [
+        pltpu.make_async_copy(a, b, sems.at[k])
+        for k, (a, b) in enumerate(((analysis_ref, first_ref), (synthesis_ref, second_ref)))
+    ]
+    for table in tables:
+        table.start()
     rows, _, cols, points = own_ref.shape
     own = rows * cols
     near = near_ref.shape[0]
@@ -154,9 +165,11 @@
     everything = [pos_ref[d] for d in range(3)]
     centred = [v - jnp.sum(v, axis=1, keepdims=True) * (1.0 / points) for v in everything]
     flat = jnp.concatenate(centred, axis=0).astype(BF16)
-    coeff = jnp.dot(flat, analysis_ref[...], preferred_element_type=F32)
+    tables[0].wait()
+    coeff = jnp.dot(flat, first_ref[...], preferred_element_type=F32)
     scaled = (coeff * stiffness_ref[...]).astype(BF16)
-    force = -jnp.dot(scaled, synthesis_ref[...], preferred_element_type=F32)
+    tables[1].wait()
+    force = -jnp.dot(scaled, second_ref[...], preferred_element_type=F32)
     forces = [force[d * slots : (d + 1) * slots] for d in range(3)]
     for g in range((near + wall) // 8):
         a = own + 8 * g
@@ -177,7 +190,7 @@
         put_rows(moment_ref, c, 16, own, moments)
         return carry
 
-    lax.fori_loop(0, own, cell, 0)
+    lax.fori_loop(0, own, cell, 0, unroll=2)
     moments = [get_rows(moment_ref, k * own, own) for k in range(15)]
     own_pos = [v[0:own] for v in everything]
     sums = stokes_finish(own_pos, moments)
@@ -199,10 +212,11 @@
     tiles = points // LANES
     in_vmem = pl.BlockSpec(memory_space=pltpu.VMEM)
     in_smem = pl.BlockSpec(memory_space=pltpu.SMEM)
+    in_hbm = pl.BlockSpec(memory_space=pl.ANY)
     pairs = own * points * (near // own) * points
     return pl.pallas_call(
         near_kernel,
-        in_specs=[in_smem] * 2 + [in_vmem] * 9,
+        in_specs=[in_smem] * 2 + [in_vmem] * 6 + [in_hbm, in_vmem, in_hbm],
         out_specs=[in_vmem] * 3,
         out_shape=[
             jax.ShapeDtypeStruct((rows, 3, cols, points), F32),
@@ -215,6 +229,9 @@
             pltpu.VMEM((tiles, near * STOKES_ROWS, LANES), F32),
             pltpu.VMEM((tiles, own * 8, LANES), F32),
             pltpu.VMEM((tiles, own * 16, LANES), F32),
+            pltpu.VMEM(tables[0].shape, BF16),
+            pltpu.VMEM(tables[2].shape, BF16),
+            pltpu.SemaphoreType.DMA((2,)),
         ],
         compiler_params=pltpu.CompilerParams(vmem_limit_bytes=50 * 2**20),
         cost_estimate=pl.CostEstimate(
@@ -235,7 +252,7 @@
         put_rows(moment_ref, p, 16, patches, moments)
         return carry
 
-    lax.fori_loop(0, patches, patch, 0)
+    lax.fori_loop(0, patches, patch, 0, unroll=True)
     sums = stokes_finish(pos, [get_rows(moment_ref, k * patches, patches) for k in range(15)])
     for d in range(3):
         out_ref[d] = layer_ref[d] + (2.0 * STOKES_SCALE) * sums[d]
@@ -263,83 +280,126 @@
     )(raw, pos, layer)
 
 
-def layer_kernel(listed_ref, own_ref, before_ref, after_ref, out_ref, raw_ref, target_ref, left_ref, feature_ref, moment_ref):
+def layer_sums(listed_ref, own_ref, left_ref, feature_ref, target_ref, moment_ref):
     patches = own_ref.shape[1]
-    for block, ref in enumerate((before_ref, own_ref, after_ref)):
-        y = [ref[d] for d in range(3)]
-        normal = [ref[3 + d] for d in range(3)]
-        weight = ref[9]
-        value = [ref[6 + d] * weight for d in range(3)]
-        square = y[0] * y[0] + y[1] * y[1] + y[2] * y[2]
-        one, zero = jnp.ones_like(square), jnp.zeros_like(square)
-        rows = [-2.0 * y[0], -2.0 * y[1], -2.0 * y[2], square, one, zero, zero, zero]
-        for v in (value, normal):
-            rows += [v[0], v[1], v[2], -(y[0] * v[0] + y[1] * v[1] + y[2] * v[2])]
-            rows += [zero] * 4
-        rows += [y[0], y[1], y[2], one, zero, zero, zero, zero]
-        for k, row in enumerate(rows):
-            put_rows(raw_ref, block * patches * LAYER_ROWS + k, patches, LAYER_ROWS, row)
-    pos = [own_ref[d] for d in range(3)]
-    target_raw(target_ref, 0, pos)
-
-    def prepare(s, carry):
-        raw = get_rows(raw_ref, pl.multiple_of(s * LAYER_ROWS, 8), LAYER_ROWS)
-        for k in range(3):
-            left_ref[s, k] = source_rows(raw[8 * k : 8 * k + 8])
-        split = [p.astype(F32) for p in parts(raw[24:32])]
-        split.append(jnp.zeros_like(split[0]))
-        feature_ref[s] = jnp.concatenate(split, axis=0).astype(BF16)
-        return carry
-
-    lax.fori_loop(0, 3 * patches, prepare, 0)
-    listed = listed_ref.shape[1]
+    x = [own_ref[d] for d in range(3)]
+    target_raw(target_ref, 0, x, TARGET_ROWS)
+    rows = [x[0] * x[0], x[1] * x[1], x[2] * x[2], x[0] * x[1], x[0] * x[2], x[1] * x[2]]
+    rows += x + [jnp.ones_like(x[0])] + [jnp.zeros_like(x[0])] * 6
+    for k, row in enumerate(rows):
+        put_rows(target_ref, 8 + k, patches, TARGET_ROWS, row)
 
     def patch(p, carry):
-        target = target_rows(get_rows(target_ref, pl.multiple_of(p * 8, 8), 8))
+        raw = get_rows(target_ref, pl.multiple_of(p * TARGET_ROWS, 8), TARGET_ROWS)
+        near, form = target_rows(raw[0:8]), target_rows(raw[8:24])
         total = None
-        for k in range(listed + 1):
-            s = patches + p if k == 0 else listed_ref[p, k - 1]
-            square = product(left_ref[s, 0], target)
-            along_q = product(left_ref[s, 1], target)
-            along_n = product(left_ref[s, 2], target)
+        for k in range(listed_ref.shape[1]):
+            s = listed_ref[p, k]
+            square = product(left_ref[s, 0:64], near)
+            scalar = product(left_ref[s, 64:192], form)
             root = lax.rsqrt(jnp.maximum(square, SOFT))
             double = root * root
-            scalar = (along_q * along_n * (double * double * root)).astype(BF16)
+            scalar = (scalar * (double * double * root)).astype(BF16)
             part = jnp.dot(feature_ref[s], scalar, preferred_element_type=F32)
             total = part if total is None else total + part
         moments = total[0:8] + total[8:16] + total[16:24]
         put_rows(moment_ref, p, 8, patches, moments)
         return carry
 
-    lax.fori_loop(0, patches, patch, 0)
+    lax.fori_loop(0, patches, patch, 0, unroll=True)
     moments = [get_rows(moment_ref, k * patches, patches) for k in range(4)]
+    return [(-2.0 * LAYER_SCALE) * (x[d] * moments[3] - moments[d]) for d in range(3)]
+
+
+def layer_first(listed_ref, own_ref, before_ref, after_ref, out_ref, left_ref, feature_ref, raw_ref, target_ref, moment_ref):
+    patches = own_ref.shape[1]
+    for block, ref in enumerate((before_ref, own_ref, after_ref)):
+        y = [ref[d] for d in range(3)]
+        n = [ref[3 + d] for d in range(3)]
+        v = [ref[6 + d] * ref[9] for d in range(3)]
+        square = y[0] * y[0] + y[1] * y[1] + y[2] * y[2]
+        along_n = y[0] * n[0] + y[1] * n[1] + y[2] * n[2]
+        along_v = y[0] * v[0] + y[1] * v[1] + y[2] * v[2]
+        one, zero = jnp.ones_like(square), jnp.zeros_like(square)
+        rows = [-2.0 * y[0], -2.0 * y[1], -2.0 * y[2], square, one, zero, zero, zero]
+        rows += [v[d] * n[d] for d in range(3)]
+        rows += [v[a] * n[b] + v[b] * n[a] for a, b in ((0, 1), (0, 2), (1, 2))]
+        rows += [-(v[d] * along_n + n[d] * along_v) for d in range(3)]
+        rows += [along_v * along_n] + [zero] * 6
+        rows += [y[0], y[1], y[2], one, zero, zero, zero, zero]
+        for k, row in enumerate(rows):
+            put_rows(raw_ref, block * patches * LAYER_ROWS + k, patches, LAYER_ROWS, row)
+
+    def prepare(s, carry):
+        raw = get_rows(raw_ref, pl.multiple_of(s * LAYER_ROWS, 8), LAYER_ROWS)
+        left_ref[s, 0:64] = source_rows(raw[0:8])
+        left_ref[s, 64:192] = source_rows(raw[8:24])
+        split = [p.astype(F32) for p in parts(raw[24:32])]
+        split.append(jnp.zeros_like(split[0]))
+        feature_ref[s] = jnp.concatenate(split, axis=0).astype(BF16)
+        return carry
+
+    lax.fori_loop(0, 3 * patches, prepare, 0, unroll=4)
+    sums = layer_sums(listed_ref, own_ref, left_ref, feature_ref, target_ref, moment_ref)
     for d in range(3):
-        out_ref[d] = (-2.0 * LAYER_SCALE) * (pos[d] * moments[3] - moments[d])
-
-
-def layer_part(listed, own, before, after):
-    _, patches, points = own.shape
+        out_ref[d] = sums[d]
+
+
+def layer_second(listed_ref, own_ref, left_ref, feature_ref, so_far_ref, out_ref, target_ref, moment_ref):
+    sums = layer_sums(listed_ref, own_ref, left_ref, feature_ref, target_ref, moment_ref)
+    for d in range(3):
+        out_ref[d] = so_far_ref[d] + sums[d]
+
+
+def layer_part(kernel, listed, *arrays):
+    _, patches, points = arrays[0].shape
     tiles = points // LANES
     in_vmem = pl.BlockSpec(memory_space=pltpu.VMEM)
-    pairs = patches * points * (listed.shape[1] + 1) * points
+    pairs = patches * points * listed.shape[1] * points
+    out_shape = [jax.ShapeDtypeStruct((3, patches, points), F32)]
+    scratch = [
+        pltpu.VMEM((tiles, patches * TARGET_ROWS, LANES), F32),
+        pltpu.VMEM((tiles, patches * 8, LANES), F32),
+    ]
+    if kernel is layer_first:
+        out_shape += [
+            jax.ShapeDtypeStruct((3 * patches, 192, points), BF16),
+            jax.ShapeDtypeStruct((3 * patches, 32, points), BF16),
+        ]
+        scratch.insert(0, pltpu.VMEM((tiles, 3 * patches * LAYER_ROWS, LANES), F32))
     return pl.pallas_call(
-        layer_kernel,
-        in_specs=[pl.BlockSpec(memory_space=pltpu.SMEM)] + [in_vmem] * 3,
-        out_specs=in_vmem,
-        out_shape=jax.ShapeDtypeStruct((3, patches, points), F32),
-        scratch_shapes=[
-            pltpu.VMEM((tiles, 3 * patches * LAYER_ROWS, LANES), F32),
-            pltpu.VMEM((tiles, patches * 8, LANES), F32),
-            pltpu.VMEM((3 * patches, 3, 64, points), BF16),
-            pltpu.VMEM((3 * patches, 32, points), BF16),
-            pltpu.VMEM((tiles, patches * 8, LANES), F32),
-        ],
+        kernel,
+        in_specs=[pl.BlockSpec(memory_space=pltpu.SMEM)] + [in_vmem] * len(arrays),
+        out_specs=[in_vmem] * len(out_shape),
+        out_shape=out_shape,
+        scratch_shapes=scratch,
         compiler_params=pltpu.CompilerParams(vmem_limit_bytes=24 * 2**20),
         cost_estimate=pl.CostEstimate(
             flops=1000 * pairs, bytes_accessed=2**20, transcendentals=pairs
         ),
-        name="layer",
-    )(listed, own, before, after)
+        name=kernel.__name__,
+    )(listed, *arrays)
+
+
+def move_kernel(*refs):
+    *tops, pos_ref, velocity_ref, out_ref = refs
+    top = functools.reduce(jnp.maximum, [t[...] for t in tops])
+    step = 1.0 / (top[0:1, 0:1] + 1e-06)
+    rows, _, cols, _ = pos_ref.shape
+    for r in range(rows):
+        for d in range(3):
+            out_ref[r, d] = pos_ref[r, d] + step * velocity_ref[r, d]
+
+
+def move_part(tops, pos, velocity):
+    in_vmem = pl.BlockSpec(memory_space=pltpu.VMEM)
+    return pl.pallas_call(
+        move_kernel,
+        in_specs=[in_vmem] * (len(tops) + 2),
+        out_specs=in_vmem,
+        out_shape=jax.ShapeDtypeStruct(pos.shape, F32),
+        name="move",
+    )(*tops, pos, velocity)
 
 
 def neighbours(low, high, axis):
@@ -363,15 +423,16 @@
 
 
 def over_all(value):
+    values = [value]
     for axis, inner in (("cy", 2), ("cx", 4)):
         outer = lax.axis_size(axis) // inner
         for along_outer in (False, True):
-            came = [
+            value = functools.reduce(jnp.maximum, values)
+            values = [value] + [
                 lax.ppermute(value, axis, pairs)
                 for pairs in rotations(outer, inner, along_outer)
             ]
-            value = functools.reduce(jnp.maximum, came, value)
-    return value
+    return values
 
 
 def body(
@@ -409,15 +470,19 @@
     all_patches = patches * lax.axis_size(AXES)
     start = lax.axis_index(AXES) * patches
     listed = (patch_near - start + patches) % all_patches
-    layer = layer_part(listed, packed, wall_below, wall_above)
+    itself = patches + jnp.arange(patches, dtype=jnp.int32)[:, None]
+    listed = jnp.concatenate([itself, listed], axis=1)
+    early = listed[:, :FIRST]
+    layer, lefts, features = layer_part(layer_first, early, packed, wall_below, wall_above)
 
     def code(cell):
         row = (cell // all_cols - first_row + HALO) % all_rows
         col = (cell % all_cols - first_col + HALO) % all_cols
         return (row * 16 + col).reshape(-1)
 
+    near_code, layer = lax.optimization_barrier((code(cell_near), layer))
     velocity, top, wall_raw = near_part(
-        code(cell_near),
+        near_code,
         code(cell_to_patch),
         below,
         pos,
@@ -427,13 +492,13 @@
         cell_drag.reshape(-1, 1),
         (analysis, stiffness[None, :], synthesis),
     )
-    top = over_all(top)
-    density_next = layer
+    top, late = lax.optimization_barrier((top, listed[:, FIRST:]))
+    tops = over_all(top)
+    [density_next] = layer_part(layer_second, late, packed, lefts, features, layer)
     per = cell_to_patch.shape[1]
     for stage in range(per):
         density_next = wall_part(stage, per, wall_raw, walls[0], density_next)
-    step = 1.0 / (top[0, 0] + 1e-06)
-    moved = pos + step * velocity
+    moved = move_part(tops, pos, velocity)
     return jnp.transpose(moved, (0, 2, 1, 3)), jnp.transpose(density_next, (1, 0, 2))
 
 

time: 102 us -> 96.6 us (0.947)
  the two profiles are of different devices: /device:TPU:0 before, /device:TPU:76 now
where the time goes in v3:
time: 96.6 us; the launch traced here: 96.3 us
  Pallas kernels  55.8 us (58%)
  starting transfers between devices  28.3 us (29%)
  waiting for transfers between devices  6.29 us (7%)
  local copies, waits for them, and re-layouts  3.12 us (3%)
  other arithmetic  1.91 us (2%)
    pallas_call x1, Pallas kernels, near_part(): pl.pallas_call(near_kernel, in_specs=[in_smem] * 2 + [in_vmem] * 6 + [in_...  37.3 us
    ppermute x10, starting transfers between devices, over_all(): lax.ppermute(value, axis, pairs)  23.9 us
    pallas_call x2, Pallas kernels, layer_part(): pl.pallas_call(kernel, in_specs=[pl.BlockSpec(memory_space=pltpu.SMEM)] +...  9.07 us
    pallas_call x2, Pallas kernels, wall_part(): pl.pallas_call(functools.partial(wall_kernel, stage, per), in_specs=[in_v...  7.67 us
    ppermute x6, waiting for transfers between devices, neighbours(): return (lax.ppermute(high, axis, up), lax.ppermute(low, axis, down))  5.44 us
    ppermute x6, starting transfers between devices, neighbours(): return (lax.ppermute(high, axis, up), lax.ppermute(low, axis, down))  4.33 us
  transfers between devices with their start and end apart: 16, of which 3 were waited for; matrix products, arithmetic and copies ran while one was open for 4% of the time, Pallas kernels for 17%

profile of v3, /device:TPU:76, one launch (start us, length us, event | category | flops | bytes accessed | tf_op | source)
XLA Modules:
  0.0 96.3 jit_solution(4450882220819661028)
XLA Ops:
  0.7 0.8 pad_maximum_fusion.2.own_ref
  1.5 0.5 collective-permute-start
  2.0 0.5 collective-permute-start.3
  2.5 1.5 %collective-permute-start.2 = (f32[4,3,4,1024]{3,2,1,0:T(4,128)}, f32[4,3,4,1024]{3,2,1,0:T(4,128)S(1)}, u32[]{:S(2)}, u32[]{:S(2)}) collective-permute-start(f32[4,3,4,1024]{3,2,1,0:T(4,128)} %bitcast.10), channel_id=1, source_target_pairs={{0,8},{8,16},{16,24},{24,32},{32,40},{40,48},{48,56},{56,64},{64,7... | collective-permute-start | bytes 589832 | tf_op jit(solution)/shard_map/ppermute | solution.py:409
  4.0 1.1 %fusion.12 = (f32[4,3,3,1024]{3,2,1,0:T(4,128)S(1)}, f32[4,3,3,1024]{3,2,1,0:T(4,128)S(1)}) fusion(f32[4,3,4,1024]{3,2,1,0:T(4,128)} %bitcast.11), kind=kLoop, calls=%fused_computation.44 | loop fusion | bytes 589824 | tf_op jit(solution)/shard_map/slice | solution.py:464
  5.1 0.8 copy.19
  5.9 0.7 fusion
  6.6 3.9 %collective-permute-done.2.below_ref = f32[4,3,4,1024]{3,2,1,0:T(4,128)S(1)} collective-permute-done((f32[4,3,4,1024]{3,2,1,0:T(4,128)}, f32[4,3,4,1024]{3,2,1,0:T(4,128)S(1)}, u32[]{:S(2)}, u32[]{:S(2)}) %collective-permute-start.2) | collective-permute-done | bytes 196640 | tf_op jit(solution)/shard_map/ppermute | solution.py:409
  10.7 0.1 pad_maximum_fusion
  10.8 0.1 collective-permute-start.4
  10.9 0.1 pad_maximum_fusion.1
  11.1 1.6 %collective-permute-start.5 = (f32[10,3,3,1024]{3,2,1,0:T(4,128)S(1)}, f32[10,3,3,1024]{3,2,1,0:T(4,128)S(1)}, u32[]{:S(2)}, u32[]{:S(2)}) collective-permute-start(f32[10,3,3,1024]{3,2,1,0:T(4,128)S(1)} %pad_maximum_fusion.1), channel_id=1, source_target_pairs={{1,0},{2,1},{3,2},{4,3},{5,4},{6,5},{7,6},{0,7},{9,8},{10,9},{11,1... | collective-permute-start | bytes 1105928 | tf_op jit(solution)/shard_map/ppermute | solution.py:409
  12.9 0.1 copy.18
  13.4 4.1 %layer_first.1 = (f32[3,8,256]{2,1,0:T(8,128)S(1)}, bf16[24,192,256]{2,1,0:T(8,128)(2,1)S(1)}, bf16[24,32,256]{2,1,0:T(8,128)(2,1)S(1)}) custom-call(s32[8,2]{1,0:T(8,128)S(1)} %bitcast.17, f32[10,8,256]{2,1,0:T(8,128)S(1)} %pad_maximum_fusion.2.own_ref, f32[10,8,256]{2,1,0:T(8,128)S(1)} %collective-permute-done.before_ref, ...), custom_call_target="tpu_custom_call" | custom-call | flops 1048576000 | bytes 1048576 | tf_op jit(solution)/shard_map/layer_first/pallas_call | solution.py:370
  17.5 1.6 %collective-permute-done.4.left_ref = f32[10,3,3,1024]{3,2,1,0:T(4,128)S(1)} collective-permute-done((f32[10,3,3,1024]{3,2,1,0:T(4,128)S(1)}, f32[10,3,3,1024]{3,2,1,0:T(4,128)S(1)}, u32[]{:S(2)}, u32[]{:S(2)}) %collective-permute-start.4) | collective-permute-done | bytes 368672 | tf_op jit(solution)/shard_map/ppermute | solution.py:409
  19.1 37.3 %near.1 = (f32[4,3,4,1024]{3,2,1,0:T(4,128)S(1)}, f32[8,128]{1,0:T(8,128)S(1)}, f32[8,384,128]{2,1,0:T(8,128)S(1)}) custom-call(s32[32]{0:T(128)S(1)} %reshape.21.near_ref, s32[16]{0:T(128)S(1)} %reshape.22.wall_ref, f32[4,3,4,1024]{3,2,1,0:T(4,128)S(1)} %collective-permute-done.2.below_ref, f32[4,3,4,1024]{3,2,1,0:T(4,128)S(1)} %bitcast.13, ...), custom_call_target="tpu_custom_call" | custom-call | flops 33554432000 | bytes 8388608 | tf_op jit(solution)/shard_map/near/pallas_call | solution.py:217
  56.4 1.8 %collective-permute-start.6 = (f32[8,128]{1,0:T(8,128)S(1)}, f32[8,128]{1,0:T(8,128)S(1)}, u32[]{:S(2)}, u32[]{:S(2)}) collective-permute-start(f32[8,128]{1,0:T(8,128)S(1)} %get-tuple-element.15), channel_id=1, source_target_pairs={{0,1},{1,0},{2,3},{3,2},{4,5},{5,4},{6,7},{7,6},{8,9},{9,8},{10,11... | collective-permute-start | bytes 12296 | tf_op jit(solution)/shard_map/ppermute | solution.py:432
  58.2 0.8 collective-permute-done.6
  59.0 0.9 collective-permute-start.9
  59.9 2.0 %collective-permute-start.8 = (f32[8,128]{1,0:T(8,128)S(1)}, f32[8,128]{1,0:T(8,128)S(1)}, u32[]{:S(2)}, u32[]{:S(2)}) collective-permute-start(f32[8,128]{1,0:T(8,128)S(1)} %max.21), channel_id=1, source_target_pairs={{0,4},{1,5},{2,6},{3,7},{4,0},{5,1},{6,2},{7,3},{8,12},{9,13},{10,... | collective-permute-start | bytes 12296 | tf_op jit(solution)/shard_map/ppermute | solution.py:432
  61.9 2.6 %collective-permute-start.7 = (f32[8,128]{1,0:T(8,128)S(1)}, f32[8,128]{1,0:T(8,128)S(1)}, u32[]{:S(2)}, u32[]{:S(2)}) collective-permute-start(f32[8,128]{1,0:T(8,128)S(1)} %max.21), channel_id=1, source_target_pairs={{0,2},{1,3},{2,4},{3,5},{4,6},{5,7},{6,0},{7,1},{8,10},{9,11},{10,... | collective-permute-start | bytes 12296 | tf_op jit(solution)/shard_map/ppermute | solution.py:432
  64.5 4.9 %layer_second.1.layer_ref = f32[3,8,256]{2,1,0:T(8,128)S(1)} custom-call(s32[8,3]{1,0:T(8,128)S(1)} %slice.39.listed_ref, f32[10,8,256]{2,1,0:T(8,128)S(1)} %pad_maximum_fusion.2.own_ref, bf16[24,192,256]{2,1,0:T(8,128)(2,1)S(1)} %get-tuple-element.19.left_ref, bf16[24,32,256]{2,1,0:T(8,128)(2,1)S(1)} %get-tuple-element.20.feature_ref, ...), custom_call_target="tpu_custom_call" | custom-call | flops 1572864000 | bytes 1048576 | tf_op jit(solution)/shard_map/layer_second/pallas_call | solution.py:370
  69.5 2.4 %collective-permute-start.12 = (f32[8,128]{1,0:T(8,128)S(1)}, f32[8,128]{1,0:T(8,128)S(1)}, u32[]{:S(2)}, u32[]{:S(2)}) collective-permute-start(f32[8,128]{1,0:T(8,128)S(1)} %maximum_maximum_fusion.1), channel_id=1, source_target_pairs={{0,24},{8,0},{16,8},{24,16},{32,56},{40,32},{48,40},{56,48},{64,88... | collective-permute-start | bytes 12296 | tf_op jit(solution)/shard_map/ppermute | solution.py:432
  71.9 3.6 %collective-permute-start.11 = (f32[8,128]{1,0:T(8,128)S(1)}, f32[8,128]{1,0:T(8,128)S(1)}, u32[]{:S(2)}, u32[]{:S(2)}) collective-permute-start(f32[8,128]{1,0:T(8,128)S(1)} %maximum_maximum_fusion.1), channel_id=1, source_target_pairs={{0,16},{8,24},{16,0},{24,8},{32,48},{40,56},{48,32},{56,40},{64,80... | collective-permute-start | bytes 12296 | tf_op jit(solution)/shard_map/ppermute | solution.py:432
  75.5 2.0 %collective-permute-start.10 = (f32[8,128]{1,0:T(8,128)S(1)}, f32[8,128]{1,0:T(8,128)S(1)}, u32[]{:S(2)}, u32[]{:S(2)}) collective-permute-start(f32[8,128]{1,0:T(8,128)S(1)} %maximum_maximum_fusion.1), channel_id=1, source_target_pairs={{0,8},{8,16},{16,24},{24,0},{32,40},{40,48},{48,56},{56,32},{64,72... | collective-permute-start | bytes 12296 | tf_op jit(solution)/shard_map/ppermute | solution.py:432
  77.5 3.5 %wall_0.1.layer_ref = f32[3,8,256]{2,1,0:T(8,128)S(1)} custom-call(f32[8,384,128]{2,1,0:T(8,128)S(1)} %get-tuple-element.17.raw_ref, f32[3,8,256]{2,1,0:T(8,128)S(1)} %bitcast.15, f32[3,8,256]{2,1,0:T(8,128)S(1)} %layer_second.1.layer_ref), custom_call_target="tpu_custom_call" | custom-call | flops 2097152000 | bytes 2097152 | tf_op jit(solution)/shard_map/wall_0/pallas_call | solution.py:266
  81.1 0.2 collective-permute-start.15
  81.2 6.0 %collective-permute-start.14 = (f32[8,128]{1,0:T(8,128)S(1)}, f32[8,128]{1,0:T(8,128)S(1)}, u32[]{:S(2)}, u32[]{:S(2)}) collective-permute-start(f32[8,128]{1,0:T(8,128)S(1)} %maximum_maximum_fusion.refs_0_), channel_id=1, source_target_pairs={{0,64},{8,72},{16,80},{24,88},{32,96},{40,104},{48,112},{56,120},{... | collective-permute-start | bytes 12296 | tf_op jit(solution)/shard_map/ppermute | solution.py:432
  87.2 2.5 %collective-permute-start.13 = (f32[8,128]{1,0:T(8,128)S(1)}, f32[8,128]{1,0:T(8,128)S(1)}, u32[]{:S(2)}, u32[]{:S(2)}) collective-permute-start(f32[8,128]{1,0:T(8,128)S(1)} %maximum_maximum_fusion.refs_0_), channel_id=1, source_target_pairs={{0,32},{8,40},{16,48},{24,56},{32,64},{40,72},{48,80},{56,88},{64,... | collective-permute-start | bytes 12296 | tf_op jit(solution)/shard_map/ppermute | solution.py:432
  89.8 4.1 %wall_1.1 = f32[3,8,256]{2,1,0:T(8,128)} custom-call(f32[8,384,128]{2,1,0:T(8,128)S(1)} %get-tuple-element.17.raw_ref, f32[3,8,256]{2,1,0:T(8,128)S(1)} %bitcast.16, f32[3,8,256]{2,1,0:T(8,128)S(1)} %wall_0.1.layer_ref), custom_call_target="tpu_custom_call" | custom-call | flops 2097152000 | bytes 2097152 | tf_op jit(solution)/shard_map/wall_1/pallas_call | solution.py:266
  94.0 0.5 copy-done.5
  94.5 1.8 %move.1 = f32[4,3,4,1024]{3,2,1,0:T(4,128)} custom-call(f32[8,128]{1,0:T(8,128)} %copy-done.4, f32[8,128]{1,0:T(8,128)} %copy-done.7, f32[8,128]{1,0:T(8,128)} %copy-done.6, f32[8,128]{1,0:T(8,128)} %copy-done.5, f32[4,3,4,1024]{3,2,1,0:T(4,128)} %bitcast.12, f32[4,3,4,1024]{3,2,1,0:T(4,128)} %copy-done.1), custom_call_target="tpu_custom_call" | custom-call | tf_op jit(solution)/shard_map/move/pallas_call | solution.py:396
  (47 shorter events, 0.8 us)
Async XLA Ops:
  0.6 12.1 %copy-start.9 = (s32[8,2]{0,1:T(2,128)S(1)}, s32[8,2]{0,1:T(2,128)}, u32[]{:S(2)}) copy-start(s32[8,2]{0,1:T(2,128)} %param.23) | copy-start | bytes 196
  0.6 12.5 %copy-start.8 = (f32[4,4]{1,0:T(4,128)S(1)}, f32[4,4]{1,0:T(4,128)}, u32[]{:S(2)}) copy-start(f32[4,4]{1,0:T(4,128)} %param.13) | copy-start | bytes 196
  1.5 11.9 %collective-permute-start.1 = (f32[10,8,256]{2,1,0:T(8,128)S(1)}, f32[10,8,256]{2,1,0:T(8,128)S(1)}, u32[]{:S(2)}, u32[]{:S(2)}) collective-permute-start(f32[10,8,256]{2,1,0:T(8,128)S(1)} %pad_maximum_fusion.2.own_ref), channel_id=1, source_target_pairs={{1,0},{2,1},{3,2},{4,3},{5,4},{6,5},{7,6},{8,7},{9,8},{10,9},{11,1... | collective-permute-start | bytes 245768 | tf_op jit(solution)/shard_map/ppermute | solution.py:409
  1.5 11.8 %collective-permute-start = (f32[10,8,256]{2,1,0:T(8,128)S(1)}, f32[10,8,256]{2,1,0:T(8,128)S(1)}, u32[]{:S(2)}, u32[]{:S(2)}) collective-permute-start(f32[10,8,256]{2,1,0:T(8,128)S(1)} %pad_maximum_fusion.2.own_ref), channel_id=1, source_target_pairs={{0,1},{1,2},{2,3},{3,4},{4,5},{5,6},{6,7},{7,8},{8,9},{9,10},{10,1... | collective-permute-start | bytes 245768 | tf_op jit(solution)/shard_map/ppermute | solution.py:409
  2.0 8.6 %collective-permute-start.3 = (f32[4,3,4,1024]{3,2,1,0:T(4,128)}, f32[4,3,4,1024]{3,2,1,0:T(4,128)S(1)}, u32[]{:S(2)}, u32[]{:S(2)}) collective-permute-start(f32[4,3,4,1024]{3,2,1,0:T(4,128)} %bitcast.9), channel_id=1, source_target_pairs={{8,0},{16,8},{24,16},{32,24},{40,32},{48,40},{56,48},{64,56},{72,6... | collective-permute-start | bytes 589832 | tf_op jit(solution)/shard_map/ppermute | solution.py:409
  2.5 8.0 %collective-permute-start.2 = (f32[4,3,4,1024]{3,2,1,0:T(4,128)}, f32[4,3,4,1024]{3,2,1,0:T(4,128)S(1)}, u32[]{:S(2)}, u32[]{:S(2)}) collective-permute-start(f32[4,3,4,1024]{3,2,1,0:T(4,128)} %bitcast.10), channel_id=1, source_target_pairs={{0,8},{8,16},{16,24},{24,32},{32,40},{40,48},{48,56},{56,64},{64,7... | collective-permute-start | bytes 589832 | tf_op jit(solution)/shard_map/ppermute | solution.py:409
  10.8 8.3 %collective-permute-start.4 = (f32[10,3,3,1024]{3,2,1,0:T(4,128)S(1)}, f32[10,3,3,1024]{3,2,1,0:T(4,128)S(1)}, u32[]{:S(2)}, u32[]{:S(2)}) collective-permute-start(f32[10,3,3,1024]{3,2,1,0:T(4,128)S(1)} %pad_maximum_fusion), channel_id=1, source_target_pairs={{0,1},{1,2},{2,3},{3,4},{4,5},{5,6},{6,7},{7,0},{8,9},{9,10},{10,1... | collective-permute-start | bytes 1105928 | tf_op jit(solution)/shard_map/ppermute | solution.py:409
  11.0 8.0 %copy-start = (f32[4,4,3,1024]{3,1,2,0:T(4,128)S(1)}, f32[4,4,3,1024]{3,1,2,0:T(4,128)}, u32[]{:S(2)}) copy-start(f32[4,4,3,1024]{3,1,2,0:T(4,128)} %param.12) | copy-start | bytes 589828
  11.1 8.0 %copy-start.3 = (f32[1024]{0:T(1024)S(1)}, f32[1024]{0:T(1024)}, u32[]{:S(2)}) copy-start(f32[1024]{0:T(1024)} %param.16) | copy-start | bytes 12292
  11.1 8.0 %collective-permute-start.5 = (f32[10,3,3,1024]{3,2,1,0:T(4,128)S(1)}, f32[10,3,3,1024]{3,2,1,0:T(4,128)S(1)}, u32[]{:S(2)}, u32[]{:S(2)}) collective-permute-start(f32[10,3,3,1024]{3,2,1,0:T(4,128)S(1)} %pad_maximum_fusion.1), channel_id=1, source_target_pairs={{1,0},{2,1},{3,2},{4,3},{5,4},{6,5},{7,6},{0,7},{9,8},{10,9},{11,1... | collective-permute-start | bytes 1105928 | tf_op jit(solution)/shard_map/ppermute | solution.py:409
  56.4 13.1 %copy-start.1 = (f32[4,3,4,1024]{3,2,1,0:T(4,128)}, f32[4,3,4,1024]{3,2,1,0:T(4,128)S(1)}, u32[]{:S(2)}) copy-start(f32[4,3,4,1024]{3,2,1,0:T(4,128)S(1)} %get-tuple-element.16.refs_5_) | copy-start | bytes 589828
  56.4 2.6 %collective-permute-start.6 = (f32[8,128]{1,0:T(8,128)S(1)}, f32[8,128]{1,0:T(8,128)S(1)}, u32[]{:S(2)}, u32[]{:S(2)}) collective-permute-start(f32[8,128]{1,0:T(8,128)S(1)} %get-tuple-element.15), channel_id=1, source_target_pairs={{0,1},{1,0},{2,3},{3,2},{4,5},{5,4},{6,7},{7,6},{8,9},{9,8},{10,11... | collective-permute-start | bytes 12296 | tf_op jit(solution)/shard_map/ppermute | solution.py:432
  59.0 10.5 %collective-permute-start.9 = (f32[8,128]{1,0:T(8,128)S(1)}, f32[8,128]{1,0:T(8,128)S(1)}, u32[]{:S(2)}, u32[]{:S(2)}) collective-permute-start(f32[8,128]{1,0:T(8,128)S(1)} %max.21), channel_id=1, source_target_pairs={{0,6},{1,7},{2,0},{3,1},{4,2},{5,3},{6,4},{7,5},{8,14},{9,15},{10,... | collective-permute-start | bytes 12296 | tf_op jit(solution)/shard_map/ppermute | solution.py:432
  59.9 9.6 %collective-permute-start.8 = (f32[8,128]{1,0:T(8,128)S(1)}, f32[8,128]{1,0:T(8,128)S(1)}, u32[]{:S(2)}, u32[]{:S(2)}) collective-permute-start(f32[8,128]{1,0:T(8,128)S(1)} %max.21), channel_id=1, source_target_pairs={{0,4},{1,5},{2,6},{3,7},{4,0},{5,1},{6,2},{7,3},{8,12},{9,13},{10,... | collective-permute-start | bytes 12296 | tf_op jit(solution)/shard_map/ppermute | solution.py:432
  61.9 7.6 %collective-permute-start.7 = (f32[8,128]{1,0:T(8,128)S(1)}, f32[8,128]{1,0:T(8,128)S(1)}, u32[]{:S(2)}, u32[]{:S(2)}) collective-permute-start(f32[8,128]{1,0:T(8,128)S(1)} %max.21), channel_id=1, source_target_pairs={{0,2},{1,3},{2,4},{3,5},{4,6},{5,7},{6,0},{7,1},{8,10},{9,11},{10,... | collective-permute-start | bytes 12296 | tf_op jit(solution)/shard_map/ppermute | solution.py:432
  64.5 13.0 %copy-start.2 = (f32[8,3,256]{2,0,1:T(8,128)S(1)}, f32[8,3,256]{2,0,1:T(8,128)}, u32[]{:S(2)}) copy-start(f32[8,3,256]{2,0,1:T(8,128)} %param.18) | copy-start | bytes 73732
  69.5 11.5 %collective-permute-start.12 = (f32[8,128]{1,0:T(8,128)S(1)}, f32[8,128]{1,0:T(8,128)S(1)}, u32[]{:S(2)}, u32[]{:S(2)}) collective-permute-start(f32[8,128]{1,0:T(8,128)S(1)} %maximum_maximum_fusion.1), channel_id=1, source_target_pairs={{0,24},{8,0},{16,8},{24,16},{32,56},{40,32},{48,40},{56,48},{64,88... | collective-permute-start | bytes 12296 | tf_op jit(solution)/shard_map/ppermute | solution.py:432
  71.9 9.1 %collective-permute-start.11 = (f32[8,128]{1,0:T(8,128)S(1)}, f32[8,128]{1,0:T(8,128)S(1)}, u32[]{:S(2)}, u32[]{:S(2)}) collective-permute-start(f32[8,128]{1,0:T(8,128)S(1)} %maximum_maximum_fusion.1), channel_id=1, source_target_pairs={{0,16},{8,24},{16,0},{24,8},{32,48},{40,56},{48,32},{56,40},{64,80... | collective-permute-start | bytes 12296 | tf_op jit(solution)/shard_map/ppermute | solution.py:432
  75.5 5.5 %collective-permute-start.10 = (f32[8,128]{1,0:T(8,128)S(1)}, f32[8,128]{1,0:T(8,128)S(1)}, u32[]{:S(2)}, u32[]{:S(2)}) collective-permute-start(f32[8,128]{1,0:T(8,128)S(1)} %maximum_maximum_fusion.1), channel_id=1, source_target_pairs={{0,8},{8,16},{16,24},{24,0},{32,40},{40,48},{48,56},{56,32},{64,72... | collective-permute-start | bytes 12296 | tf_op jit(solution)/shard_map/ppermute | solution.py:432
  81.1 12.8 %copy-start.4 = (f32[8,128]{1,0:T(8,128)}, f32[8,128]{1,0:T(8,128)S(1)}, u32[]{:S(2)}) copy-start(f32[8,128]{1,0:T(8,128)S(1)} %maximum_maximum_fusion.refs_0_) | copy-start | bytes 12292
  81.1 12.8 %collective-permute-start.15 = (f32[8,128]{1,0:T(8,128)S(1)}, f32[8,128]{1,0:T(8,128)S(1)}, u32[]{:S(2)}, u32[]{:S(2)}) collective-permute-start(f32[8,128]{1,0:T(8,128)S(1)} %maximum_maximum_fusion.refs_0_), channel_id=1, source_target_pairs={{0,96},{8,104},{16,112},{24,120},{32,0},{40,8},{48,16},{56,24},{64... | collective-permute-start | bytes 12296 | tf_op jit(solution)/shard_map/ppermute | solution.py:432
  81.2 12.7 %collective-permute-start.14 = (f32[8,128]{1,0:T(8,128)S(1)}, f32[8,128]{1,0:T(8,128)S(1)}, u32[]{:S(2)}, u32[]{:S(2)}) collective-permute-start(f32[8,128]{1,0:T(8,128)S(1)} %maximum_maximum_fusion.refs_0_), channel_id=1, source_target_pairs={{0,64},{8,72},{16,80},{24,88},{32,96},{40,104},{48,112},{56,120},{... | collective-permute-start | bytes 12296 | tf_op jit(solution)/shard_map/ppermute | solution.py:432
  87.2 6.7 %collective-permute-start.13 = (f32[8,128]{1,0:T(8,128)S(1)}, f32[8,128]{1,0:T(8,128)S(1)}, u32[]{:S(2)}, u32[]{:S(2)}) collective-permute-start(f32[8,128]{1,0:T(8,128)S(1)} %maximum_maximum_fusion.refs_0_), channel_id=1, source_target_pairs={{0,32},{8,40},{16,48},{24,56},{32,64},{40,72},{48,80},{56,88},{64,... | collective-permute-start | bytes 12296 | tf_op jit(solution)/shard_map/ppermute | solution.py:432
  93.9 0.6 copy-start.5
  93.9 0.6 copy-start.6
  93.9 0.6 copy-start.7

commit v4 on v3

--- a/solution.py
+++ b/solution.py
@@ -118,8 +118,12 @@
     below_ref,
     own_ref,
     above_ref,
+    left_below_ref,
     left_ref,
+    left_above_ref,
+    right_below_ref,
     right_ref,
+    right_above_ref,
     drag_ref,
     analysis_ref,
     stiffness_ref,
@@ -147,12 +151,15 @@
     near = near_ref.shape[0]
     wall = wall_ref.shape[0]
     slots = own + near + wall
-    ext_ref[:, :, 0:HALO, :] = left_ref[...]
-    inner = slice(HALO, HALO + cols)
-    ext_ref[0:HALO, :, inner, :] = below_ref[rows - HALO :]
-    ext_ref[HALO : HALO + rows, :, inner, :] = own_ref[...]
-    ext_ref[HALO + rows :, :, inner, :] = above_ref[0:HALO]
-    ext_ref[:, :, HALO + cols :, :] = right_ref[...]
+    columns = (
+        (slice(0, HALO), (left_below_ref, left_ref, left_above_ref)),
+        (slice(HALO, HALO + cols), (below_ref, own_ref, above_ref)),
+        (slice(HALO + cols, cols + 2 * HALO), (right_below_ref, right_ref, right_above_ref)),
+    )
+    for where, (before, beside, after) in columns:
+        ext_ref[0:HALO, :, where, :] = before[rows - HALO :]
+        ext_ref[HALO : HALO + rows, :, where, :] = beside[...]
+        ext_ref[HALO + rows :, :, where, :] = after[0:HALO]
     for r in range(rows):
         for d in range(3):
             pos_ref[d, r * cols : (r + 1) * cols, :] = own_ref[r, d]
@@ -216,7 +223,7 @@
     pairs = own * points * (near // own) * points
     return pl.pallas_call(
         near_kernel,
-        in_specs=[in_smem] * 2 + [in_vmem] * 6 + [in_hbm, in_vmem, in_hbm],
+        in_specs=[in_smem] * 2 + [in_vmem] * 10 + [in_hbm, in_vmem, in_hbm],
         out_specs=[in_vmem] * 3,
         out_shape=[
             jax.ShapeDtypeStruct((rows, 3, cols, points), F32),
@@ -238,7 +245,7 @@
             flops=1000 * pairs, bytes_accessed=8 * 2**20, transcendentals=pairs
         ),
         name="near",
-    )(near_code, wall_code, below, pos, above, left, right, drag, *tables)
+    )(near_code, wall_code, below, pos, above, *left, *right, drag, *tables)
 
 
 def wall_kernel(stage, per, raw_ref, pos_ref, layer_ref, out_ref, target_ref, moment_ref):
@@ -398,6 +405,7 @@
         in_specs=[in_vmem] * (len(tops) + 2),
         out_specs=in_vmem,
         out_shape=jax.ShapeDtypeStruct(pos.shape, F32),
+        compiler_params=pltpu.CompilerParams(vmem_limit_bytes=8 * 2**20),
         name="move",
     )(*tops, pos, velocity)
 
@@ -407,6 +415,16 @@
     up = [(i, (i + 1) % size) for i in range(size)]
     down = [(b, a) for a, b in up]
     return lax.ppermute(high, axis, up), lax.ppermute(low, axis, down)
+
+
+def shifted(value, up, along):
+    rows, cols = lax.axis_size("cx"), lax.axis_size("cy")
+    pairs = [
+        (i * cols + j, (i + up) % rows * cols + (j + along) % cols)
+        for i in range(rows)
+        for j in range(cols)
+    ]
+    return lax.ppermute(value, AXES, pairs)
 
 
 def rotations(outer, inner, along_outer):
@@ -459,12 +477,11 @@
     walls = [jnp.transpose(v, (1, 0, 2)) for v in (wall_pos, wall_normal, density)]
     packed = jnp.concatenate(walls + [wall_weight[None]], axis=0)
 
-    below, above = neighbours(pos, pos, "cx")
+    below, above = shifted(pos, 1, 0), shifted(pos, -1, 0)
     wall_below, wall_above = neighbours(packed, packed, AXES)
-    strips = [v[:, :, c : c + HALO] for c in (0, cols - HALO) for v in (below[rows - HALO :], pos, above[:HALO])]
-    left, right = neighbours(
-        jnp.concatenate(strips[:3], axis=0), jnp.concatenate(strips[3:], axis=0), "cy"
-    )
+    low, high = pos[:, :, :HALO], pos[:, :, cols - HALO :]
+    left = [shifted(high, up, 1) for up in (1, 0, -1)]
+    right = [shifted(low, up, -1) for up in (1, 0, -1)]
 
     patches = wall_pos.shape[0]
     all_patches = patches * lax.axis_size(AXES)

time: 96.6 us -> 104 us (1.077)
  the two profiles are of different devices: /device:TPU:76 before, /device:TPU:0 now
where the time goes in v4:
time: 104 us; the launch traced here: 103 us
  Pallas kernels  54.8 us (53%)
  starting transfers between devices  33.6 us (32%)
  waiting for transfers between devices  8.08 us (8%)
  local copies, waits for them, and re-layouts  3.06 us (3%)
  other arithmetic  2.33 us (2%)
    pallas_call x1, Pallas kernels, near_part(): pl.pallas_call(near_kernel, in_specs=[in_smem] * 2 + [in_vmem] * 10 + [in...  37.3 us
    ppermute x8, starting transfers between devices, shifted(): return lax.ppermute(value, AXES, pairs)  19.1 us
    pallas_call x2, Pallas kernels, layer_part(): pl.pallas_call(kernel, in_specs=[pl.BlockSpec(memory_space=pltpu.SMEM)] +...  9.06 us
    ppermute x2, starting transfers between devices, neighbours(): return (lax.ppermute(high, axis, up), lax.ppermute(low, axis, down))  8.24 us
    pallas_call x2, Pallas kernels, wall_part(): pl.pallas_call(functools.partial(wall_kernel, stage, per), in_specs=[in_v...  7.67 us
    ppermute x10, starting transfers between devices, over_all(): lax.ppermute(value, axis, pairs)  6.21 us
    ppermute x8, waiting for transfers between devices, shifted(): return lax.ppermute(value, AXES, pairs)  6.11 us
  transfers between devices with their start and end apart: 20, of which 4 were waited for; matrix products, arithmetic and copies ran while one was open for 4% of the time, Pallas kernels for 16%

profile of v4, /device:TPU:0, one launch (start us, length us, event | category | flops | bytes accessed | tf_op | source)
XLA Modules:
  0.0 102.7 jit_solution(2685158028390098446)
XLA Ops:
  0.6 0.8 pad_maximum_fusion.own_ref
  1.4 8.2 %collective-permute-start.1 = (f32[10,8,256]{2,1,0:T(8,128)S(1)}, f32[10,8,256]{2,1,0:T(8,128)S(1)}, u32[]{:S(2)}, u32[]{:S(2)}) collective-permute-start(f32[10,8,256]{2,1,0:T(8,128)S(1)} %pad_maximum_fusion.own_ref), channel_id=1, source_target_pairs={{1,0},{2,1},{3,2},{4,3},{5,4},{6,5},{7,6},{8,7},{9,8},{10,9},{11,1... | collective-permute-start | bytes 245768 | tf_op jit(solution)/shard_map/ppermute | solution.py:417
  9.7 1.1 %fusion.11 = (f32[4,3,3,1024]{3,2,1,0:T(4,128)S(1)}, f32[4,3,3,1024]{3,2,1,0:T(4,128)S(1)}) fusion(f32[4,3,4,1024]{3,2,1,0:T(4,128)} %bitcast.9), kind=kLoop, calls=%fused_computation.41 | loop fusion | bytes 589824 | tf_op jit(solution)/shard_map/slice | solution.py:482
  10.8 7.2 %collective-permute-start.9 = (f32[4,3,3,1024]{3,2,1,0:T(4,128)S(1)}, f32[4,3,3,1024]{3,2,1,0:T(4,128)S(1)}, u32[]{:S(2)}, u32[]{:S(2)}) collective-permute-start(f32[4,3,3,1024]{3,2,1,0:T(4,128)S(1)} %get-tuple-element.22), channel_id=1, source_target_pairs={{0,127},{1,120},{2,121},{3,122},{4,123},{5,124},{6,125},{7,126},{8... | collective-permute-start | bytes 442376 | tf_op jit(solution)/shard_map/ppermute | solution.py:427
  18.0 0.8 copy.19
  18.8 0.7 fusion
  19.5 0.7 fusion.6
  20.3 0.7 collective-permute-start.3
  20.9 1.4 %collective-permute-start.2 = (f32[4,3,4,1024]{3,2,1,0:T(4,128)}, f32[4,3,4,1024]{3,2,1,0:T(4,128)S(1)}, u32[]{:S(2)}, u32[]{:S(2)}) collective-permute-start(f32[4,3,4,1024]{3,2,1,0:T(4,128)} %bitcast.11), channel_id=1, source_target_pairs={{0,8},{1,9},{2,10},{3,11},{4,12},{5,13},{6,14},{7,15},{8,16},{9,17... | collective-permute-start | bytes 589832 | tf_op jit(solution)/shard_map/ppermute | solution.py:427
  22.4 7.8 %collective-permute-start.6 = (f32[4,3,3,1024]{3,2,1,0:T(4,128)S(1)}, f32[4,3,3,1024]{3,2,1,0:T(4,128)S(1)}, u32[]{:S(2)}, u32[]{:S(2)}) collective-permute-start(f32[4,3,3,1024]{3,2,1,0:T(4,128)S(1)} %get-tuple-element.23), channel_id=1, source_target_pairs={{0,121},{1,122},{2,123},{3,124},{4,125},{5,126},{6,127},{7,120},{8... | collective-permute-start | bytes 442376 | tf_op jit(solution)/shard_map/ppermute | solution.py:427
  30.2 2.0 %collective-permute-start.5 = (f32[4,3,3,1024]{3,2,1,0:T(4,128)S(1)}, f32[4,3,3,1024]{3,2,1,0:T(4,128)S(1)}, u32[]{:S(2)}, u32[]{:S(2)}) collective-permute-start(f32[4,3,3,1024]{3,2,1,0:T(4,128)S(1)} %get-tuple-element.23), channel_id=1, source_target_pairs={{0,1},{1,2},{2,3},{3,4},{4,5},{5,6},{6,7},{7,0},{8,9},{9,10},{10,1... | collective-permute-start | bytes 442376 | tf_op jit(solution)/shard_map/ppermute | solution.py:427
  32.3 0.1 copy.20
  32.4 0.1 reshape.22.wall_ref
  32.5 0.1 copy.18
  32.6 0.1 reshape.21.near_ref
  32.7 0.8 reshape.24.drag_ref
  33.4 4.1 %layer_first.1 = (f32[3,8,256]{2,1,0:T(8,128)S(1)}, bf16[24,192,256]{2,1,0:T(8,128)(2,1)S(1)}, bf16[24,32,256]{2,1,0:T(8,128)(2,1)S(1)}) custom-call(s32[8,2]{1,0:T(8,128)S(1)} %bitcast.17, f32[10,8,256]{2,1,0:T(8,128)S(1)} %pad_maximum_fusion.own_ref, f32[10,8,256]{2,1,0:T(8,128)S(1)} %collective-permute-done.before_ref, ...), custom_call_target="tpu_custom_call" | custom-call | flops 1048576000 | bytes 1048576 | tf_op jit(solution)/shard_map/layer_first/pallas_call | solution.py:377
  37.6 6.1 %collective-permute-done.4.left_below_ref = f32[4,3,3,1024]{3,2,1,0:T(4,128)S(1)} collective-permute-done((f32[4,3,3,1024]{3,2,1,0:T(4,128)S(1)}, f32[4,3,3,1024]{3,2,1,0:T(4,128)S(1)}, u32[]{:S(2)}, u32[]{:S(2)}) %collective-permute-start.4) | collective-permute-done | bytes 147488 | tf_op jit(solution)/shard_map/ppermute | solution.py:427
  43.7 37.3 %near.1 = (f32[4,3,4,1024]{3,2,1,0:T(4,128)S(1)}, f32[8,128]{1,0:T(8,128)S(1)}, f32[8,384,128]{2,1,0:T(8,128)S(1)}) custom-call(s32[32]{0:T(128)S(1)} %reshape.21.near_ref, s32[16]{0:T(128)S(1)} %reshape.22.wall_ref, f32[4,3,4,1024]{3,2,1,0:T(4,128)S(1)} %collective-permute-done.2.below_ref, f32[4,3,4,1024]{3,2,1,0:T(4,128)S(1)} %bitcast.12, ...), custom_call_target="tpu_custom_call" | custom-call | flops 33554432000 | bytes 8388608 | tf_op jit(solution)/shard_map/near/pallas_call | solution.py:224
  81.0 0.1 collective-permute-start.10
  81.1 1.2 %collective-permute-done.10 = f32[8,128]{1,0:T(8,128)S(1)} collective-permute-done((f32[8,128]{1,0:T(8,128)S(1)}, f32[8,128]{1,0:T(8,128)S(1)}, u32[]{:S(2)}, u32[]{:S(2)}) %collective-permute-start.10) | collective-permute-done | bytes 4128 | tf_op jit(solution)/shard_map/ppermute | solution.py:450
  82.3 2.0 %collective-permute-start.11 = (f32[8,128]{1,0:T(8,128)S(1)}, f32[8,128]{1,0:T(8,128)S(1)}, u32[]{:S(2)}, u32[]{:S(2)}) collective-permute-start(f32[8,128]{1,0:T(8,128)S(1)} %max.21), channel_id=1, source_target_pairs={{0,2},{1,3},{2,4},{3,5},{4,6},{5,7},{6,0},{7,1},{8,10},{9,11},{10,... | collective-permute-start | bytes 12296 | tf_op jit(solution)/shard_map/ppermute | solution.py:450
  84.3 4.9 %layer_second.1.layer_ref = f32[3,8,256]{2,1,0:T(8,128)S(1)} custom-call(s32[8,3]{1,0:T(8,128)S(1)} %slice.15.listed_ref, f32[10,8,256]{2,1,0:T(8,128)S(1)} %pad_maximum_fusion.own_ref, bf16[24,192,256]{2,1,0:T(8,128)(2,1)S(1)} %get-tuple-element.19.left_ref, bf16[24,32,256]{2,1,0:T(8,128)(2,1)S(1)} %get-tuple-element.20.feature_ref, ...), custom_call_target="tpu_custom_call" | custom-call | flops 1572864000 | bytes 1048576 | tf_op jit(solution)/shard_map/layer_second/pallas_call | solution.py:377
  89.3 0.1 collective-permute-start.16
  89.4 0.1 collective-permute-start.15
  89.5 1.9 %collective-permute-start.14 = (f32[8,128]{1,0:T(8,128)S(1)}, f32[8,128]{1,0:T(8,128)S(1)}, u32[]{:S(2)}, u32[]{:S(2)}) collective-permute-start(f32[8,128]{1,0:T(8,128)S(1)} %maximum_maximum_fusion.1), channel_id=1, source_target_pairs={{0,8},{8,16},{16,24},{24,0},{32,40},{40,48},{48,56},{56,32},{64,72... | collective-permute-start | bytes 12296 | tf_op jit(solution)/shard_map/ppermute | solution.py:450
  91.4 3.5 %wall_0.1.layer_ref = f32[3,8,256]{2,1,0:T(8,128)S(1)} custom-call(f32[8,384,128]{2,1,0:T(8,128)S(1)} %get-tuple-element.17.raw_ref, f32[3,8,256]{2,1,0:T(8,128)S(1)} %bitcast.15, f32[3,8,256]{2,1,0:T(8,128)S(1)} %layer_second.1.layer_ref), custom_call_target="tpu_custom_call" | custom-call | flops 2097152000 | bytes 2097152 | tf_op jit(solution)/shard_map/wall_0/pallas_call | solution.py:273
  94.9 0.7 collective-permute-done.14
  95.7 1.9 %collective-permute-start.17 = (f32[8,128]{1,0:T(8,128)S(1)}, f32[8,128]{1,0:T(8,128)S(1)}, u32[]{:S(2)}, u32[]{:S(2)}) collective-permute-start(f32[8,128]{1,0:T(8,128)S(1)} %maximum_maximum_fusion.refs_0_), channel_id=1, source_target_pairs={{0,32},{8,40},{16,48},{24,56},{32,64},{40,72},{48,80},{56,88},{64,... | collective-permute-start | bytes 12296 | tf_op jit(solution)/shard_map/ppermute | solution.py:450
  97.7 4.1 %wall_1.1 = f32[3,8,256]{2,1,0:T(8,128)} custom-call(f32[8,384,128]{2,1,0:T(8,128)S(1)} %get-tuple-element.17.raw_ref, f32[3,8,256]{2,1,0:T(8,128)S(1)} %bitcast.16, f32[3,8,256]{2,1,0:T(8,128)S(1)} %wall_0.1.layer_ref), custom_call_target="tpu_custom_call" | custom-call | flops 2097152000 | bytes 2097152 | tf_op jit(solution)/shard_map/wall_1/pallas_call | solution.py:273
  101.8 0.1 collective-permute-done.17.refs_1_
  101.9 0.7 move.1
  (37 shorter events, 0.3 us)
Async XLA Ops:
  1.4 18.8 %collective-permute-start.1 = (f32[10,8,256]{2,1,0:T(8,128)S(1)}, f32[10,8,256]{2,1,0:T(8,128)S(1)}, u32[]{:S(2)}, u32[]{:S(2)}) collective-permute-start(f32[10,8,256]{2,1,0:T(8,128)S(1)} %pad_maximum_fusion.own_ref), channel_id=1, source_target_pairs={{1,0},{2,1},{3,2},{4,3},{5,4},{6,5},{7,6},{8,7},{9,8},{10,9},{11,1... | collective-permute-start | bytes 245768 | tf_op jit(solution)/shard_map/ppermute | solution.py:417
  9.7 11.2 %collective-permute-start = (f32[10,8,256]{2,1,0:T(8,128)S(1)}, f32[10,8,256]{2,1,0:T(8,128)S(1)}, u32[]{:S(2)}, u32[]{:S(2)}) collective-permute-start(f32[10,8,256]{2,1,0:T(8,128)S(1)} %pad_maximum_fusion.own_ref), channel_id=1, source_target_pairs={{0,1},{1,2},{2,3},{3,4},{4,5},{5,6},{6,7},{7,8},{8,9},{9,10},{10,1... | collective-permute-start | bytes 245768 | tf_op jit(solution)/shard_map/ppermute | solution.py:417
  10.8 32.9 %copy-start = (f32[4,4,3,1024]{3,1,2,0:T(4,128)S(1)}, f32[4,4,3,1024]{3,1,2,0:T(4,128)}, u32[]{:S(2)}) copy-start(f32[4,4,3,1024]{3,1,2,0:T(4,128)} %param.12) | copy-start | bytes 589828
  10.8 32.9 %copy-start.2 = (f32[1024]{0:T(1024)S(1)}, f32[1024]{0:T(1024)}, u32[]{:S(2)}) copy-start(f32[1024]{0:T(1024)} %param.16) | copy-start | bytes 12292
  10.8 11.6 %collective-permute-start.9 = (f32[4,3,3,1024]{3,2,1,0:T(4,128)S(1)}, f32[4,3,3,1024]{3,2,1,0:T(4,128)S(1)}, u32[]{:S(2)}, u32[]{:S(2)}) collective-permute-start(f32[4,3,3,1024]{3,2,1,0:T(4,128)S(1)} %get-tuple-element.22), channel_id=1, source_target_pairs={{0,127},{1,120},{2,121},{3,122},{4,123},{5,124},{6,125},{7,126},{8... | collective-permute-start | bytes 442376 | tf_op jit(solution)/shard_map/ppermute | solution.py:427
  18.0 12.2 %collective-permute-start.8 = (f32[4,3,3,1024]{3,2,1,0:T(4,128)S(1)}, f32[4,3,3,1024]{3,2,1,0:T(4,128)S(1)}, u32[]{:S(2)}, u32[]{:S(2)}) collective-permute-start(f32[4,3,3,1024]{3,2,1,0:T(4,128)S(1)} %get-tuple-element.22), channel_id=1, source_target_pairs={{0,7},{1,0},{2,1},{3,2},{4,3},{5,4},{6,5},{7,6},{8,15},{9,8},{10,9... | collective-permute-start | bytes 442376 | tf_op jit(solution)/shard_map/ppermute | solution.py:427
  18.0 14.1 %collective-permute-start.7 = (f32[4,3,3,1024]{3,2,1,0:T(4,128)S(1)}, f32[4,3,3,1024]{3,2,1,0:T(4,128)S(1)}, u32[]{:S(2)}, u32[]{:S(2)}) collective-permute-start(f32[4,3,3,1024]{3,2,1,0:T(4,128)S(1)} %get-tuple-element.22), channel_id=1, source_target_pairs={{0,15},{1,8},{2,9},{3,10},{4,11},{5,12},{6,13},{7,14},{8,23},{9,16... | collective-permute-start | bytes 442376 | tf_op jit(solution)/shard_map/ppermute | solution.py:427
  20.3 23.4 %collective-permute-start.3 = (f32[4,3,4,1024]{3,2,1,0:T(4,128)}, f32[4,3,4,1024]{3,2,1,0:T(4,128)S(1)}, u32[]{:S(2)}, u32[]{:S(2)}) collective-permute-start(f32[4,3,4,1024]{3,2,1,0:T(4,128)} %bitcast.10), channel_id=1, source_target_pairs={{0,120},{1,121},{2,122},{3,123},{4,124},{5,125},{6,126},{7,127},{8... | collective-permute-start | bytes 589832 | tf_op jit(solution)/shard_map/ppermute | solution.py:427
  20.9 22.8 %collective-permute-start.2 = (f32[4,3,4,1024]{3,2,1,0:T(4,128)}, f32[4,3,4,1024]{3,2,1,0:T(4,128)S(1)}, u32[]{:S(2)}, u32[]{:S(2)}) collective-permute-start(f32[4,3,4,1024]{3,2,1,0:T(4,128)} %bitcast.11), channel_id=1, source_target_pairs={{0,8},{1,9},{2,10},{3,11},{4,12},{5,13},{6,14},{7,15},{8,16},{9,17... | collective-permute-start | bytes 589832 | tf_op jit(solution)/shard_map/ppermute | solution.py:427
  22.4 15.2 %collective-permute-start.6 = (f32[4,3,3,1024]{3,2,1,0:T(4,128)S(1)}, f32[4,3,3,1024]{3,2,1,0:T(4,128)S(1)}, u32[]{:S(2)}, u32[]{:S(2)}) collective-permute-start(f32[4,3,3,1024]{3,2,1,0:T(4,128)S(1)} %get-tuple-element.23), channel_id=1, source_target_pairs={{0,121},{1,122},{2,123},{3,124},{4,125},{5,126},{6,127},{7,120},{8... | collective-permute-start | bytes 442376 | tf_op jit(solution)/shard_map/ppermute | solution.py:427
  30.2 7.4 %collective-permute-start.5 = (f32[4,3,3,1024]{3,2,1,0:T(4,128)S(1)}, f32[4,3,3,1024]{3,2,1,0:T(4,128)S(1)}, u32[]{:S(2)}, u32[]{:S(2)}) collective-permute-start(f32[4,3,3,1024]{3,2,1,0:T(4,128)S(1)} %get-tuple-element.23), channel_id=1, source_target_pairs={{0,1},{1,2},{2,3},{3,4},{4,5},{5,6},{6,7},{7,0},{8,9},{9,10},{10,1... | collective-permute-start | bytes 442376 | tf_op jit(solution)/shard_map/ppermute | solution.py:427
  32.2 11.5 %collective-permute-start.4 = (f32[4,3,3,1024]{3,2,1,0:T(4,128)S(1)}, f32[4,3,3,1024]{3,2,1,0:T(4,128)S(1)}, u32[]{:S(2)}, u32[]{:S(2)}) collective-permute-start(f32[4,3,3,1024]{3,2,1,0:T(4,128)S(1)} %get-tuple-element.23), channel_id=1, source_target_pairs={{0,9},{1,10},{2,11},{3,12},{4,13},{5,14},{6,15},{7,8},{8,17},{9,18... | collective-permute-start | bytes 442376 | tf_op jit(solution)/shard_map/ppermute | solution.py:427
  81.0 1.2 %collective-permute-start.10 = (f32[8,128]{1,0:T(8,128)S(1)}, f32[8,128]{1,0:T(8,128)S(1)}, u32[]{:S(2)}, u32[]{:S(2)}) collective-permute-start(f32[8,128]{1,0:T(8,128)S(1)} %get-tuple-element.15), channel_id=1, source_target_pairs={{0,1},{1,0},{2,3},{3,2},{4,5},{5,4},{6,7},{7,6},{8,9},{9,8},{10,11... | collective-permute-start | bytes 12296 | tf_op jit(solution)/shard_map/ppermute | solution.py:450
  82.3 7.0 %collective-permute-start.13 = (f32[8,128]{1,0:T(8,128)S(1)}, f32[8,128]{1,0:T(8,128)S(1)}, u32[]{:S(2)}, u32[]{:S(2)}) collective-permute-start(f32[8,128]{1,0:T(8,128)S(1)} %max.21), channel_id=1, source_target_pairs={{0,6},{1,7},{2,0},{3,1},{4,2},{5,3},{6,4},{7,5},{8,14},{9,15},{10,... | collective-permute-start | bytes 12296 | tf_op jit(solution)/shard_map/ppermute | solution.py:450
  82.3 7.0 %collective-permute-start.12 = (f32[8,128]{1,0:T(8,128)S(1)}, f32[8,128]{1,0:T(8,128)S(1)}, u32[]{:S(2)}, u32[]{:S(2)}) collective-permute-start(f32[8,128]{1,0:T(8,128)S(1)} %max.21), channel_id=1, source_target_pairs={{0,4},{1,5},{2,6},{3,7},{4,0},{5,1},{6,2},{7,3},{8,12},{9,13},{10,... | collective-permute-start | bytes 12296 | tf_op jit(solution)/shard_map/ppermute | solution.py:450
  82.3 7.0 %collective-permute-start.11 = (f32[8,128]{1,0:T(8,128)S(1)}, f32[8,128]{1,0:T(8,128)S(1)}, u32[]{:S(2)}, u32[]{:S(2)}) collective-permute-start(f32[8,128]{1,0:T(8,128)S(1)} %max.21), channel_id=1, source_target_pairs={{0,2},{1,3},{2,4},{3,5},{4,6},{5,7},{6,0},{7,1},{8,10},{9,11},{10,... | collective-permute-start | bytes 12296 | tf_op jit(solution)/shard_map/ppermute | solution.py:450
  84.3 7.1 %copy-start.1 = (f32[8,3,256]{2,0,1:T(8,128)S(1)}, f32[8,3,256]{2,0,1:T(8,128)}, u32[]{:S(2)}) copy-start(f32[8,3,256]{2,0,1:T(8,128)} %param.18) | copy-start | bytes 73732
  89.3 5.6 %collective-permute-start.16 = (f32[8,128]{1,0:T(8,128)S(1)}, f32[8,128]{1,0:T(8,128)S(1)}, u32[]{:S(2)}, u32[]{:S(2)}) collective-permute-start(f32[8,128]{1,0:T(8,128)S(1)} %maximum_maximum_fusion.1), channel_id=1, source_target_pairs={{0,24},{8,0},{16,8},{24,16},{32,56},{40,32},{48,40},{56,48},{64,88... | collective-permute-start | bytes 12296 | tf_op jit(solution)/shard_map/ppermute | solution.py:450
  89.4 5.6 %collective-permute-start.15 = (f32[8,128]{1,0:T(8,128)S(1)}, f32[8,128]{1,0:T(8,128)S(1)}, u32[]{:S(2)}, u32[]{:S(2)}) collective-permute-start(f32[8,128]{1,0:T(8,128)S(1)} %maximum_maximum_fusion.1), channel_id=1, source_target_pairs={{0,16},{8,24},{16,0},{24,8},{32,48},{40,56},{48,32},{56,40},{64,80... | collective-permute-start | bytes 12296 | tf_op jit(solution)/shard_map/ppermute | solution.py:450
  89.5 6.2 %collective-permute-start.14 = (f32[8,128]{1,0:T(8,128)S(1)}, f32[8,128]{1,0:T(8,128)S(1)}, u32[]{:S(2)}, u32[]{:S(2)}) collective-permute-start(f32[8,128]{1,0:T(8,128)S(1)} %maximum_maximum_fusion.1), channel_id=1, source_target_pairs={{0,8},{8,16},{16,24},{24,0},{32,40},{40,48},{48,56},{56,32},{64,72... | collective-permute-start | bytes 12296 | tf_op jit(solution)/shard_map/ppermute | solution.py:450
  95.7 6.2 %collective-permute-start.19 = (f32[8,128]{1,0:T(8,128)S(1)}, f32[8,128]{1,0:T(8,128)S(1)}, u32[]{:S(2)}, u32[]{:S(2)}) collective-permute-start(f32[8,128]{1,0:T(8,128)S(1)} %maximum_maximum_fusion.refs_0_), channel_id=1, source_target_pairs={{0,96},{8,104},{16,112},{24,120},{32,0},{40,8},{48,16},{56,24},{64... | collective-permute-start | bytes 12296 | tf_op jit(solution)/shard_map/ppermute | solution.py:450
  95.7 6.1 %collective-permute-start.18 = (f32[8,128]{1,0:T(8,128)S(1)}, f32[8,128]{1,0:T(8,128)S(1)}, u32[]{:S(2)}, u32[]{:S(2)}) collective-permute-start(f32[8,128]{1,0:T(8,128)S(1)} %maximum_maximum_fusion.refs_0_), channel_id=1, source_target_pairs={{0,64},{8,72},{16,80},{24,88},{32,96},{40,104},{48,112},{56,120},{... | collective-permute-start | bytes 12296 | tf_op jit(solution)/shard_map/ppermute | solution.py:450
  95.7 6.2 %collective-permute-start.17 = (f32[8,128]{1,0:T(8,128)S(1)}, f32[8,128]{1,0:T(8,128)S(1)}, u32[]{:S(2)}, u32[]{:S(2)}) collective-permute-start(f32[8,128]{1,0:T(8,128)S(1)} %maximum_maximum_fusion.refs_0_), channel_id=1, source_target_pairs={{0,32},{8,40},{16,48},{24,56},{32,64},{40,72},{48,80},{56,88},{64,... | collective-permute-start | bytes 12296 | tf_op jit(solution)/shard_map/ppermute | solution.py:450

commit v5 on v3

--- a/solution.py
+++ b/solution.py
@@ -398,6 +398,7 @@
         in_specs=[in_vmem] * (len(tops) + 2),
         out_specs=in_vmem,
         out_shape=jax.ShapeDtypeStruct(pos.shape, F32),
+        compiler_params=pltpu.CompilerParams(vmem_limit_bytes=8 * 2**20),
         name="move",
     )(*tops, pos, velocity)
 
@@ -460,6 +461,7 @@
     packed = jnp.concatenate(walls + [wall_weight[None]], axis=0)
 
     below, above = neighbours(pos, pos, "cx")
+    below, above, packed = lax.optimization_barrier((below, above, packed))
     wall_below, wall_above = neighbours(packed, packed, AXES)
     strips = [v[:, :, c : c + HALO] for c in (0, cols - HALO) for v in (below[rows - HALO :], pos, above[:HALO])]
     left, right = neighbours(

time: 96.6 us -> 95.2 us (0.986)
  the two profiles are of different devices: /device:TPU:76 before, /device:TPU:0 now
where the time goes in v5:
time: 95.2 us; the launch traced here: 93.5 us
  Pallas kernels  54.8 us (58%)
  waiting for transfers between devices  17.2 us (18%)
  starting transfers between devices  16.1 us (17%)
  local copies, waits for them, and re-layouts  2.59 us (3%)
  other arithmetic  1.89 us (2%)
    pallas_call x1, Pallas kernels, near_part(): pl.pallas_call(near_kernel, in_specs=[in_smem] * 2 + [in_vmem] * 6 + [in_...  37.3 us
    ppermute x6, waiting for transfers between devices, neighbours(): return (lax.ppermute(high, axis, up), lax.ppermute(low, axis, down))  15.2 us
    ppermute x6, starting transfers between devices, neighbours(): return (lax.ppermute(high, axis, up), lax.ppermute(low, axis, down))  9.87 us
    pallas_call x2, Pallas kernels, layer_part(): pl.pallas_call(kernel, in_specs=[pl.BlockSpec(memory_space=pltpu.SMEM)] +...  9.07 us
    pallas_call x2, Pallas kernels, wall_part(): pl.pallas_call(functools.partial(wall_kernel, stage, per), in_specs=[in_v...  7.67 us
    ppermute x10, starting transfers between devices, over_all(): lax.ppermute(value, axis, pairs)  6.22 us
    ppermute x10, waiting for transfers between devices, over_all(): lax.ppermute(value, axis, pairs)  1.97 us
  transfers between devices with their start and end apart: 16, of which 7 were waited for; matrix products, arithmetic and copies ran while one was open for 4% of the time, Pallas kernels for 18%

profile of v5, /device:TPU:0, one launch (start us, length us, event | category | flops | bytes accessed | tf_op | source)
XLA Modules:
  0.0 93.5 jit_solution(10107941290698854216)
XLA Ops:
  0.6 6.4 %collective-permute-start.1 = (f32[4,3,4,1024]{3,2,1,0:T(4,128)}, f32[4,3,4,1024]{3,2,1,0:T(4,128)S(1)}, u32[]{:S(2)}, u32[]{:S(2)}) collective-permute-start(f32[4,3,4,1024]{3,2,1,0:T(4,128)} %bitcast.9), channel_id=1, source_target_pairs={{8,0},{16,8},{24,16},{32,24},{40,32},{48,40},{56,48},{64,56},{72,6... | collective-permute-start | bytes 589832 | tf_op jit(solution)/shard_map/ppermute | solution.py:410
  7.0 1.1 %fusion.12 = (f32[4,3,3,1024]{3,2,1,0:T(4,128)S(1)}, f32[4,3,3,1024]{3,2,1,0:T(4,128)S(1)}) fusion(f32[4,3,4,1024]{3,2,1,0:T(4,128)} %bitcast.11), kind=kLoop, calls=%fused_computation.44 | loop fusion | bytes 589824 | tf_op jit(solution)/shard_map/slice | solution.py:466
  8.2 0.8 copy.19
  8.9 0.8 pad_maximum_fusion.2.own_ref
  9.7 0.7 fusion
  10.5 1.0 %collective-permute-done.1.above_ref = f32[4,3,4,1024]{3,2,1,0:T(4,128)S(1)} collective-permute-done((f32[4,3,4,1024]{3,2,1,0:T(4,128)}, f32[4,3,4,1024]{3,2,1,0:T(4,128)S(1)}, u32[]{:S(2)}, u32[]{:S(2)}) %collective-permute-start.1) | collective-permute-done | bytes 196640 | tf_op jit(solution)/shard_map/ppermute | solution.py:410
  11.5 5.4 %collective-permute-done.below_ref = f32[4,3,4,1024]{3,2,1,0:T(4,128)S(1)} collective-permute-done((f32[4,3,4,1024]{3,2,1,0:T(4,128)}, f32[4,3,4,1024]{3,2,1,0:T(4,128)S(1)}, u32[]{:S(2)}, u32[]{:S(2)}) %collective-permute-start) | collective-permute-done | bytes 196640 | tf_op jit(solution)/shard_map/ppermute | solution.py:410
  16.9 0.2 fusion.11
  17.1 0.1 pad_maximum_fusion
  17.2 0.1 pad_maximum_fusion.1
  17.4 3.0 %collective-permute-start.5 = (f32[10,3,3,1024]{3,2,1,0:T(4,128)S(1)}, f32[10,3,3,1024]{3,2,1,0:T(4,128)S(1)}, u32[]{:S(2)}, u32[]{:S(2)}) collective-permute-start(f32[10,3,3,1024]{3,2,1,0:T(4,128)S(1)} %pad_maximum_fusion.1), channel_id=1, source_target_pairs={{1,0},{2,1},{3,2},{4,3},{5,4},{6,5},{7,6},{0,7},{9,8},{10,9},{11,1... | collective-permute-start | bytes 1105928 | tf_op jit(solution)/shard_map/ppermute | solution.py:410
  20.5 0.1 copy.18
  20.6 0.1 reshape.21.near_ref
  20.9 0.5 collective-permute-start.2
  21.5 1.5 %collective-permute-done.3.after_ref = f32[10,8,256]{2,1,0:T(8,128)S(1)} collective-permute-done((f32[10,8,256]{2,1,0:T(8,128)S(1)}, f32[10,8,256]{2,1,0:T(8,128)S(1)}, u32[]{:S(2)}, u32[]{:S(2)}) %collective-permute-start.3) | collective-permute-done | bytes 81952 | tf_op jit(solution)/shard_map/ppermute | solution.py:410
  23.0 7.3 %collective-permute-done.2.before_ref = f32[10,8,256]{2,1,0:T(8,128)S(1)} collective-permute-done((f32[10,8,256]{2,1,0:T(8,128)S(1)}, f32[10,8,256]{2,1,0:T(8,128)S(1)}, u32[]{:S(2)}, u32[]{:S(2)}) %collective-permute-start.2) | collective-permute-done | bytes 81952 | tf_op jit(solution)/shard_map/ppermute | solution.py:410
  30.3 4.1 %layer_first.1 = (f32[3,8,256]{2,1,0:T(8,128)S(1)}, bf16[24,192,256]{2,1,0:T(8,128)(2,1)S(1)}, bf16[24,32,256]{2,1,0:T(8,128)(2,1)S(1)}) custom-call(s32[8,2]{1,0:T(8,128)S(1)} %bitcast.17, f32[10,8,256]{2,1,0:T(8,128)S(1)} %pad_maximum_fusion.2.own_ref, f32[10,8,256]{2,1,0:T(8,128)S(1)} %collective-permute-done.2.before_ref, ...), custom_call_target="tpu_custom_call" | custom-call | flops 1048576000 | bytes 1048576 | tf_op jit(solution)/shard_map/layer_first/pallas_call | solution.py:370
  34.5 37.3 %near.1 = (f32[4,3,4,1024]{3,2,1,0:T(4,128)S(1)}, f32[8,128]{1,0:T(8,128)S(1)}, f32[8,384,128]{2,1,0:T(8,128)S(1)}) custom-call(s32[32]{0:T(128)S(1)} %reshape.21.near_ref, s32[16]{0:T(128)S(1)} %reshape.22.wall_ref, f32[4,3,4,1024]{3,2,1,0:T(4,128)S(1)} %collective-permute-done.below_ref, f32[4,3,4,1024]{3,2,1,0:T(4,128)S(1)} %bitcast.12, ...), custom_call_target="tpu_custom_call" | custom-call | flops 33554432000 | bytes 8388608 | tf_op jit(solution)/shard_map/near/pallas_call | solution.py:217
  71.8 0.1 collective-permute-start.6
  71.9 1.2 %collective-permute-done.6 = f32[8,128]{1,0:T(8,128)S(1)} collective-permute-done((f32[8,128]{1,0:T(8,128)S(1)}, f32[8,128]{1,0:T(8,128)S(1)}, u32[]{:S(2)}, u32[]{:S(2)}) %collective-permute-start.6) | collective-permute-done | bytes 4128 | tf_op jit(solution)/shard_map/ppermute | solution.py:433
  73.0 1.2 %collective-permute-start.8 = (f32[8,128]{1,0:T(8,128)S(1)}, f32[8,128]{1,0:T(8,128)S(1)}, u32[]{:S(2)}, u32[]{:S(2)}) collective-permute-start(f32[8,128]{1,0:T(8,128)S(1)} %max.21), channel_id=1, source_target_pairs={{0,4},{1,5},{2,6},{3,7},{4,0},{5,1},{6,2},{7,3},{8,12},{9,13},{10,... | collective-permute-start | bytes 12296 | tf_op jit(solution)/shard_map/ppermute | solution.py:433
  74.3 0.8 collective-permute-start.7
  75.1 4.9 %layer_second.1.layer_ref = f32[3,8,256]{2,1,0:T(8,128)S(1)} custom-call(s32[8,3]{1,0:T(8,128)S(1)} %slice.39.listed_ref, f32[10,8,256]{2,1,0:T(8,128)S(1)} %pad_maximum_fusion.2.own_ref, bf16[24,192,256]{2,1,0:T(8,128)(2,1)S(1)} %get-tuple-element.25.left_ref, bf16[24,32,256]{2,1,0:T(8,128)(2,1)S(1)} %get-tuple-element.26.feature_ref, ...), custom_call_target="tpu_custom_call" | custom-call | flops 1572864000 | bytes 1048576 | tf_op jit(solution)/shard_map/layer_second/pallas_call | solution.py:370
  80.2 0.3 collective-permute-start.11
  80.5 1.7 %collective-permute-start.10 = (f32[8,128]{1,0:T(8,128)S(1)}, f32[8,128]{1,0:T(8,128)S(1)}, u32[]{:S(2)}, u32[]{:S(2)}) collective-permute-start(f32[8,128]{1,0:T(8,128)S(1)} %maximum_maximum_fusion.1), channel_id=1, source_target_pairs={{0,8},{8,16},{16,24},{24,0},{32,40},{40,48},{48,56},{56,32},{64,72... | collective-permute-start | bytes 12296 | tf_op jit(solution)/shard_map/ppermute | solution.py:433
  82.2 3.5 %wall_0.1.layer_ref = f32[3,8,256]{2,1,0:T(8,128)S(1)} custom-call(f32[8,384,128]{2,1,0:T(8,128)S(1)} %get-tuple-element.23.raw_ref, f32[3,8,256]{2,1,0:T(8,128)S(1)} %bitcast.15, f32[3,8,256]{2,1,0:T(8,128)S(1)} %layer_second.1.layer_ref), custom_call_target="tpu_custom_call" | custom-call | flops 2097152000 | bytes 2097152 | tf_op jit(solution)/shard_map/wall_0/pallas_call | solution.py:266
  85.7 0.7 collective-permute-done.10
  86.4 0.1 collective-permute-start.14
  86.5 1.9 %collective-permute-start.13 = (f32[8,128]{1,0:T(8,128)S(1)}, f32[8,128]{1,0:T(8,128)S(1)}, u32[]{:S(2)}, u32[]{:S(2)}) collective-permute-start(f32[8,128]{1,0:T(8,128)S(1)} %maximum_maximum_fusion.refs_0_), channel_id=1, source_target_pairs={{0,32},{8,40},{16,48},{24,56},{32,64},{40,72},{48,80},{56,88},{64,... | collective-permute-start | bytes 12296 | tf_op jit(solution)/shard_map/ppermute | solution.py:433
  88.5 4.1 %wall_1.1 = f32[3,8,256]{2,1,0:T(8,128)} custom-call(f32[8,384,128]{2,1,0:T(8,128)S(1)} %get-tuple-element.23.raw_ref, f32[3,8,256]{2,1,0:T(8,128)S(1)} %bitcast.16, f32[3,8,256]{2,1,0:T(8,128)S(1)} %wall_0.1.layer_ref), custom_call_target="tpu_custom_call" | custom-call | flops 2097152000 | bytes 2097152 | tf_op jit(solution)/shard_map/wall_1/pallas_call | solution.py:266
  92.6 0.1 collective-permute-done.13.refs_1_
  92.7 0.7 move.1
  (36 shorter events, 0.6 us)
Async XLA Ops:
  0.6 19.7 %copy-start.4 = (s32[8,2]{0,1:T(2,128)S(1)}, s32[8,2]{0,1:T(2,128)}, u32[]{:S(2)}) copy-start(s32[8,2]{0,1:T(2,128)} %param.23) | copy-start | bytes 196
  0.6 10.9 %collective-permute-start.1 = (f32[4,3,4,1024]{3,2,1,0:T(4,128)}, f32[4,3,4,1024]{3,2,1,0:T(4,128)S(1)}, u32[]{:S(2)}, u32[]{:S(2)}) collective-permute-start(f32[4,3,4,1024]{3,2,1,0:T(4,128)} %bitcast.9), channel_id=1, source_target_pairs={{8,0},{16,8},{24,16},{32,24},{40,32},{48,40},{56,48},{64,56},{72,6... | collective-permute-start | bytes 589832 | tf_op jit(solution)/shard_map/ppermute | solution.py:410
  7.0 9.9 %collective-permute-start = (f32[4,3,4,1024]{3,2,1,0:T(4,128)}, f32[4,3,4,1024]{3,2,1,0:T(4,128)S(1)}, u32[]{:S(2)}, u32[]{:S(2)}) collective-permute-start(f32[4,3,4,1024]{3,2,1,0:T(4,128)} %bitcast.10), channel_id=1, source_target_pairs={{0,8},{8,16},{16,24},{24,32},{32,40},{40,48},{48,56},{56,64},{64,7... | collective-permute-start | bytes 589832 | tf_op jit(solution)/shard_map/ppermute | solution.py:410
  7.0 13.8 %copy-start.3 = (f32[4,4]{1,0:T(4,128)S(1)}, f32[4,4]{1,0:T(4,128)}, u32[]{:S(2)}) copy-start(f32[4,4]{1,0:T(4,128)} %param.13) | copy-start | bytes 196
  17.2 17.2 %collective-permute-start.4 = (f32[10,3,3,1024]{3,2,1,0:T(4,128)S(1)}, f32[10,3,3,1024]{3,2,1,0:T(4,128)S(1)}, u32[]{:S(2)}, u32[]{:S(2)}) collective-permute-start(f32[10,3,3,1024]{3,2,1,0:T(4,128)S(1)} %pad_maximum_fusion), channel_id=1, source_target_pairs={{0,1},{1,2},{2,3},{3,4},{4,5},{5,6},{6,7},{7,0},{8,9},{9,10},{10,1... | collective-permute-start | bytes 1105928 | tf_op jit(solution)/shard_map/ppermute | solution.py:410
  17.4 17.1 %copy-start = (f32[4,4,3,1024]{3,1,2,0:T(4,128)S(1)}, f32[4,4,3,1024]{3,1,2,0:T(4,128)}, u32[]{:S(2)}) copy-start(f32[4,4,3,1024]{3,1,2,0:T(4,128)} %param.12) | copy-start | bytes 589828
  17.4 17.1 %copy-start.2 = (f32[1024]{0:T(1024)S(1)}, f32[1024]{0:T(1024)}, u32[]{:S(2)}) copy-start(f32[1024]{0:T(1024)} %param.16) | copy-start | bytes 12292
  17.4 17.0 %collective-permute-start.5 = (f32[10,3,3,1024]{3,2,1,0:T(4,128)S(1)}, f32[10,3,3,1024]{3,2,1,0:T(4,128)S(1)}, u32[]{:S(2)}, u32[]{:S(2)}) collective-permute-start(f32[10,3,3,1024]{3,2,1,0:T(4,128)S(1)} %pad_maximum_fusion.1), channel_id=1, source_target_pairs={{1,0},{2,1},{3,2},{4,3},{5,4},{6,5},{7,6},{0,7},{9,8},{10,9},{11,1... | collective-permute-start | bytes 1105928 | tf_op jit(solution)/shard_map/ppermute | solution.py:410
  20.9 2.1 %collective-permute-start.3 = (f32[10,8,256]{2,1,0:T(8,128)S(1)}, f32[10,8,256]{2,1,0:T(8,128)S(1)}, u32[]{:S(2)}, u32[]{:S(2)}) collective-permute-start(f32[10,8,256]{2,1,0:T(8,128)S(1)} %pad_maximum_fusion.2.own_ref), channel_id=1, source_target_pairs={{1,0},{2,1},{3,2},{4,3},{5,4},{6,5},{7,6},{8,7},{9,8},{10,9},{11,1... | collective-permute-start | bytes 245768 | tf_op jit(solution)/shard_map/ppermute | solution.py:410
  20.9 9.4 %collective-permute-start.2 = (f32[10,8,256]{2,1,0:T(8,128)S(1)}, f32[10,8,256]{2,1,0:T(8,128)S(1)}, u32[]{:S(2)}, u32[]{:S(2)}) collective-permute-start(f32[10,8,256]{2,1,0:T(8,128)S(1)} %pad_maximum_fusion.2.own_ref), channel_id=1, source_target_pairs={{0,1},{1,2},{2,3},{3,4},{4,5},{5,6},{6,7},{7,8},{8,9},{9,10},{10,1... | collective-permute-start | bytes 245768 | tf_op jit(solution)/shard_map/ppermute | solution.py:410
  71.8 1.2 %collective-permute-start.6 = (f32[8,128]{1,0:T(8,128)S(1)}, f32[8,128]{1,0:T(8,128)S(1)}, u32[]{:S(2)}, u32[]{:S(2)}) collective-permute-start(f32[8,128]{1,0:T(8,128)S(1)} %get-tuple-element.21), channel_id=1, source_target_pairs={{0,1},{1,0},{2,3},{3,2},{4,5},{5,4},{6,7},{7,6},{8,9},{9,8},{10,11... | collective-permute-start | bytes 12296 | tf_op jit(solution)/shard_map/ppermute | solution.py:433
  73.0 7.0 %collective-permute-start.9 = (f32[8,128]{1,0:T(8,128)S(1)}, f32[8,128]{1,0:T(8,128)S(1)}, u32[]{:S(2)}, u32[]{:S(2)}) collective-permute-start(f32[8,128]{1,0:T(8,128)S(1)} %max.21), channel_id=1, source_target_pairs={{0,6},{1,7},{2,0},{3,1},{4,2},{5,3},{6,4},{7,5},{8,14},{9,15},{10,... | collective-permute-start | bytes 12296 | tf_op jit(solution)/shard_map/ppermute | solution.py:433
  73.0 7.0 %collective-permute-start.8 = (f32[8,128]{1,0:T(8,128)S(1)}, f32[8,128]{1,0:T(8,128)S(1)}, u32[]{:S(2)}, u32[]{:S(2)}) collective-permute-start(f32[8,128]{1,0:T(8,128)S(1)} %max.21), channel_id=1, source_target_pairs={{0,4},{1,5},{2,6},{3,7},{4,0},{5,1},{6,2},{7,3},{8,12},{9,13},{10,... | collective-permute-start | bytes 12296 | tf_op jit(solution)/shard_map/ppermute | solution.py:433
  74.3 5.8 %collective-permute-start.7 = (f32[8,128]{1,0:T(8,128)S(1)}, f32[8,128]{1,0:T(8,128)S(1)}, u32[]{:S(2)}, u32[]{:S(2)}) collective-permute-start(f32[8,128]{1,0:T(8,128)S(1)} %max.21), channel_id=1, source_target_pairs={{0,2},{1,3},{2,4},{3,5},{4,6},{5,7},{6,0},{7,1},{8,10},{9,11},{10,... | collective-permute-start | bytes 12296 | tf_op jit(solution)/shard_map/ppermute | solution.py:433
  75.1 7.1 %copy-start.1 = (f32[8,3,256]{2,0,1:T(8,128)S(1)}, f32[8,3,256]{2,0,1:T(8,128)}, u32[]{:S(2)}) copy-start(f32[8,3,256]{2,0,1:T(8,128)} %param.18) | copy-start | bytes 73732
  80.1 5.6 %collective-permute-start.12 = (f32[8,128]{1,0:T(8,128)S(1)}, f32[8,128]{1,0:T(8,128)S(1)}, u32[]{:S(2)}, u32[]{:S(2)}) collective-permute-start(f32[8,128]{1,0:T(8,128)S(1)} %maximum_maximum_fusion.1), channel_id=1, source_target_pairs={{0,24},{8,0},{16,8},{24,16},{32,56},{40,32},{48,40},{56,48},{64,88... | collective-permute-start | bytes 12296 | tf_op jit(solution)/shard_map/ppermute | solution.py:433
  80.2 5.6 %collective-permute-start.11 = (f32[8,128]{1,0:T(8,128)S(1)}, f32[8,128]{1,0:T(8,128)S(1)}, u32[]{:S(2)}, u32[]{:S(2)}) collective-permute-start(f32[8,128]{1,0:T(8,128)S(1)} %maximum_maximum_fusion.1), channel_id=1, source_target_pairs={{0,16},{8,24},{16,0},{24,8},{32,48},{40,56},{48,32},{56,40},{64,80... | collective-permute-start | bytes 12296 | tf_op jit(solution)/shard_map/ppermute | solution.py:433
  80.5 6.0 %collective-permute-start.10 = (f32[8,128]{1,0:T(8,128)S(1)}, f32[8,128]{1,0:T(8,128)S(1)}, u32[]{:S(2)}, u32[]{:S(2)}) collective-permute-start(f32[8,128]{1,0:T(8,128)S(1)} %maximum_maximum_fusion.1), channel_id=1, source_target_pairs={{0,8},{8,16},{16,24},{24,0},{32,40},{40,48},{48,56},{56,32},{64,72... | collective-permute-start | bytes 12296 | tf_op jit(solution)/shard_map/ppermute | solution.py:433
  86.4 6.2 %collective-permute-start.15 = (f32[8,128]{1,0:T(8,128)S(1)}, f32[8,128]{1,0:T(8,128)S(1)}, u32[]{:S(2)}, u32[]{:S(2)}) collective-permute-start(f32[8,128]{1,0:T(8,128)S(1)} %maximum_maximum_fusion.refs_0_), channel_id=1, source_target_pairs={{0,96},{8,104},{16,112},{24,120},{32,0},{40,8},{48,16},{56,24},{64... | collective-permute-start | bytes 12296 | tf_op jit(solution)/shard_map/ppermute | solution.py:433
  86.4 6.2 %collective-permute-start.14 = (f32[8,128]{1,0:T(8,128)S(1)}, f32[8,128]{1,0:T(8,128)S(1)}, u32[]{:S(2)}, u32[]{:S(2)}) collective-permute-start(f32[8,128]{1,0:T(8,128)S(1)} %maximum_maximum_fusion.refs_0_), channel_id=1, source_target_pairs={{0,64},{8,72},{16,80},{24,88},{32,96},{40,104},{48,112},{56,120},{... | collective-permute-start | bytes 12296 | tf_op jit(solution)/shard_map/ppermute | solution.py:433
  86.5 6.2 %collective-permute-start.13 = (f32[8,128]{1,0:T(8,128)S(1)}, f32[8,128]{1,0:T(8,128)S(1)}, u32[]{:S(2)}, u32[]{:S(2)}) collective-permute-start(f32[8,128]{1,0:T(8,128)S(1)} %maximum_maximum_fusion.refs_0_), channel_id=1, source_target_pairs={{0,32},{8,40},{16,48},{24,56},{32,64},{40,72},{48,80},{56,88},{64,... | collective-permute-start | bytes 12296 | tf_op jit(solution)/shard_map/ppermute | solution.py:433

commit v6 on v5

--- a/solution.py
+++ b/solution.py
@@ -461,12 +461,14 @@
     packed = jnp.concatenate(walls + [wall_weight[None]], axis=0)
 
     below, above = neighbours(pos, pos, "cx")
-    below, above, packed = lax.optimization_barrier((below, above, packed))
+    own_strips = pos[:, :, :HALO], pos[:, :, cols - HALO :]
+    packed, own_strips = lax.optimization_barrier((packed, own_strips))
     wall_below, wall_above = neighbours(packed, packed, AXES)
-    strips = [v[:, :, c : c + HALO] for c in (0, cols - HALO) for v in (below[rows - HALO :], pos, above[:HALO])]
-    left, right = neighbours(
-        jnp.concatenate(strips[:3], axis=0), jnp.concatenate(strips[3:], axis=0), "cy"
+    low, high = (
+        jnp.concatenate([below[rows - HALO :, :, c : c + HALO], own, above[:HALO, :, c : c + HALO]])
+        for c, own in zip((0, cols - HALO), own_strips)
     )
+    left, right = neighbours(low, high, "cy")
 
     patches = wall_pos.shape[0]
     all_patches = patches * lax.axis_size(AXES)

time: 95.2 us -> 94.3 us (level)
  the two profiles are of different devices: /device:TPU:0 before, /device:TPU:50 now
where the time goes in v6:
time: 94.3 us; the launch traced here: 94 us
  Pallas kernels  54.8 us (58%)
  starting transfers between devices  28.1 us (30%)
  waiting for transfers between devices  5.9 us (6%)
  local copies, waits for them, and re-layouts  2.52 us (3%)
  other arithmetic  1.9 us (2%)
    pallas_call x1, Pallas kernels, near_part(): pl.pallas_call(near_kernel, in_specs=[in_smem] * 2 + [in_vmem] * 6 + [in_...  37.3 us
    ppermute x10, starting transfers between devices, over_all(): lax.ppermute(value, axis, pairs)  24.9 us
    pallas_call x2, Pallas kernels, layer_part(): pl.pallas_call(kernel, in_specs=[pl.BlockSpec(memory_space=pltpu.SMEM)] +...  9.07 us
    pallas_call x2, Pallas kernels, wall_part(): pl.pallas_call(functools.partial(wall_kernel, stage, per), in_specs=[in_v...  7.67 us
    ppermute x6, waiting for transfers between devices, neighbours(): return (lax.ppermute(high, axis, up), lax.ppermute(low, axis, down))  4.72 us
    ppermute x6, starting transfers between devices, neighbours(): return (lax.ppermute(high, axis, up), lax.ppermute(low, axis, down))  3.15 us
  transfers between devices with their start and end apart: 16, of which 4 were waited for; matrix products, arithmetic and copies ran while one was open for 5% of the time, Pallas kernels for 18%

profile of v6, /device:TPU:50, one launch (start us, length us, event | category | flops | bytes accessed | tf_op | source)
XLA Modules:
  0.0 94.0 jit_solution(5938966151976555601)
XLA Ops:
  0.6 0.6 collective-permute-start.3
  1.3 1.5 %collective-permute-start.2 = (f32[4,3,4,1024]{3,2,1,0:T(4,128)}, f32[4,3,4,1024]{3,2,1,0:T(4,128)S(1)}, u32[]{:S(2)}, u32[]{:S(2)}) collective-permute-start(f32[4,3,4,1024]{3,2,1,0:T(4,128)} %bitcast.10), channel_id=1, source_target_pairs={{0,8},{8,16},{16,24},{24,32},{32,40},{40,48},{48,56},{56,64},{64,7... | collective-permute-start | bytes 589832 | tf_op jit(solution)/shard_map/ppermute | solution.py:410
  2.7 1.1 %fusion.13 = (f32[4,3,3,1024]{3,2,1,0:T(4,128)S(1)}, f32[4,3,3,1024]{3,2,1,0:T(4,128)S(1)}) fusion(f32[4,3,4,1024]{3,2,1,0:T(4,128)} %bitcast.11), kind=kLoop, calls=%fused_computation.45 | loop fusion | bytes 589824 | tf_op jit(solution)/shard_map/slice | solution.py:464
  3.9 0.8 pad_maximum_fusion.2.own_ref
  4.7 0.5 collective-permute-start
  5.2 0.8 copy.19
  6.0 0.7 fusion
  6.7 1.7 %collective-permute-done.2.below_ref = f32[4,3,4,1024]{3,2,1,0:T(4,128)S(1)} collective-permute-done((f32[4,3,4,1024]{3,2,1,0:T(4,128)}, f32[4,3,4,1024]{3,2,1,0:T(4,128)S(1)}, u32[]{:S(2)}, u32[]{:S(2)}) %collective-permute-start.2) | collective-permute-done | bytes 196640 | tf_op jit(solution)/shard_map/ppermute | solution.py:410
  8.6 0.1 pad_maximum_fusion.1
  8.7 0.1 pad_maximum_fusion
  8.9 0.5 collective-permute-start.4
  9.6 0.1 copy.18
  9.7 0.1 reshape.21.near_ref
  10.0 4.1 %layer_first.1 = (f32[3,8,256]{2,1,0:T(8,128)S(1)}, bf16[24,192,256]{2,1,0:T(8,128)(2,1)S(1)}, bf16[24,32,256]{2,1,0:T(8,128)(2,1)S(1)}) custom-call(s32[8,2]{1,0:T(8,128)S(1)} %bitcast.17, f32[10,8,256]{2,1,0:T(8,128)S(1)} %pad_maximum_fusion.2.own_ref, f32[10,8,256]{2,1,0:T(8,128)S(1)} %collective-permute-done.before_ref, ...), custom_call_target="tpu_custom_call" | custom-call | flops 1048576000 | bytes 1048576 | tf_op jit(solution)/shard_map/layer_first/pallas_call | solution.py:370
  14.2 0.9 collective-permute-done.5.right_ref
  15.1 2.1 %collective-permute-done.4.left_ref = f32[10,3,3,1024]{3,2,1,0:T(4,128)S(1)} collective-permute-done((f32[10,3,3,1024]{3,2,1,0:T(4,128)S(1)}, f32[10,3,3,1024]{3,2,1,0:T(4,128)S(1)}, u32[]{:S(2)}, u32[]{:S(2)}) %collective-permute-start.4) | collective-permute-done | bytes 368672 | tf_op jit(solution)/shard_map/ppermute | solution.py:410
  17.2 37.3 %near.1 = (f32[4,3,4,1024]{3,2,1,0:T(4,128)S(1)}, f32[8,128]{1,0:T(8,128)S(1)}, f32[8,384,128]{2,1,0:T(8,128)S(1)}) custom-call(s32[32]{0:T(128)S(1)} %reshape.21.near_ref, s32[16]{0:T(128)S(1)} %reshape.22.wall_ref, f32[4,3,4,1024]{3,2,1,0:T(4,128)S(1)} %collective-permute-done.2.below_ref, f32[4,3,4,1024]{3,2,1,0:T(4,128)S(1)} %bitcast.12, ...), custom_call_target="tpu_custom_call" | custom-call | flops 33554432000 | bytes 8388608 | tf_op jit(solution)/shard_map/near/pallas_call | solution.py:217
  54.5 0.1 collective-permute-start.6
  54.6 1.2 %collective-permute-done.6 = f32[8,128]{1,0:T(8,128)S(1)} collective-permute-done((f32[8,128]{1,0:T(8,128)S(1)}, f32[8,128]{1,0:T(8,128)S(1)}, u32[]{:S(2)}, u32[]{:S(2)}) %collective-permute-start.6) | collective-permute-done | bytes 4128 | tf_op jit(solution)/shard_map/ppermute | solution.py:433
  55.7 0.4 collective-permute-start.9
  56.2 4.6 %collective-permute-start.8 = (f32[8,128]{1,0:T(8,128)S(1)}, f32[8,128]{1,0:T(8,128)S(1)}, u32[]{:S(2)}, u32[]{:S(2)}) collective-permute-start(f32[8,128]{1,0:T(8,128)S(1)} %max.21), channel_id=1, source_target_pairs={{0,4},{1,5},{2,6},{3,7},{4,0},{5,1},{6,2},{7,3},{8,12},{9,13},{10,... | collective-permute-start | bytes 12296 | tf_op jit(solution)/shard_map/ppermute | solution.py:433
  60.8 2.6 %collective-permute-start.7 = (f32[8,128]{1,0:T(8,128)S(1)}, f32[8,128]{1,0:T(8,128)S(1)}, u32[]{:S(2)}, u32[]{:S(2)}) collective-permute-start(f32[8,128]{1,0:T(8,128)S(1)} %max.21), channel_id=1, source_target_pairs={{0,2},{1,3},{2,4},{3,5},{4,6},{5,7},{6,0},{7,1},{8,10},{9,11},{10,... | collective-permute-start | bytes 12296 | tf_op jit(solution)/shard_map/ppermute | solution.py:433
  63.4 4.9 %layer_second.1.layer_ref = f32[3,8,256]{2,1,0:T(8,128)S(1)} custom-call(s32[8,3]{1,0:T(8,128)S(1)} %slice.31.listed_ref, f32[10,8,256]{2,1,0:T(8,128)S(1)} %pad_maximum_fusion.2.own_ref, bf16[24,192,256]{2,1,0:T(8,128)(2,1)S(1)} %get-tuple-element.25.left_ref, bf16[24,32,256]{2,1,0:T(8,128)(2,1)S(1)} %get-tuple-element.26.feature_ref, ...), custom_call_target="tpu_custom_call" | custom-call | flops 1572864000 | bytes 1048576 | tf_op jit(solution)/shard_map/layer_second/pallas_call | solution.py:370
  68.4 2.5 %collective-permute-start.12 = (f32[8,128]{1,0:T(8,128)S(1)}, f32[8,128]{1,0:T(8,128)S(1)}, u32[]{:S(2)}, u32[]{:S(2)}) collective-permute-start(f32[8,128]{1,0:T(8,128)S(1)} %maximum_maximum_fusion.1), channel_id=1, source_target_pairs={{0,24},{8,0},{16,8},{24,16},{32,56},{40,32},{48,40},{56,48},{64,88... | collective-permute-start | bytes 12296 | tf_op jit(solution)/shard_map/ppermute | solution.py:433
  70.9 4.0 %collective-permute-start.11 = (f32[8,128]{1,0:T(8,128)S(1)}, f32[8,128]{1,0:T(8,128)S(1)}, u32[]{:S(2)}, u32[]{:S(2)}) collective-permute-start(f32[8,128]{1,0:T(8,128)S(1)} %maximum_maximum_fusion.1), channel_id=1, source_target_pairs={{0,16},{8,24},{16,0},{24,8},{32,48},{40,56},{48,32},{56,40},{64,80... | collective-permute-start | bytes 12296 | tf_op jit(solution)/shard_map/ppermute | solution.py:433
  74.9 2.5 %collective-permute-start.10 = (f32[8,128]{1,0:T(8,128)S(1)}, f32[8,128]{1,0:T(8,128)S(1)}, u32[]{:S(2)}, u32[]{:S(2)}) collective-permute-start(f32[8,128]{1,0:T(8,128)S(1)} %maximum_maximum_fusion.1), channel_id=1, source_target_pairs={{0,8},{8,16},{16,24},{24,0},{32,40},{40,48},{48,56},{56,32},{64,72... | collective-permute-start | bytes 12296 | tf_op jit(solution)/shard_map/ppermute | solution.py:433
  77.5 3.5 %wall_0.1.layer_ref = f32[3,8,256]{2,1,0:T(8,128)S(1)} custom-call(f32[8,384,128]{2,1,0:T(8,128)S(1)} %get-tuple-element.23.raw_ref, f32[3,8,256]{2,1,0:T(8,128)S(1)} %bitcast.15, f32[3,8,256]{2,1,0:T(8,128)S(1)} %layer_second.1.layer_ref), custom_call_target="tpu_custom_call" | custom-call | flops 2097152000 | bytes 2097152 | tf_op jit(solution)/shard_map/wall_0/pallas_call | solution.py:266
  81.0 0.6 collective-permute-start.15
  81.6 5.0 %collective-permute-start.14 = (f32[8,128]{1,0:T(8,128)S(1)}, f32[8,128]{1,0:T(8,128)S(1)}, u32[]{:S(2)}, u32[]{:S(2)}) collective-permute-start(f32[8,128]{1,0:T(8,128)S(1)} %maximum_maximum_fusion.refs_0_), channel_id=1, source_target_pairs={{0,64},{8,72},{16,80},{24,88},{32,96},{40,104},{48,112},{56,120},{... | collective-permute-start | bytes 12296 | tf_op jit(solution)/shard_map/ppermute | solution.py:433
  86.6 2.5 %collective-permute-start.13 = (f32[8,128]{1,0:T(8,128)S(1)}, f32[8,128]{1,0:T(8,128)S(1)}, u32[]{:S(2)}, u32[]{:S(2)}) collective-permute-start(f32[8,128]{1,0:T(8,128)S(1)} %maximum_maximum_fusion.refs_0_), channel_id=1, source_target_pairs={{0,32},{8,40},{16,48},{24,56},{32,64},{40,72},{48,80},{56,88},{64,... | collective-permute-start | bytes 12296 | tf_op jit(solution)/shard_map/ppermute | solution.py:433
  89.1 4.1 %wall_1.1 = f32[3,8,256]{2,1,0:T(8,128)} custom-call(f32[8,384,128]{2,1,0:T(8,128)S(1)} %get-tuple-element.23.raw_ref, f32[3,8,256]{2,1,0:T(8,128)S(1)} %bitcast.16, f32[3,8,256]{2,1,0:T(8,128)S(1)} %wall_0.1.layer_ref), custom_call_target="tpu_custom_call" | custom-call | flops 2097152000 | bytes 2097152 | tf_op jit(solution)/shard_map/wall_1/pallas_call | solution.py:266
  93.3 0.7 move.1
  (37 shorter events, 0.7 us)
Async XLA Ops:
  0.6 8.8 %copy-start.4 = (s32[8,2]{0,1:T(2,128)S(1)}, s32[8,2]{0,1:T(2,128)}, u32[]{:S(2)}) copy-start(s32[8,2]{0,1:T(2,128)} %param.23) | copy-start | bytes 196
  0.6 9.2 %copy-start.3 = (f32[4,4]{1,0:T(4,128)S(1)}, f32[4,4]{1,0:T(4,128)}, u32[]{:S(2)}) copy-start(f32[4,4]{1,0:T(4,128)} %param.13) | copy-start | bytes 196
  0.6 7.8 %collective-permute-start.3 = (f32[4,3,4,1024]{3,2,1,0:T(4,128)}, f32[4,3,4,1024]{3,2,1,0:T(4,128)S(1)}, u32[]{:S(2)}, u32[]{:S(2)}) collective-permute-start(f32[4,3,4,1024]{3,2,1,0:T(4,128)} %bitcast.9), channel_id=1, source_target_pairs={{8,0},{16,8},{24,16},{32,24},{40,32},{48,40},{56,48},{64,56},{72,6... | collective-permute-start | bytes 589832 | tf_op jit(solution)/shard_map/ppermute | solution.py:410
  1.3 7.2 %collective-permute-start.2 = (f32[4,3,4,1024]{3,2,1,0:T(4,128)}, f32[4,3,4,1024]{3,2,1,0:T(4,128)S(1)}, u32[]{:S(2)}, u32[]{:S(2)}) collective-permute-start(f32[4,3,4,1024]{3,2,1,0:T(4,128)} %bitcast.10), channel_id=1, source_target_pairs={{0,8},{8,16},{16,24},{24,32},{32,40},{40,48},{48,56},{56,64},{64,7... | collective-permute-start | bytes 589832 | tf_op jit(solution)/shard_map/ppermute | solution.py:410
  4.7 5.4 %collective-permute-start.1 = (f32[10,8,256]{2,1,0:T(8,128)S(1)}, f32[10,8,256]{2,1,0:T(8,128)S(1)}, u32[]{:S(2)}, u32[]{:S(2)}) collective-permute-start(f32[10,8,256]{2,1,0:T(8,128)S(1)} %pad_maximum_fusion.2.own_ref), channel_id=1, source_target_pairs={{1,0},{2,1},{3,2},{4,3},{5,4},{6,5},{7,6},{8,7},{9,8},{10,9},{11,1... | collective-permute-start | bytes 245768 | tf_op jit(solution)/shard_map/ppermute | solution.py:410
  4.7 5.3 %collective-permute-start = (f32[10,8,256]{2,1,0:T(8,128)S(1)}, f32[10,8,256]{2,1,0:T(8,128)S(1)}, u32[]{:S(2)}, u32[]{:S(2)}) collective-permute-start(f32[10,8,256]{2,1,0:T(8,128)S(1)} %pad_maximum_fusion.2.own_ref), channel_id=1, source_target_pairs={{0,1},{1,2},{2,3},{3,4},{4,5},{5,6},{6,7},{7,8},{8,9},{9,10},{10,1... | collective-permute-start | bytes 245768 | tf_op jit(solution)/shard_map/ppermute | solution.py:410
  8.7 6.4 %collective-permute-start.5 = (f32[10,3,3,1024]{3,2,1,0:T(4,128)S(1)}, f32[10,3,3,1024]{3,2,1,0:T(4,128)S(1)}, u32[]{:S(2)}, u32[]{:S(2)}) collective-permute-start(f32[10,3,3,1024]{3,2,1,0:T(4,128)S(1)} %pad_maximum_fusion.1), channel_id=1, source_target_pairs={{1,0},{2,1},{3,2},{4,3},{5,4},{6,5},{7,6},{0,7},{9,8},{10,9},{11,1... | collective-permute-start | bytes 1105928 | tf_op jit(solution)/shard_map/ppermute | solution.py:410
  8.9 8.3 %copy-start = (f32[4,4,3,1024]{3,1,2,0:T(4,128)S(1)}, f32[4,4,3,1024]{3,1,2,0:T(4,128)}, u32[]{:S(2)}) copy-start(f32[4,4,3,1024]{3,1,2,0:T(4,128)} %param.12) | copy-start | bytes 589828
  8.9 8.3 %copy-start.2 = (f32[1024]{0:T(1024)S(1)}, f32[1024]{0:T(1024)}, u32[]{:S(2)}) copy-start(f32[1024]{0:T(1024)} %param.16) | copy-start | bytes 12292
  8.9 8.3 %collective-permute-start.4 = (f32[10,3,3,1024]{3,2,1,0:T(4,128)S(1)}, f32[10,3,3,1024]{3,2,1,0:T(4,128)S(1)}, u32[]{:S(2)}, u32[]{:S(2)}) collective-permute-start(f32[10,3,3,1024]{3,2,1,0:T(4,128)S(1)} %pad_maximum_fusion), channel_id=1, source_target_pairs={{0,1},{1,2},{2,3},{3,4},{4,5},{5,6},{6,7},{7,0},{8,9},{9,10},{10,1... | collective-permute-start | bytes 1105928 | tf_op jit(solution)/shard_map/ppermute | solution.py:410
  54.5 1.2 %collective-permute-start.6 = (f32[8,128]{1,0:T(8,128)S(1)}, f32[8,128]{1,0:T(8,128)S(1)}, u32[]{:S(2)}, u32[]{:S(2)}) collective-permute-start(f32[8,128]{1,0:T(8,128)S(1)} %get-tuple-element.21), channel_id=1, source_target_pairs={{0,1},{1,0},{2,3},{3,2},{4,5},{5,4},{6,7},{7,6},{8,9},{9,8},{10,11... | collective-permute-start | bytes 12296 | tf_op jit(solution)/shard_map/ppermute | solution.py:433
  55.7 12.6 %collective-permute-start.9 = (f32[8,128]{1,0:T(8,128)S(1)}, f32[8,128]{1,0:T(8,128)S(1)}, u32[]{:S(2)}, u32[]{:S(2)}) collective-permute-start(f32[8,128]{1,0:T(8,128)S(1)} %max.21), channel_id=1, source_target_pairs={{0,6},{1,7},{2,0},{3,1},{4,2},{5,3},{6,4},{7,5},{8,14},{9,15},{10,... | collective-permute-start | bytes 12296 | tf_op jit(solution)/shard_map/ppermute | solution.py:433
  56.2 12.2 %collective-permute-start.8 = (f32[8,128]{1,0:T(8,128)S(1)}, f32[8,128]{1,0:T(8,128)S(1)}, u32[]{:S(2)}, u32[]{:S(2)}) collective-permute-start(f32[8,128]{1,0:T(8,128)S(1)} %max.21), channel_id=1, source_target_pairs={{0,4},{1,5},{2,6},{3,7},{4,0},{5,1},{6,2},{7,3},{8,12},{9,13},{10,... | collective-permute-start | bytes 12296 | tf_op jit(solution)/shard_map/ppermute | solution.py:433
  60.8 7.6 %collective-permute-start.7 = (f32[8,128]{1,0:T(8,128)S(1)}, f32[8,128]{1,0:T(8,128)S(1)}, u32[]{:S(2)}, u32[]{:S(2)}) collective-permute-start(f32[8,128]{1,0:T(8,128)S(1)} %max.21), channel_id=1, source_target_pairs={{0,2},{1,3},{2,4},{3,5},{4,6},{5,7},{6,0},{7,1},{8,10},{9,11},{10,... | collective-permute-start | bytes 12296 | tf_op jit(solution)/shard_map/ppermute | solution.py:433
  63.4 14.0 %copy-start.1 = (f32[8,3,256]{2,0,1:T(8,128)S(1)}, f32[8,3,256]{2,0,1:T(8,128)}, u32[]{:S(2)}) copy-start(f32[8,3,256]{2,0,1:T(8,128)} %param.18) | copy-start | bytes 73732
  68.4 12.6 %collective-permute-start.12 = (f32[8,128]{1,0:T(8,128)S(1)}, f32[8,128]{1,0:T(8,128)S(1)}, u32[]{:S(2)}, u32[]{:S(2)}) collective-permute-start(f32[8,128]{1,0:T(8,128)S(1)} %maximum_maximum_fusion.1), channel_id=1, source_target_pairs={{0,24},{8,0},{16,8},{24,16},{32,56},{40,32},{48,40},{56,48},{64,88... | collective-permute-start | bytes 12296 | tf_op jit(solution)/shard_map/ppermute | solution.py:433
  70.9 10.1 %collective-permute-start.11 = (f32[8,128]{1,0:T(8,128)S(1)}, f32[8,128]{1,0:T(8,128)S(1)}, u32[]{:S(2)}, u32[]{:S(2)}) collective-permute-start(f32[8,128]{1,0:T(8,128)S(1)} %maximum_maximum_fusion.1), channel_id=1, source_target_pairs={{0,16},{8,24},{16,0},{24,8},{32,48},{40,56},{48,32},{56,40},{64,80... | collective-permute-start | bytes 12296 | tf_op jit(solution)/shard_map/ppermute | solution.py:433
  74.9 6.1 %collective-permute-start.10 = (f32[8,128]{1,0:T(8,128)S(1)}, f32[8,128]{1,0:T(8,128)S(1)}, u32[]{:S(2)}, u32[]{:S(2)}) collective-permute-start(f32[8,128]{1,0:T(8,128)S(1)} %maximum_maximum_fusion.1), channel_id=1, source_target_pairs={{0,8},{8,16},{16,24},{24,0},{32,40},{40,48},{48,56},{56,32},{64,72... | collective-permute-start | bytes 12296 | tf_op jit(solution)/shard_map/ppermute | solution.py:433
  81.0 12.2 %collective-permute-start.15 = (f32[8,128]{1,0:T(8,128)S(1)}, f32[8,128]{1,0:T(8,128)S(1)}, u32[]{:S(2)}, u32[]{:S(2)}) collective-permute-start(f32[8,128]{1,0:T(8,128)S(1)} %maximum_maximum_fusion.refs_0_), channel_id=1, source_target_pairs={{0,96},{8,104},{16,112},{24,120},{32,0},{40,8},{48,16},{56,24},{64... | collective-permute-start | bytes 12296 | tf_op jit(solution)/shard_map/ppermute | solution.py:433
  81.6 11.7 %collective-permute-start.14 = (f32[8,128]{1,0:T(8,128)S(1)}, f32[8,128]{1,0:T(8,128)S(1)}, u32[]{:S(2)}, u32[]{:S(2)}) collective-permute-start(f32[8,128]{1,0:T(8,128)S(1)} %maximum_maximum_fusion.refs_0_), channel_id=1, source_target_pairs={{0,64},{8,72},{16,80},{24,88},{32,96},{40,104},{48,112},{56,120},{... | collective-permute-start | bytes 12296 | tf_op jit(solution)/shard_map/ppermute | solution.py:433
  86.6 6.7 %collective-permute-start.13 = (f32[8,128]{1,0:T(8,128)S(1)}, f32[8,128]{1,0:T(8,128)S(1)}, u32[]{:S(2)}, u32[]{:S(2)}) collective-permute-start(f32[8,128]{1,0:T(8,128)S(1)} %maximum_maximum_fusion.refs_0_), channel_id=1, source_target_pairs={{0,32},{8,40},{16,48},{24,56},{32,64},{40,72},{48,80},{56,88},{64,... | collective-permute-start | bytes 12296 | tf_op jit(solution)/shard_map/ppermute | solution.py:433

commit v7 on v6

--- a/solution.py
+++ b/solution.py
@@ -9,7 +9,6 @@
 from jax.sharding import PartitionSpec as P
 
 HALO = 3
-FIRST = 2
 AXES = ("cx", "cy")
 SOFT = 0.25
 STOKES_SCALE = 1.0 / (8.0 * math.pi)
@@ -280,7 +279,7 @@
     )(raw, pos, layer)
 
 
-def layer_sums(listed_ref, own_ref, left_ref, feature_ref, target_ref, moment_ref):
+def layer_sums(sources, own_ref, left_ref, feature_ref, target_ref, moment_ref):
     patches = own_ref.shape[1]
     x = [own_ref[d] for d in range(3)]
     target_raw(target_ref, 0, x, TARGET_ROWS)
@@ -293,8 +292,7 @@
         raw = get_rows(target_ref, pl.multiple_of(p * TARGET_ROWS, 8), TARGET_ROWS)
         near, form = target_rows(raw[0:8]), target_rows(raw[8:24])
         total = None
-        for k in range(listed_ref.shape[1]):
-            s = listed_ref[p, k]
+        for s in sources(p):
             square = product(left_ref[s, 0:64], near)
             scalar = product(left_ref[s, 64:192], form)
             root = lax.rsqrt(jnp.maximum(square, SOFT))
@@ -311,9 +309,9 @@
     return [(-2.0 * LAYER_SCALE) * (x[d] * moments[3] - moments[d]) for d in range(3)]
 
 
-def layer_first(listed_ref, own_ref, before_ref, after_ref, out_ref, left_ref, feature_ref, raw_ref, target_ref, moment_ref):
-    patches = own_ref.shape[1]
-    for block, ref in enumerate((before_ref, own_ref, after_ref)):
+def layer_prepare(blocks, left_ref, feature_ref, raw_ref):
+    patches = blocks[0][0].shape[1]
+    for block, (ref, _) in enumerate(blocks):
         y = [ref[d] for d in range(3)]
         n = [ref[3 + d] for d in range(3)]
         v = [ref[6 + d] * ref[9] for d in range(3)]
@@ -330,46 +328,85 @@
         for k, row in enumerate(rows):
             put_rows(raw_ref, block * patches * LAYER_ROWS + k, patches, LAYER_ROWS, row)
 
-    def prepare(s, carry):
-        raw = get_rows(raw_ref, pl.multiple_of(s * LAYER_ROWS, 8), LAYER_ROWS)
-        left_ref[s, 0:64] = source_rows(raw[0:8])
-        left_ref[s, 64:192] = source_rows(raw[8:24])
-        split = [p.astype(F32) for p in parts(raw[24:32])]
-        split.append(jnp.zeros_like(split[0]))
-        feature_ref[s] = jnp.concatenate(split, axis=0).astype(BF16)
-        return carry
-
-    lax.fori_loop(0, 3 * patches, prepare, 0, unroll=4)
-    sums = layer_sums(listed_ref, own_ref, left_ref, feature_ref, target_ref, moment_ref)
+    for block, (_, first) in enumerate(blocks):
+
+        def prepare(i, carry, block=block, first=first):
+            base = (block * patches + i) * LAYER_ROWS
+            raw = get_rows(raw_ref, pl.multiple_of(base, 8), LAYER_ROWS)
+            left_ref[first + i, 0:64] = source_rows(raw[0:8])
+            left_ref[first + i, 64:192] = source_rows(raw[8:24])
+            split = [p.astype(F32) for p in parts(raw[24:32])]
+            split.append(jnp.zeros_like(split[0]))
+            feature_ref[first + i] = jnp.concatenate(split, axis=0).astype(BF16)
+            return carry
+
+        lax.fori_loop(0, patches, prepare, 0, unroll=4)
+
+
+def layer_first(own_ref, out_ref, left_ref, feature_ref, raw_ref, target_ref, moment_ref):
+    layer_prepare([(own_ref, 0)], left_ref, feature_ref, raw_ref)
+    sums = layer_sums(lambda p: [p], own_ref, left_ref, feature_ref, target_ref, moment_ref)
     for d in range(3):
         out_ref[d] = sums[d]
 
 
-def layer_second(listed_ref, own_ref, left_ref, feature_ref, so_far_ref, out_ref, target_ref, moment_ref):
-    sums = layer_sums(listed_ref, own_ref, left_ref, feature_ref, target_ref, moment_ref)
+def layer_second(
+    listed_ref,
+    own_ref,
+    before_ref,
+    after_ref,
+    own_left_ref,
+    own_feature_ref,
+    so_far_ref,
+    out_ref,
+    left_ref,
+    feature_ref,
+    raw_ref,
+    target_ref,
+    moment_ref,
+):
+    patches = own_ref.shape[1]
+    left_ref[patches : 2 * patches] = own_left_ref[...]
+    feature_ref[patches : 2 * patches] = own_feature_ref[...]
+    blocks = [(before_ref, 0), (after_ref, 2 * patches)]
+    layer_prepare(blocks, left_ref, feature_ref, raw_ref)
+    count = listed_ref.shape[1]
+    sums = layer_sums(
+        lambda p: [listed_ref[p, k] for k in range(count)],
+        own_ref,
+        left_ref,
+        feature_ref,
+        target_ref,
+        moment_ref,
+    )
     for d in range(3):
         out_ref[d] = so_far_ref[d] + sums[d]
 
 
-def layer_part(kernel, listed, *arrays):
+def layer_part(kernel, *arrays, listed=None):
     _, patches, points = arrays[0].shape
     tiles = points // LANES
     in_vmem = pl.BlockSpec(memory_space=pltpu.VMEM)
-    pairs = patches * points * listed.shape[1] * points
+    in_smem = pl.BlockSpec(memory_space=pltpu.SMEM)
     out_shape = [jax.ShapeDtypeStruct((3, patches, points), F32)]
+    blocks, sources = (2, listed.shape[1]) if listed is not None else (1, 1)
     scratch = [
+        pltpu.VMEM((tiles, blocks * patches * LAYER_ROWS, LANES), F32),
         pltpu.VMEM((tiles, patches * TARGET_ROWS, LANES), F32),
         pltpu.VMEM((tiles, patches * 8, LANES), F32),
     ]
-    if kernel is layer_first:
-        out_shape += [
-            jax.ShapeDtypeStruct((3 * patches, 192, points), BF16),
-            jax.ShapeDtypeStruct((3 * patches, 32, points), BF16),
-        ]
-        scratch.insert(0, pltpu.VMEM((tiles, 3 * patches * LAYER_ROWS, LANES), F32))
+    if listed is None:
+        sides = (patches, 192, points), (patches, 32, points)
+        out_shape += [jax.ShapeDtypeStruct(side, BF16) for side in sides]
+        scalars = ()
+    else:
+        sides = (3 * patches, 192, points), (3 * patches, 32, points)
+        scratch = [pltpu.VMEM(side, BF16) for side in sides] + scratch
+        scalars = (listed,)
+    pairs = patches * points * sources * points
     return pl.pallas_call(
         kernel,
-        in_specs=[pl.BlockSpec(memory_space=pltpu.SMEM)] + [in_vmem] * len(arrays),
+        in_specs=[in_smem] * len(scalars) + [in_vmem] * len(arrays),
         out_specs=[in_vmem] * len(out_shape),
         out_shape=out_shape,
         scratch_shapes=scratch,
@@ -378,7 +415,7 @@
             flops=1000 * pairs, bytes_accessed=2**20, transcendentals=pairs
         ),
         name=kernel.__name__,
-    )(listed, *arrays)
+    )(*scalars, *arrays)
 
 
 def move_kernel(*refs):
@@ -462,8 +499,8 @@
 
     below, above = neighbours(pos, pos, "cx")
     own_strips = pos[:, :, :HALO], pos[:, :, cols - HALO :]
-    packed, own_strips = lax.optimization_barrier((packed, own_strips))
-    wall_below, wall_above = neighbours(packed, packed, AXES)
+    below, above, later = lax.optimization_barrier((below, above, packed))
+    wall_below, wall_above = neighbours(later, later, AXES)
     low, high = (
         jnp.concatenate([below[rows - HALO :, :, c : c + HALO], own, above[:HALO, :, c : c + HALO]])
         for c, own in zip((0, cols - HALO), own_strips)
@@ -474,10 +511,7 @@
     all_patches = patches * lax.axis_size(AXES)
     start = lax.axis_index(AXES) * patches
     listed = (patch_near - start + patches) % all_patches
-    itself = patches + jnp.arange(patches, dtype=jnp.int32)[:, None]
-    listed = jnp.concatenate([itself, listed], axis=1)
-    early = listed[:, :FIRST]
-    layer, lefts, features = layer_part(layer_first, early, packed, wall_below, wall_above)
+    layer, lefts, features = layer_part(layer_first, later)
 
     def code(cell):
         row = (cell // all_cols - first_row + HALO) % all_rows
@@ -496,9 +530,11 @@
         cell_drag.reshape(-1, 1),
         (analysis, stiffness[None, :], synthesis),
     )
-    top, late = lax.optimization_barrier((top, listed[:, FIRST:]))
+    top, listed = lax.optimization_barrier((top, listed))
     tops = over_all(top)
-    [density_next] = layer_part(layer_second, late, packed, lefts, features, layer)
+    [density_next] = layer_part(
+        layer_second, packed, wall_below, wall_above, lefts, features, layer, listed=listed
+    )
     per = cell_to_patch.shape[1]
     for stage in range(per):
         density_next = wall_part(stage, per, wall_raw, walls[0], density_next)

time: 94.3 us -> 92.6 us (0.982)
  the two profiles are of different devices: /device:TPU:50 before, /device:TPU:0 now
where the time goes in v7:
time: 92.6 us; the launch traced here: 91.4 us
  Pallas kernels  54.8 us (59%)
  starting transfers between devices  27.5 us (30%)
  waiting for transfers between devices  4.67 us (5%)
  other arithmetic  1.82 us (2%)
  local copies, waits for them, and re-layouts  1.81 us (2%)
    pallas_call x1, Pallas kernels, near_part(): pl.pallas_call(near_kernel, in_specs=[in_smem] * 2 + [in_vmem] * 6 + [in_...  37.3 us
    ppermute x6, starting transfers between devices, neighbours(): return (lax.ppermute(high, axis, up), lax.ppermute(low, axis, down))  15.7 us
    ppermute x10, starting transfers between devices, over_all(): lax.ppermute(value, axis, pairs)  11.8 us
    pallas_call x2, Pallas kernels, layer_part(): pl.pallas_call(kernel, in_specs=[in_smem] * len(scalars) + [in_vmem] * le...  9.07 us
    pallas_call x2, Pallas kernels, wall_part(): pl.pallas_call(functools.partial(wall_kernel, stage, per), in_specs=[in_v...  7.67 us
    ppermute x6, waiting for transfers between devices, neighbours(): return (lax.ppermute(high, axis, up), lax.ppermute(low, axis, down))  2.73 us
    ppermute x10, waiting for transfers between devices, over_all(): lax.ppermute(value, axis, pairs)  1.93 us
  transfers between devices with their start and end apart: 16, of which 4 were waited for; matrix products, arithmetic and copies ran while one was open for 4% of the time, Pallas kernels for 59%

profile of v7, /device:TPU:0, one launch (start us, length us, event | category | flops | bytes accessed | tf_op | source)
XLA Modules:
  0.0 91.4 jit_solution(9282223779714545761)
XLA Ops:
  0.7 1.6 %collective-permute-start = (f32[4,3,4,1024]{3,2,1,0:T(4,128)}, f32[4,3,4,1024]{3,2,1,0:T(4,128)S(1)}, u32[]{:S(2)}, u32[]{:S(2)}) collective-permute-start(f32[4,3,4,1024]{3,2,1,0:T(4,128)} %bitcast.8), channel_id=1, source_target_pairs={{0,8},{8,16},{16,24},{24,32},{32,40},{40,48},{48,56},{56,64},{64,7... | collective-permute-start | bytes 589832 | tf_op jit(solution)/shard_map/ppermute | solution.py:447
  2.3 4.8 %collective-permute-start.1 = (f32[4,3,4,1024]{3,2,1,0:T(4,128)}, f32[4,3,4,1024]{3,2,1,0:T(4,128)S(1)}, u32[]{:S(2)}, u32[]{:S(2)}) collective-permute-start(f32[4,3,4,1024]{3,2,1,0:T(4,128)} %bitcast.9), channel_id=1, source_target_pairs={{8,0},{16,8},{24,16},{32,24},{40,32},{48,40},{56,48},{64,56},{72,6... | collective-permute-start | bytes 589832 | tf_op jit(solution)/shard_map/ppermute | solution.py:447
  7.1 1.1 %fusion.12 = (f32[4,3,3,1024]{3,2,1,0:T(4,128)S(1)}, f32[4,3,3,1024]{3,2,1,0:T(4,128)S(1)}) fusion(f32[4,3,4,1024]{3,2,1,0:T(4,128)} %bitcast.10), kind=kLoop, calls=%fused_computation.42 | loop fusion | bytes 589824 | tf_op jit(solution)/shard_map/slice | solution.py:501
  8.2 0.8 pad_maximum_fusion.2.own_ref
  9.0 0.7 fusion
  9.8 2.4 %collective-permute-done.below_ref = f32[4,3,4,1024]{3,2,1,0:T(4,128)S(1)} collective-permute-done((f32[4,3,4,1024]{3,2,1,0:T(4,128)}, f32[4,3,4,1024]{3,2,1,0:T(4,128)S(1)}, u32[]{:S(2)}, u32[]{:S(2)}) %collective-permute-start) | collective-permute-done | bytes 196640 | tf_op jit(solution)/shard_map/ppermute | solution.py:447
  12.2 0.2 fusion.11
  12.4 0.1 pad_maximum_fusion.1
  12.5 1.9 %collective-permute-start.3 = (f32[10,3,3,1024]{3,2,1,0:T(4,128)S(1)}, f32[10,3,3,1024]{3,2,1,0:T(4,128)S(1)}, u32[]{:S(2)}, u32[]{:S(2)}) collective-permute-start(f32[10,3,3,1024]{3,2,1,0:T(4,128)S(1)} %pad_maximum_fusion.1), channel_id=1, source_target_pairs={{1,0},{2,1},{3,2},{4,3},{5,4},{6,5},{7,6},{0,7},{9,8},{10,9},{11,1... | collective-permute-start | bytes 1105928 | tf_op jit(solution)/shard_map/ppermute | solution.py:447
  14.4 0.1 pad_maximum_fusion
  14.6 0.1 copy.18
  14.7 0.1 reshape.13.near_ref
  14.8 0.1 copy.19
  15.2 7.3 %collective-permute-start.15 = (f32[10,8,256]{2,1,0:T(8,128)S(1)}, f32[10,8,256]{2,1,0:T(8,128)S(1)}, u32[]{:S(2)}, u32[]{:S(2)}) collective-permute-start(f32[10,8,256]{2,1,0:T(8,128)S(1)} %pad_maximum_fusion.2.own_ref), channel_id=1, source_target_pairs={{1,0},{2,1},{3,2},{4,3},{5,4},{6,5},{7,6},{8,7},{9,8},{10,9},{11,1... | collective-permute-start | bytes 245768 | tf_op jit(solution)/shard_map/ppermute | solution.py:447
  22.4 2.1 %layer_first.1 = (f32[3,8,256]{2,1,0:T(8,128)S(1)}, bf16[8,192,256]{2,1,0:T(8,128)(2,1)S(1)}, bf16[8,32,256]{2,1,0:T(8,128)(2,1)S(1)}) custom-call(f32[10,8,256]{2,1,0:T(8,128)S(1)} %pad_maximum_fusion.2.own_ref), custom_call_target="tpu_custom_call" | custom-call | flops 524288000 | bytes 1048576 | tf_op jit(solution)/shard_map/layer_first/pallas_call | solution.py:407
  24.5 0.3 collective-permute-done.2.left_ref
  24.9 37.3 %near.1 = (f32[4,3,4,1024]{3,2,1,0:T(4,128)S(1)}, f32[8,128]{1,0:T(8,128)S(1)}, f32[8,384,128]{2,1,0:T(8,128)S(1)}) custom-call(s32[32]{0:T(128)S(1)} %reshape.13.near_ref, s32[16]{0:T(128)S(1)} %reshape.14.wall_ref, f32[4,3,4,1024]{3,2,1,0:T(4,128)S(1)} %collective-permute-done.below_ref, f32[4,3,4,1024]{3,2,1,0:T(4,128)S(1)} %bitcast.11, ...), custom_call_target="tpu_custom_call" | custom-call | flops 33554432000 | bytes 8388608 | tf_op jit(solution)/shard_map/near/pallas_call | solution.py:216
  62.2 0.1 collective-permute-start.4
  62.3 1.2 %collective-permute-done.4 = f32[8,128]{1,0:T(8,128)S(1)} collective-permute-done((f32[8,128]{1,0:T(8,128)S(1)}, f32[8,128]{1,0:T(8,128)S(1)}, u32[]{:S(2)}, u32[]{:S(2)}) %collective-permute-start.4) | collective-permute-done | bytes 4128 | tf_op jit(solution)/shard_map/ppermute | solution.py:470
  63.5 1.4 %collective-permute-start.6 = (f32[8,128]{1,0:T(8,128)S(1)}, f32[8,128]{1,0:T(8,128)S(1)}, u32[]{:S(2)}, u32[]{:S(2)}) collective-permute-start(f32[8,128]{1,0:T(8,128)S(1)} %max.21), channel_id=1, source_target_pairs={{0,4},{1,5},{2,6},{3,7},{4,0},{5,1},{6,2},{7,3},{8,12},{9,13},{10,... | collective-permute-start | bytes 12296 | tf_op jit(solution)/shard_map/ppermute | solution.py:470
  64.8 1.9 %collective-permute-start.7 = (f32[8,128]{1,0:T(8,128)S(1)}, f32[8,128]{1,0:T(8,128)S(1)}, u32[]{:S(2)}, u32[]{:S(2)}) collective-permute-start(f32[8,128]{1,0:T(8,128)S(1)} %max.21), channel_id=1, source_target_pairs={{0,6},{1,7},{2,0},{3,1},{4,2},{5,3},{6,4},{7,5},{8,14},{9,15},{10,... | collective-permute-start | bytes 12296 | tf_op jit(solution)/shard_map/ppermute | solution.py:470
  66.7 7.0 %layer_second.1.layer_ref = f32[3,8,256]{2,1,0:T(8,128)S(1)} custom-call(s32[8,4]{1,0:T(8,128)S(1)} %add_select_fusion.listed_ref, f32[10,8,256]{2,1,0:T(8,128)S(1)} %pad_maximum_fusion.2.own_ref, f32[10,8,256]{2,1,0:T(8,128)S(1)} %collective-permute-done.14.before_ref, f32[10,8,256]{2,1,0:T(8,128)S(1)} %collective-permute-done.15.after_ref, ...), custom_call_target="tpu_custom_call" | custom-call | flops 2097152000 | bytes 1048576 | tf_op jit(solution)/shard_map/layer_second/pallas_call | solution.py:407
  73.7 1.3 %collective-permute-start.10 = (f32[8,128]{1,0:T(8,128)S(1)}, f32[8,128]{1,0:T(8,128)S(1)}, u32[]{:S(2)}, u32[]{:S(2)}) collective-permute-start(f32[8,128]{1,0:T(8,128)S(1)} %maximum_maximum_fusion.1), channel_id=1, source_target_pairs={{0,24},{8,0},{16,8},{24,16},{32,56},{40,32},{48,40},{56,48},{64,88... | collective-permute-start | bytes 12296 | tf_op jit(solution)/shard_map/ppermute | solution.py:470
  75.1 0.7 collective-permute-start.8
  75.8 0.8 collective-permute-start.9
  76.6 3.5 %wall_0.1.layer_ref = f32[3,8,256]{2,1,0:T(8,128)S(1)} custom-call(f32[8,384,128]{2,1,0:T(8,128)S(1)} %get-tuple-element.23.raw_ref, f32[3,8,256]{2,1,0:T(8,128)S(1)} %bitcast.14, f32[3,8,256]{2,1,0:T(8,128)S(1)} %layer_second.1.layer_ref), custom_call_target="tpu_custom_call" | custom-call | flops 2097152000 | bytes 2097152 | tf_op jit(solution)/shard_map/wall_0/pallas_call | solution.py:265
  80.2 0.8 collective-permute-done.9
  81.0 1.3 %collective-permute-start.11 = (f32[8,128]{1,0:T(8,128)S(1)}, f32[8,128]{1,0:T(8,128)S(1)}, u32[]{:S(2)}, u32[]{:S(2)}) collective-permute-start(f32[8,128]{1,0:T(8,128)S(1)} %maximum_maximum_fusion.refs_0_), channel_id=1, source_target_pairs={{0,32},{8,40},{16,48},{24,56},{32,64},{40,72},{48,80},{56,88},{64,... | collective-permute-start | bytes 12296 | tf_op jit(solution)/shard_map/ppermute | solution.py:470
  82.2 3.6 %collective-permute-start.12 = (f32[8,128]{1,0:T(8,128)S(1)}, f32[8,128]{1,0:T(8,128)S(1)}, u32[]{:S(2)}, u32[]{:S(2)}) collective-permute-start(f32[8,128]{1,0:T(8,128)S(1)} %maximum_maximum_fusion.refs_0_), channel_id=1, source_target_pairs={{0,64},{8,72},{16,80},{24,88},{32,96},{40,104},{48,112},{56,120},{... | collective-permute-start | bytes 12296 | tf_op jit(solution)/shard_map/ppermute | solution.py:470
  85.9 0.7 collective-permute-start.13
  86.5 4.1 %wall_1.1 = f32[3,8,256]{2,1,0:T(8,128)} custom-call(f32[8,384,128]{2,1,0:T(8,128)S(1)} %get-tuple-element.23.raw_ref, f32[3,8,256]{2,1,0:T(8,128)S(1)} %bitcast.15, f32[3,8,256]{2,1,0:T(8,128)S(1)} %wall_0.1.layer_ref), custom_call_target="tpu_custom_call" | custom-call | flops 2097152000 | bytes 2097152 | tf_op jit(solution)/shard_map/wall_1/pallas_call | solution.py:265
  90.7 0.7 move.1
  (35 shorter events, 0.4 us)
Async XLA Ops:
  0.6 13.9 %copy-start.5 = (s32[8,2]{0,1:T(2,128)S(1)}, s32[8,2]{0,1:T(2,128)}, u32[]{:S(2)}) copy-start(s32[8,2]{0,1:T(2,128)} %param.23) | copy-start | bytes 196
  0.6 14.3 %copy-start.3 = (f32[4,4]{1,0:T(4,128)S(1)}, f32[4,4]{1,0:T(4,128)}, u32[]{:S(2)}) copy-start(f32[4,4]{1,0:T(4,128)} %param.13) | copy-start | bytes 196
  0.7 14.4 %copy-start.4 = (s32[8,4]{0,1:T(4,128)S(1)}, s32[8,4]{0,1:T(4,128)}, u32[]{:S(2)}) copy-start(s32[8,4]{0,1:T(4,128)} %param.22) | copy-start | bytes 388
  0.7 11.5 %collective-permute-start = (f32[4,3,4,1024]{3,2,1,0:T(4,128)}, f32[4,3,4,1024]{3,2,1,0:T(4,128)S(1)}, u32[]{:S(2)}, u32[]{:S(2)}) collective-permute-start(f32[4,3,4,1024]{3,2,1,0:T(4,128)} %bitcast.8), channel_id=1, source_target_pairs={{0,8},{8,16},{16,24},{24,32},{32,40},{40,48},{48,56},{56,64},{64,7... | collective-permute-start | bytes 589832 | tf_op jit(solution)/shard_map/ppermute | solution.py:447
  2.3 9.9 %collective-permute-start.1 = (f32[4,3,4,1024]{3,2,1,0:T(4,128)}, f32[4,3,4,1024]{3,2,1,0:T(4,128)S(1)}, u32[]{:S(2)}, u32[]{:S(2)}) collective-permute-start(f32[4,3,4,1024]{3,2,1,0:T(4,128)} %bitcast.9), channel_id=1, source_target_pairs={{8,0},{16,8},{24,16},{32,24},{40,32},{48,40},{56,48},{64,56},{72,6... | collective-permute-start | bytes 589832 | tf_op jit(solution)/shard_map/ppermute | solution.py:447
  12.3 12.6 %copy-start = (f32[4,4,3,1024]{3,1,2,0:T(4,128)S(1)}, f32[4,4,3,1024]{3,1,2,0:T(4,128)}, u32[]{:S(2)}) copy-start(f32[4,4,3,1024]{3,1,2,0:T(4,128)} %param.12) | copy-start | bytes 589828
  12.3 12.5 %copy-start.2 = (f32[1024]{0:T(1024)S(1)}, f32[1024]{0:T(1024)}, u32[]{:S(2)}) copy-start(f32[1024]{0:T(1024)} %param.16) | copy-start | bytes 12292
  12.5 12.1 %collective-permute-start.3 = (f32[10,3,3,1024]{3,2,1,0:T(4,128)S(1)}, f32[10,3,3,1024]{3,2,1,0:T(4,128)S(1)}, u32[]{:S(2)}, u32[]{:S(2)}) collective-permute-start(f32[10,3,3,1024]{3,2,1,0:T(4,128)S(1)} %pad_maximum_fusion.1), channel_id=1, source_target_pairs={{1,0},{2,1},{3,2},{4,3},{5,4},{6,5},{7,6},{0,7},{9,8},{10,9},{11,1... | collective-permute-start | bytes 1105928 | tf_op jit(solution)/shard_map/ppermute | solution.py:447
  14.5 10.4 %collective-permute-start.2 = (f32[10,3,3,1024]{3,2,1,0:T(4,128)S(1)}, f32[10,3,3,1024]{3,2,1,0:T(4,128)S(1)}, u32[]{:S(2)}, u32[]{:S(2)}) collective-permute-start(f32[10,3,3,1024]{3,2,1,0:T(4,128)S(1)} %pad_maximum_fusion), channel_id=1, source_target_pairs={{0,1},{1,2},{2,3},{3,4},{4,5},{5,6},{6,7},{7,0},{8,9},{9,10},{10,1... | collective-permute-start | bytes 1105928 | tf_op jit(solution)/shard_map/ppermute | solution.py:447
  15.1 51.6 %collective-permute-start.14 = (f32[10,8,256]{2,1,0:T(8,128)S(1)}, f32[10,8,256]{2,1,0:T(8,128)S(1)}, u32[]{:S(2)}, u32[]{:S(2)}) collective-permute-start(f32[10,8,256]{2,1,0:T(8,128)S(1)} %pad_maximum_fusion.2.own_ref), channel_id=1, source_target_pairs={{0,1},{1,2},{2,3},{3,4},{4,5},{5,6},{6,7},{7,8},{8,9},{9,10},{10,1... | collective-permute-start | bytes 245768 | tf_op jit(solution)/shard_map/ppermute | solution.py:447
  15.2 51.5 %collective-permute-start.15 = (f32[10,8,256]{2,1,0:T(8,128)S(1)}, f32[10,8,256]{2,1,0:T(8,128)S(1)}, u32[]{:S(2)}, u32[]{:S(2)}) collective-permute-start(f32[10,8,256]{2,1,0:T(8,128)S(1)} %pad_maximum_fusion.2.own_ref), channel_id=1, source_target_pairs={{1,0},{2,1},{3,2},{4,3},{5,4},{6,5},{7,6},{8,7},{9,8},{10,9},{11,1... | collective-permute-start | bytes 245768 | tf_op jit(solution)/shard_map/ppermute | solution.py:447
  62.2 1.2 %collective-permute-start.4 = (f32[8,128]{1,0:T(8,128)S(1)}, f32[8,128]{1,0:T(8,128)S(1)}, u32[]{:S(2)}, u32[]{:S(2)}) collective-permute-start(f32[8,128]{1,0:T(8,128)S(1)} %get-tuple-element.21), channel_id=1, source_target_pairs={{0,1},{1,0},{2,3},{3,2},{4,5},{5,4},{6,7},{7,6},{8,9},{9,8},{10,11... | collective-permute-start | bytes 12296 | tf_op jit(solution)/shard_map/ppermute | solution.py:470
  63.5 10.2 %collective-permute-start.5 = (f32[8,128]{1,0:T(8,128)S(1)}, f32[8,128]{1,0:T(8,128)S(1)}, u32[]{:S(2)}, u32[]{:S(2)}) collective-permute-start(f32[8,128]{1,0:T(8,128)S(1)} %max.21), channel_id=1, source_target_pairs={{0,2},{1,3},{2,4},{3,5},{4,6},{5,7},{6,0},{7,1},{8,10},{9,11},{10,... | collective-permute-start | bytes 12296 | tf_op jit(solution)/shard_map/ppermute | solution.py:470
  63.5 10.2 %collective-permute-start.6 = (f32[8,128]{1,0:T(8,128)S(1)}, f32[8,128]{1,0:T(8,128)S(1)}, u32[]{:S(2)}, u32[]{:S(2)}) collective-permute-start(f32[8,128]{1,0:T(8,128)S(1)} %max.21), channel_id=1, source_target_pairs={{0,4},{1,5},{2,6},{3,7},{4,0},{5,1},{6,2},{7,3},{8,12},{9,13},{10,... | collective-permute-start | bytes 12296 | tf_op jit(solution)/shard_map/ppermute | solution.py:470
  64.8 8.9 %collective-permute-start.7 = (f32[8,128]{1,0:T(8,128)S(1)}, f32[8,128]{1,0:T(8,128)S(1)}, u32[]{:S(2)}, u32[]{:S(2)}) collective-permute-start(f32[8,128]{1,0:T(8,128)S(1)} %max.21), channel_id=1, source_target_pairs={{0,6},{1,7},{2,0},{3,1},{4,2},{5,3},{6,4},{7,5},{8,14},{9,15},{10,... | collective-permute-start | bytes 12296 | tf_op jit(solution)/shard_map/ppermute | solution.py:470
  66.7 9.9 %copy-start.1 = (f32[8,3,256]{2,0,1:T(8,128)S(1)}, f32[8,3,256]{2,0,1:T(8,128)}, u32[]{:S(2)}) copy-start(f32[8,3,256]{2,0,1:T(8,128)} %param.18) | copy-start | bytes 73732
  73.7 6.4 %collective-permute-start.10 = (f32[8,128]{1,0:T(8,128)S(1)}, f32[8,128]{1,0:T(8,128)S(1)}, u32[]{:S(2)}, u32[]{:S(2)}) collective-permute-start(f32[8,128]{1,0:T(8,128)S(1)} %maximum_maximum_fusion.1), channel_id=1, source_target_pairs={{0,24},{8,0},{16,8},{24,16},{32,56},{40,32},{48,40},{56,48},{64,88... | collective-permute-start | bytes 12296 | tf_op jit(solution)/shard_map/ppermute | solution.py:470
  75.1 5.1 %collective-permute-start.8 = (f32[8,128]{1,0:T(8,128)S(1)}, f32[8,128]{1,0:T(8,128)S(1)}, u32[]{:S(2)}, u32[]{:S(2)}) collective-permute-start(f32[8,128]{1,0:T(8,128)S(1)} %maximum_maximum_fusion.1), channel_id=1, source_target_pairs={{0,8},{8,16},{16,24},{24,0},{32,40},{40,48},{48,56},{56,32},{64,72... | collective-permute-start | bytes 12296 | tf_op jit(solution)/shard_map/ppermute | solution.py:470
  75.8 5.1 %collective-permute-start.9 = (f32[8,128]{1,0:T(8,128)S(1)}, f32[8,128]{1,0:T(8,128)S(1)}, u32[]{:S(2)}, u32[]{:S(2)}) collective-permute-start(f32[8,128]{1,0:T(8,128)S(1)} %maximum_maximum_fusion.1), channel_id=1, source_target_pairs={{0,16},{8,24},{16,0},{24,8},{32,48},{40,56},{48,32},{56,40},{64,80... | collective-permute-start | bytes 12296 | tf_op jit(solution)/shard_map/ppermute | solution.py:470
  81.0 9.7 %collective-permute-start.11 = (f32[8,128]{1,0:T(8,128)S(1)}, f32[8,128]{1,0:T(8,128)S(1)}, u32[]{:S(2)}, u32[]{:S(2)}) collective-permute-start(f32[8,128]{1,0:T(8,128)S(1)} %maximum_maximum_fusion.refs_0_), channel_id=1, source_target_pairs={{0,32},{8,40},{16,48},{24,56},{32,64},{40,72},{48,80},{56,88},{64,... | collective-permute-start | bytes 12296 | tf_op jit(solution)/shard_map/ppermute | solution.py:470
  82.2 8.4 %collective-permute-start.12 = (f32[8,128]{1,0:T(8,128)S(1)}, f32[8,128]{1,0:T(8,128)S(1)}, u32[]{:S(2)}, u32[]{:S(2)}) collective-permute-start(f32[8,128]{1,0:T(8,128)S(1)} %maximum_maximum_fusion.refs_0_), channel_id=1, source_target_pairs={{0,64},{8,72},{16,80},{24,88},{32,96},{40,104},{48,112},{56,120},{... | collective-permute-start | bytes 12296 | tf_op jit(solution)/shard_map/ppermute | solution.py:470
  85.9 4.8 %collective-permute-start.13 = (f32[8,128]{1,0:T(8,128)S(1)}, f32[8,128]{1,0:T(8,128)S(1)}, u32[]{:S(2)}, u32[]{:S(2)}) collective-permute-start(f32[8,128]{1,0:T(8,128)S(1)} %maximum_maximum_fusion.refs_0_), channel_id=1, source_target_pairs={{0,96},{8,104},{16,112},{24,120},{32,0},{40,8},{48,16},{56,24},{64... | collective-permute-start | bytes 12296 | tf_op jit(solution)/shard_map/ppermute | solution.py:470

commit v8 on v7

--- a/solution.py
+++ b/solution.py
@@ -118,7 +118,9 @@
     own_ref,
     above_ref,
     left_ref,
+    left_outer_ref,
     right_ref,
+    right_outer_ref,
     drag_ref,
     analysis_ref,
     stiffness_ref,
@@ -146,12 +148,15 @@
     near = near_ref.shape[0]
     wall = wall_ref.shape[0]
     slots = own + near + wall
-    ext_ref[:, :, 0:HALO, :] = left_ref[...]
-    inner = slice(HALO, HALO + cols)
-    ext_ref[0:HALO, :, inner, :] = below_ref[rows - HALO :]
-    ext_ref[HALO : HALO + rows, :, inner, :] = own_ref[...]
-    ext_ref[HALO + rows :, :, inner, :] = above_ref[0:HALO]
-    ext_ref[:, :, HALO + cols :, :] = right_ref[...]
+    columns = (
+        (slice(0, HALO), left_outer_ref, 0, left_ref, left_outer_ref, HALO),
+        (slice(HALO, HALO + cols), below_ref, rows - HALO, own_ref, above_ref, 0),
+        (slice(HALO + cols, cols + 2 * HALO), right_outer_ref, 0, right_ref, right_outer_ref, HALO),
+    )
+    for where, before, low, beside, after, high in columns:
+        ext_ref[0:HALO, :, where, :] = before[low : low + HALO]
+        ext_ref[HALO : HALO + rows, :, where, :] = beside[...]
+        ext_ref[HALO + rows :, :, where, :] = after[high : high + HALO]
     for r in range(rows):
         for d in range(3):
             pos_ref[d, r * cols : (r + 1) * cols, :] = own_ref[r, d]
@@ -215,7 +220,7 @@
     pairs = own * points * (near // own) * points
     return pl.pallas_call(
         near_kernel,
-        in_specs=[in_smem] * 2 + [in_vmem] * 6 + [in_hbm, in_vmem, in_hbm],
+        in_specs=[in_smem] * 2 + [in_vmem] * 8 + [in_hbm, in_vmem, in_hbm],
         out_specs=[in_vmem] * 3,
         out_shape=[
             jax.ShapeDtypeStruct((rows, 3, cols, points), F32),
@@ -237,7 +242,7 @@
             flops=1000 * pairs, bytes_accessed=8 * 2**20, transcendentals=pairs
         ),
         name="near",
-    )(near_code, wall_code, below, pos, above, left, right, drag, *tables)
+    )(near_code, wall_code, below, pos, above, *left, *right, drag, *tables)
 
 
 def wall_kernel(stage, per, raw_ref, pos_ref, layer_ref, out_ref, target_ref, moment_ref):
@@ -498,14 +503,14 @@
     packed = jnp.concatenate(walls + [wall_weight[None]], axis=0)
 
     below, above = neighbours(pos, pos, "cx")
-    own_strips = pos[:, :, :HALO], pos[:, :, cols - HALO :]
+    inner_left, inner_right = neighbours(pos[:, :, :HALO], pos[:, :, cols - HALO :], "cy")
     below, above, later = lax.optimization_barrier((below, above, packed))
     wall_below, wall_above = neighbours(later, later, AXES)
-    low, high = (
-        jnp.concatenate([below[rows - HALO :, :, c : c + HALO], own, above[:HALO, :, c : c + HALO]])
-        for c, own in zip((0, cols - HALO), own_strips)
-    )
-    left, right = neighbours(low, high, "cy")
+    outer = [
+        jnp.concatenate([v[:, :, c : c + HALO] for v in (below[rows - HALO :], above[:HALO])])
+        for c in (0, cols - HALO)
+    ]
+    outer_left, outer_right = neighbours(*outer, "cy")
 
     patches = wall_pos.shape[0]
     all_patches = patches * lax.axis_size(AXES)
@@ -525,8 +530,8 @@
         below,
         pos,
         above,
-        left,
-        right,
+        (inner_left, outer_left),
+        (inner_right, outer_right),
         cell_drag.reshape(-1, 1),
         (analysis, stiffness[None, :], synthesis),
     )

time: 92.6 us -> 89.7 us (0.969)
  waiting for transfers between devices: 4.67 us -> 1.2 us
    ppermute x6 -> x8, waiting for transfers between devices: 2.73 us -> 0.02 us  [neighbours(): return (lax.ppermute(high, axis, up), lax.ppermute(low, axis, down))]
    ppermute x6 -> x8, starting transfers between devices: 15.7 us -> 17.2 us  [neighbours(): return (lax.ppermute(high, axis, up), lax.ppermute(low, axis, down))]
    ppermute x10, starting transfers between devices: 11.8 us -> 10.7 us  [over_all(): lax.ppermute(value, axis, pairs)]
  transfers between devices with their start and end apart: 16 -> 18, of which waited for: 4 -> 1; matrix products, arithmetic and copies ran while one was open for 4% -> 5% of each run, Pallas kernels for 59% -> 61%
where the time goes in v8:
time: 89.7 us; the launch traced here: 89 us
  Pallas kernels  54.8 us (61%)
  starting transfers between devices  28 us (31%)
  local copies, waits for them, and re-layouts  2.43 us (3%)
  other arithmetic  1.72 us (2%)
  waiting for transfers between devices  1.2 us (1%)
  between operations  0.91 us (1%)
    pallas_call x1, Pallas kernels, near_part(): pl.pallas_call(near_kernel, in_specs=[in_smem] * 2 + [in_vmem] * 8 + [in_...  37.3 us
    ppermute x8, starting transfers between devices, neighbours(): return (lax.ppermute(high, axis, up), lax.ppermute(low, axis, down))  17.2 us
    ppermute x10, starting transfers between devices, over_all(): lax.ppermute(value, axis, pairs)  10.7 us
    pallas_call x2, Pallas kernels, layer_part(): pl.pallas_call(kernel, in_specs=[in_smem] * len(scalars) + [in_vmem] * le...  9.08 us
    pallas_call x2, Pallas kernels, wall_part(): pl.pallas_call(functools.partial(wall_kernel, stage, per), in_specs=[in_v...  7.67 us
  transfers between devices with their start and end apart: 18, of which 1 were waited for; matrix products, arithmetic and copies ran while one was open for 5% of the time, Pallas kernels for 61%

profile of v8, /device:TPU:0, one launch (start us, length us, event | category | flops | bytes accessed | tf_op | source)
XLA Modules:
  0.0 89.0 jit_solution(2034029934794864867)
XLA Ops:
  0.6 1.6 %collective-permute-start = (f32[4,3,4,1024]{3,2,1,0:T(4,128)}, f32[4,3,4,1024]{3,2,1,0:T(4,128)S(1)}, u32[]{:S(2)}, u32[]{:S(2)}) collective-permute-start(f32[4,3,4,1024]{3,2,1,0:T(4,128)} %bitcast.8), channel_id=1, source_target_pairs={{0,8},{8,16},{16,24},{24,32},{32,40},{40,48},{48,56},{56,64},{64,7... | collective-permute-start | bytes 589832 | tf_op jit(solution)/shard_map/ppermute | solution.py:452
  2.3 4.8 %collective-permute-start.1 = (f32[4,3,4,1024]{3,2,1,0:T(4,128)}, f32[4,3,4,1024]{3,2,1,0:T(4,128)S(1)}, u32[]{:S(2)}, u32[]{:S(2)}) collective-permute-start(f32[4,3,4,1024]{3,2,1,0:T(4,128)} %bitcast.9), channel_id=1, source_target_pairs={{8,0},{16,8},{24,16},{32,24},{40,32},{48,40},{56,48},{64,56},{72,6... | collective-permute-start | bytes 589832 | tf_op jit(solution)/shard_map/ppermute | solution.py:452
  7.1 1.1 %fusion.13 = (f32[4,3,3,1024]{3,2,1,0:T(4,128)S(1)}, f32[4,3,3,1024]{3,2,1,0:T(4,128)S(1)}) fusion(f32[4,3,4,1024]{3,2,1,0:T(4,128)} %bitcast.10), kind=kLoop, calls=%fused_computation.43 | loop fusion | bytes 589824 | tf_op jit(solution)/shard_map/slice | solution.py:506
  8.2 2.9 %collective-permute-start.4 = (f32[4,3,3,1024]{3,2,1,0:T(4,128)S(1)}, f32[4,3,3,1024]{3,2,1,0:T(4,128)S(1)}, u32[]{:S(2)}, u32[]{:S(2)}) collective-permute-start(f32[4,3,3,1024]{3,2,1,0:T(4,128)S(1)} %get-tuple-element.32), channel_id=1, source_target_pairs={{1,0},{2,1},{3,2},{4,3},{5,4},{6,5},{7,6},{0,7},{9,8},{10,9},{11,1... | collective-permute-start | bytes 442376 | tf_op jit(solution)/shard_map/ppermute | solution.py:452
  11.2 0.8 copy.21
  12.0 0.8 pad_maximum_fusion.2.own_ref
  12.8 0.7 fusion
  13.5 0.1 fusion.11
  13.7 0.1 pad_maximum_fusion.1
  13.7 0.5 collective-permute-start.5
  14.3 0.1 pad_maximum_fusion
  14.4 0.1 copy.18
  14.5 0.1 reshape.13.near_ref
  14.6 0.1 copy.19
  14.7 0.1 reshape.14.wall_ref
  14.8 0.1 reshape.16.drag_ref
  14.9 2.1 %layer_first.1 = (f32[3,8,256]{2,1,0:T(8,128)S(1)}, bf16[8,192,256]{2,1,0:T(8,128)(2,1)S(1)}, bf16[8,32,256]{2,1,0:T(8,128)(2,1)S(1)}) custom-call(f32[10,8,256]{2,1,0:T(8,128)S(1)} %pad_maximum_fusion.2.own_ref), custom_call_target="tpu_custom_call" | custom-call | flops 524288000 | bytes 1048576 | tf_op jit(solution)/shard_map/layer_first/pallas_call | solution.py:412
  17.0 7.3 %collective-permute-start.17 = (f32[10,8,256]{2,1,0:T(8,128)S(1)}, f32[10,8,256]{2,1,0:T(8,128)S(1)}, u32[]{:S(2)}, u32[]{:S(2)}) collective-permute-start(f32[10,8,256]{2,1,0:T(8,128)S(1)} %pad_maximum_fusion.2.own_ref), channel_id=1, source_target_pairs={{1,0},{2,1},{3,2},{4,3},{5,4},{6,5},{7,6},{8,7},{9,8},{10,9},{11,1... | collective-permute-start | bytes 245768 | tf_op jit(solution)/shard_map/ppermute | solution.py:452
  24.3 37.3 %near.1 = (f32[4,3,4,1024]{3,2,1,0:T(4,128)S(1)}, f32[8,128]{1,0:T(8,128)S(1)}, f32[8,384,128]{2,1,0:T(8,128)S(1)}) custom-call(s32[32]{0:T(128)S(1)} %reshape.13.near_ref, s32[16]{0:T(128)S(1)} %reshape.14.wall_ref, f32[4,3,4,1024]{3,2,1,0:T(4,128)S(1)} %collective-permute-done.below_ref, f32[4,3,4,1024]{3,2,1,0:T(4,128)S(1)} %bitcast.11, ...), custom_call_target="tpu_custom_call" | custom-call | flops 33554432000 | bytes 8388608 | tf_op jit(solution)/shard_map/near/pallas_call | solution.py:221
  61.6 0.1 collective-permute-start.6
  61.7 1.2 %collective-permute-done.6 = f32[8,128]{1,0:T(8,128)S(1)} collective-permute-done((f32[8,128]{1,0:T(8,128)S(1)}, f32[8,128]{1,0:T(8,128)S(1)}, u32[]{:S(2)}, u32[]{:S(2)}) %collective-permute-start.6) | collective-permute-done | bytes 4128 | tf_op jit(solution)/shard_map/ppermute | solution.py:475
  62.9 3.2 %collective-permute-start.9 = (f32[8,128]{1,0:T(8,128)S(1)}, f32[8,128]{1,0:T(8,128)S(1)}, u32[]{:S(2)}, u32[]{:S(2)}) collective-permute-start(f32[8,128]{1,0:T(8,128)S(1)} %max.21), channel_id=1, source_target_pairs={{0,6},{1,7},{2,0},{3,1},{4,2},{5,3},{6,4},{7,5},{8,14},{9,15},{10,... | collective-permute-start | bytes 12296 | tf_op jit(solution)/shard_map/ppermute | solution.py:475
  66.1 7.0 %layer_second.1.layer_ref = f32[3,8,256]{2,1,0:T(8,128)S(1)} custom-call(s32[8,4]{1,0:T(8,128)S(1)} %add_select_fusion.listed_ref, f32[10,8,256]{2,1,0:T(8,128)S(1)} %pad_maximum_fusion.2.own_ref, f32[10,8,256]{2,1,0:T(8,128)S(1)} %collective-permute-done.16.before_ref, f32[10,8,256]{2,1,0:T(8,128)S(1)} %collective-permute-done.17.after_ref, ...), custom_call_target="tpu_custom_call" | custom-call | flops 2097152000 | bytes 1048576 | tf_op jit(solution)/shard_map/layer_second/pallas_call | solution.py:412
  73.1 0.1 collective-permute-start.10
  73.2 1.0 %collective-permute-start.11 = (f32[8,128]{1,0:T(8,128)S(1)}, f32[8,128]{1,0:T(8,128)S(1)}, u32[]{:S(2)}, u32[]{:S(2)}) collective-permute-start(f32[8,128]{1,0:T(8,128)S(1)} %maximum_maximum_fusion.1), channel_id=1, source_target_pairs={{0,16},{8,24},{16,0},{24,8},{32,48},{40,56},{48,32},{56,40},{64,80... | collective-permute-start | bytes 12296 | tf_op jit(solution)/shard_map/ppermute | solution.py:475
  74.3 2.2 %collective-permute-start.12 = (f32[8,128]{1,0:T(8,128)S(1)}, f32[8,128]{1,0:T(8,128)S(1)}, u32[]{:S(2)}, u32[]{:S(2)}) collective-permute-start(f32[8,128]{1,0:T(8,128)S(1)} %maximum_maximum_fusion.1), channel_id=1, source_target_pairs={{0,24},{8,0},{16,8},{24,16},{32,56},{40,32},{48,40},{56,48},{64,88... | collective-permute-start | bytes 12296 | tf_op jit(solution)/shard_map/ppermute | solution.py:475
  76.4 3.5 %wall_0.1.layer_ref = f32[3,8,256]{2,1,0:T(8,128)S(1)} custom-call(f32[8,384,128]{2,1,0:T(8,128)S(1)} %get-tuple-element.23.raw_ref, f32[3,8,256]{2,1,0:T(8,128)S(1)} %bitcast.14, f32[3,8,256]{2,1,0:T(8,128)S(1)} %layer_second.1.layer_ref), custom_call_target="tpu_custom_call" | custom-call | flops 2097152000 | bytes 2097152 | tf_op jit(solution)/shard_map/wall_0/pallas_call | solution.py:270
  80.0 0.1 collective-permute-start.13
  80.1 3.4 %collective-permute-start.14 = (f32[8,128]{1,0:T(8,128)S(1)}, f32[8,128]{1,0:T(8,128)S(1)}, u32[]{:S(2)}, u32[]{:S(2)}) collective-permute-start(f32[8,128]{1,0:T(8,128)S(1)} %maximum_maximum_fusion.refs_0_), channel_id=1, source_target_pairs={{0,64},{8,72},{16,80},{24,88},{32,96},{40,104},{48,112},{56,120},{... | collective-permute-start | bytes 12296 | tf_op jit(solution)/shard_map/ppermute | solution.py:475
  83.5 0.7 collective-permute-start.15
  84.1 4.1 %wall_1.1 = f32[3,8,256]{2,1,0:T(8,128)} custom-call(f32[8,384,128]{2,1,0:T(8,128)S(1)} %get-tuple-element.23.raw_ref, f32[3,8,256]{2,1,0:T(8,128)S(1)} %bitcast.15, f32[3,8,256]{2,1,0:T(8,128)S(1)} %wall_0.1.layer_ref), custom_call_target="tpu_custom_call" | custom-call | flops 2097152000 | bytes 2097152 | tf_op jit(solution)/shard_map/wall_1/pallas_call | solution.py:270
  88.3 0.7 move.1
  (37 shorter events, 0.2 us)
Async XLA Ops:
  0.6 13.7 %copy-start.4 = (s32[8,2]{0,1:T(2,128)S(1)}, s32[8,2]{0,1:T(2,128)}, u32[]{:S(2)}) copy-start(s32[8,2]{0,1:T(2,128)} %param.23) | copy-start | bytes 196
  0.6 14.1 %copy-start.3 = (f32[4,4]{1,0:T(4,128)S(1)}, f32[4,4]{1,0:T(4,128)}, u32[]{:S(2)}) copy-start(f32[4,4]{1,0:T(4,128)} %param.13) | copy-start | bytes 196
  0.6 12.9 %collective-permute-start = (f32[4,3,4,1024]{3,2,1,0:T(4,128)}, f32[4,3,4,1024]{3,2,1,0:T(4,128)S(1)}, u32[]{:S(2)}, u32[]{:S(2)}) collective-permute-start(f32[4,3,4,1024]{3,2,1,0:T(4,128)} %bitcast.8), channel_id=1, source_target_pairs={{0,8},{8,16},{16,24},{24,32},{32,40},{40,48},{48,56},{56,64},{64,7... | collective-permute-start | bytes 589832 | tf_op jit(solution)/shard_map/ppermute | solution.py:452
  2.3 11.2 %collective-permute-start.1 = (f32[4,3,4,1024]{3,2,1,0:T(4,128)}, f32[4,3,4,1024]{3,2,1,0:T(4,128)S(1)}, u32[]{:S(2)}, u32[]{:S(2)}) collective-permute-start(f32[4,3,4,1024]{3,2,1,0:T(4,128)} %bitcast.9), channel_id=1, source_target_pairs={{8,0},{16,8},{24,16},{32,24},{40,32},{48,40},{56,48},{64,56},{72,6... | collective-permute-start | bytes 589832 | tf_op jit(solution)/shard_map/ppermute | solution.py:452
  8.2 8.8 %collective-permute-start.2 = (f32[4,3,3,1024]{3,2,1,0:T(4,128)S(1)}, f32[4,3,3,1024]{3,2,1,0:T(4,128)S(1)}, u32[]{:S(2)}, u32[]{:S(2)}) collective-permute-start(f32[4,3,3,1024]{3,2,1,0:T(4,128)S(1)} %get-tuple-element.33), channel_id=1, source_target_pairs={{0,1},{1,2},{2,3},{3,4},{4,5},{5,6},{6,7},{7,0},{8,9},{9,10},{10,1... | collective-permute-start | bytes 442376 | tf_op jit(solution)/shard_map/ppermute | solution.py:452
  8.2 16.0 %collective-permute-start.4 = (f32[4,3,3,1024]{3,2,1,0:T(4,128)S(1)}, f32[4,3,3,1024]{3,2,1,0:T(4,128)S(1)}, u32[]{:S(2)}, u32[]{:S(2)}) collective-permute-start(f32[4,3,3,1024]{3,2,1,0:T(4,128)S(1)} %get-tuple-element.32), channel_id=1, source_target_pairs={{1,0},{2,1},{3,2},{4,3},{5,4},{6,5},{7,6},{0,7},{9,8},{10,9},{11,1... | collective-permute-start | bytes 442376 | tf_op jit(solution)/shard_map/ppermute | solution.py:452
  13.5 10.8 %copy-start = (f32[4,4,3,1024]{3,1,2,0:T(4,128)S(1)}, f32[4,4,3,1024]{3,1,2,0:T(4,128)}, u32[]{:S(2)}) copy-start(f32[4,4,3,1024]{3,1,2,0:T(4,128)} %param.12) | copy-start | bytes 589828
  13.5 10.8 %copy-start.2 = (f32[1024]{0:T(1024)S(1)}, f32[1024]{0:T(1024)}, u32[]{:S(2)}) copy-start(f32[1024]{0:T(1024)} %param.16) | copy-start | bytes 12292
  13.7 10.5 %collective-permute-start.5 = (f32[6,3,3,1024]{3,2,1,0:T(4,128)S(1)}, f32[6,3,3,1024]{3,2,1,0:T(4,128)S(1)}, u32[]{:S(2)}, u32[]{:S(2)}) collective-permute-start(f32[6,3,3,1024]{3,2,1,0:T(4,128)S(1)} %pad_maximum_fusion.1), channel_id=1, source_target_pairs={{1,0},{2,1},{3,2},{4,3},{5,4},{6,5},{7,6},{0,7},{9,8},{10,9},{11,1... | collective-permute-start | bytes 663560 | tf_op jit(solution)/shard_map/ppermute | solution.py:452
  14.3 9.9 %collective-permute-start.3 = (f32[6,3,3,1024]{3,2,1,0:T(4,128)S(1)}, f32[6,3,3,1024]{3,2,1,0:T(4,128)S(1)}, u32[]{:S(2)}, u32[]{:S(2)}) collective-permute-start(f32[6,3,3,1024]{3,2,1,0:T(4,128)S(1)} %pad_maximum_fusion), channel_id=1, source_target_pairs={{0,1},{1,2},{2,3},{3,4},{4,5},{5,6},{6,7},{7,0},{8,9},{9,10},{10,1... | collective-permute-start | bytes 663560 | tf_op jit(solution)/shard_map/ppermute | solution.py:452
  14.9 51.2 %collective-permute-start.16 = (f32[10,8,256]{2,1,0:T(8,128)S(1)}, f32[10,8,256]{2,1,0:T(8,128)S(1)}, u32[]{:S(2)}, u32[]{:S(2)}) collective-permute-start(f32[10,8,256]{2,1,0:T(8,128)S(1)} %pad_maximum_fusion.2.own_ref), channel_id=1, source_target_pairs={{0,1},{1,2},{2,3},{3,4},{4,5},{5,6},{6,7},{7,8},{8,9},{9,10},{10,1... | collective-permute-start | bytes 245768 | tf_op jit(solution)/shard_map/ppermute | solution.py:452
  17.0 49.1 %collective-permute-start.17 = (f32[10,8,256]{2,1,0:T(8,128)S(1)}, f32[10,8,256]{2,1,0:T(8,128)S(1)}, u32[]{:S(2)}, u32[]{:S(2)}) collective-permute-start(f32[10,8,256]{2,1,0:T(8,128)S(1)} %pad_maximum_fusion.2.own_ref), channel_id=1, source_target_pairs={{1,0},{2,1},{3,2},{4,3},{5,4},{6,5},{7,6},{8,7},{9,8},{10,9},{11,1... | collective-permute-start | bytes 245768 | tf_op jit(solution)/shard_map/ppermute | solution.py:452
  61.6 1.2 %collective-permute-start.6 = (f32[8,128]{1,0:T(8,128)S(1)}, f32[8,128]{1,0:T(8,128)S(1)}, u32[]{:S(2)}, u32[]{:S(2)}) collective-permute-start(f32[8,128]{1,0:T(8,128)S(1)} %get-tuple-element.21), channel_id=1, source_target_pairs={{0,1},{1,0},{2,3},{3,2},{4,5},{5,4},{6,7},{7,6},{8,9},{9,8},{10,11... | collective-permute-start | bytes 12296 | tf_op jit(solution)/shard_map/ppermute | solution.py:475
  62.8 10.2 %collective-permute-start.7 = (f32[8,128]{1,0:T(8,128)S(1)}, f32[8,128]{1,0:T(8,128)S(1)}, u32[]{:S(2)}, u32[]{:S(2)}) collective-permute-start(f32[8,128]{1,0:T(8,128)S(1)} %max.21), channel_id=1, source_target_pairs={{0,2},{1,3},{2,4},{3,5},{4,6},{5,7},{6,0},{7,1},{8,10},{9,11},{10,... | collective-permute-start | bytes 12296 | tf_op jit(solution)/shard_map/ppermute | solution.py:475
  62.8 10.2 %collective-permute-start.8 = (f32[8,128]{1,0:T(8,128)S(1)}, f32[8,128]{1,0:T(8,128)S(1)}, u32[]{:S(2)}, u32[]{:S(2)}) collective-permute-start(f32[8,128]{1,0:T(8,128)S(1)} %max.21), channel_id=1, source_target_pairs={{0,4},{1,5},{2,6},{3,7},{4,0},{5,1},{6,2},{7,3},{8,12},{9,13},{10,... | collective-permute-start | bytes 12296 | tf_op jit(solution)/shard_map/ppermute | solution.py:475
  62.9 10.2 %collective-permute-start.9 = (f32[8,128]{1,0:T(8,128)S(1)}, f32[8,128]{1,0:T(8,128)S(1)}, u32[]{:S(2)}, u32[]{:S(2)}) collective-permute-start(f32[8,128]{1,0:T(8,128)S(1)} %max.21), channel_id=1, source_target_pairs={{0,6},{1,7},{2,0},{3,1},{4,2},{5,3},{6,4},{7,5},{8,14},{9,15},{10,... | collective-permute-start | bytes 12296 | tf_op jit(solution)/shard_map/ppermute | solution.py:475
  66.1 10.3 %copy-start.1 = (f32[8,3,256]{2,0,1:T(8,128)S(1)}, f32[8,3,256]{2,0,1:T(8,128)}, u32[]{:S(2)}) copy-start(f32[8,3,256]{2,0,1:T(8,128)} %param.18) | copy-start | bytes 73732
  73.1 6.8 %collective-permute-start.10 = (f32[8,128]{1,0:T(8,128)S(1)}, f32[8,128]{1,0:T(8,128)S(1)}, u32[]{:S(2)}, u32[]{:S(2)}) collective-permute-start(f32[8,128]{1,0:T(8,128)S(1)} %maximum_maximum_fusion.1), channel_id=1, source_target_pairs={{0,8},{8,16},{16,24},{24,0},{32,40},{40,48},{48,56},{56,32},{64,72... | collective-permute-start | bytes 12296 | tf_op jit(solution)/shard_map/ppermute | solution.py:475
  73.2 6.8 %collective-permute-start.11 = (f32[8,128]{1,0:T(8,128)S(1)}, f32[8,128]{1,0:T(8,128)S(1)}, u32[]{:S(2)}, u32[]{:S(2)}) collective-permute-start(f32[8,128]{1,0:T(8,128)S(1)} %maximum_maximum_fusion.1), channel_id=1, source_target_pairs={{0,16},{8,24},{16,0},{24,8},{32,48},{40,56},{48,32},{56,40},{64,80... | collective-permute-start | bytes 12296 | tf_op jit(solution)/shard_map/ppermute | solution.py:475
  74.3 5.7 %collective-permute-start.12 = (f32[8,128]{1,0:T(8,128)S(1)}, f32[8,128]{1,0:T(8,128)S(1)}, u32[]{:S(2)}, u32[]{:S(2)}) collective-permute-start(f32[8,128]{1,0:T(8,128)S(1)} %maximum_maximum_fusion.1), channel_id=1, source_target_pairs={{0,24},{8,0},{16,8},{24,16},{32,56},{40,32},{48,40},{56,48},{64,88... | collective-permute-start | bytes 12296 | tf_op jit(solution)/shard_map/ppermute | solution.py:475
  80.0 8.3 %collective-permute-start.13 = (f32[8,128]{1,0:T(8,128)S(1)}, f32[8,128]{1,0:T(8,128)S(1)}, u32[]{:S(2)}, u32[]{:S(2)}) collective-permute-start(f32[8,128]{1,0:T(8,128)S(1)} %maximum_maximum_fusion.refs_0_), channel_id=1, source_target_pairs={{0,32},{8,40},{16,48},{24,56},{32,64},{40,72},{48,80},{56,88},{64,... | collective-permute-start | bytes 12296 | tf_op jit(solution)/shard_map/ppermute | solution.py:475
  80.1 8.2 %collective-permute-start.14 = (f32[8,128]{1,0:T(8,128)S(1)}, f32[8,128]{1,0:T(8,128)S(1)}, u32[]{:S(2)}, u32[]{:S(2)}) collective-permute-start(f32[8,128]{1,0:T(8,128)S(1)} %maximum_maximum_fusion.refs_0_), channel_id=1, source_target_pairs={{0,64},{8,72},{16,80},{24,88},{32,96},{40,104},{48,112},{56,120},{... | collective-permute-start | bytes 12296 | tf_op jit(solution)/shard_map/ppermute | solution.py:475
  83.5 4.8 %collective-permute-start.15 = (f32[8,128]{1,0:T(8,128)S(1)}, f32[8,128]{1,0:T(8,128)S(1)}, u32[]{:S(2)}, u32[]{:S(2)}) collective-permute-start(f32[8,128]{1,0:T(8,128)S(1)} %maximum_maximum_fusion.refs_0_), channel_id=1, source_target_pairs={{0,96},{8,104},{16,112},{24,120},{32,0},{40,8},{48,16},{56,24},{64... | collective-permute-start | bytes 12296 | tf_op jit(solution)/shard_map/ppermute | solution.py:475

commit v9 on v8

--- a/solution.py
+++ b/solution.py
@@ -83,16 +83,26 @@
         put_rows(ref, first + k, 8, stride, row)
 
 
+def weighted(features, factor):
+    return lax.dot_general(
+        features, factor, (((1,), (1,)), ((), ())), preferred_element_type=F32
+    )
+
+
 def stokes_moments(raw_ref, slots, target):
     total = None
     for slot in slots:
         base = pl.multiple_of(slot * STOKES_ROWS, 8)
         left = source_rows(get_rows(raw_ref, base, 8))
-        square = product(left, target)
+        targets_first = target.shape[1] < left.shape[1]
+        square = product(target, left) if targets_first else product(left, target)
         root = lax.rsqrt(jnp.maximum(square, SOFT))
         factor = (root * root * root).astype(BF16)
         features = feature_rows(get_rows(raw_ref, base + 8, 16))
-        part = jnp.dot(features, factor, preferred_element_type=F32)
+        if targets_first:
+            part = weighted(features, factor)
+        else:
+            part = jnp.dot(features, factor, preferred_element_type=F32)
         total = part if total is None else total + part
     return total[0:16] + total[16:32] + total[32:48]
 
@@ -298,12 +308,12 @@
         near, form = target_rows(raw[0:8]), target_rows(raw[8:24])
         total = None
         for s in sources(p):
-            square = product(left_ref[s, 0:64], near)
-            scalar = product(left_ref[s, 64:192], form)
+            square = product(near, left_ref[s, 0:64])
+            scalar = product(form, left_ref[s, 64:192])
             root = lax.rsqrt(jnp.maximum(square, SOFT))
             double = root * root
             scalar = (scalar * (double * double * root)).astype(BF16)
-            part = jnp.dot(feature_ref[s], scalar, preferred_element_type=F32)
+            part = weighted(feature_ref[s], scalar)
             total = part if total is None else total + part
         moments = total[0:8] + total[8:16] + total[16:24]
         put_rows(moment_ref, p, 8, patches, moments)

time: 89.7 us -> 87.6 us (0.977)
  Pallas kernels: 54.8 us -> 52.3 us
    pallas_call x2, Pallas kernels: 7.67 us -> 5.73 us  [wall_part(): pl.pallas_call(functools.partial(wall_kernel, stage, per), in_specs=[in_v...]
  transfers between devices with their start and end apart: 18 -> 18, of which waited for: 1 -> 1; matrix products, arithmetic and copies ran while one was open for 5% -> 5% of each run, Pallas kernels for 61% -> 59%
where the time goes in v9:
time: 87.6 us; the launch traced here: 87.4 us
  Pallas kernels  52.3 us (60%)
  starting transfers between devices  28.8 us (33%)
  local copies, waits for them, and re-layouts  2.43 us (3%)
  other arithmetic  1.72 us (2%)
  waiting for transfers between devices  1.2 us (1%)
  between operations  0.9 us (1%)
    pallas_call x1, Pallas kernels, near_part(): pl.pallas_call(near_kernel, in_specs=[in_smem] * 2 + [in_vmem] * 8 + [in_...  37.3 us
    ppermute x8, starting transfers between devices, neighbours(): return (lax.ppermute(high, axis, up), lax.ppermute(low, axis, down))  17.2 us
    ppermute x10, starting transfers between devices, over_all(): lax.ppermute(value, axis, pairs)  11.6 us
    pallas_call x2, Pallas kernels, layer_part(): pl.pallas_call(kernel, in_specs=[in_smem] * len(scalars) + [in_vmem] * le...  8.49 us
    pallas_call x2, Pallas kernels, wall_part(): pl.pallas_call(functools.partial(wall_kernel, stage, per), in_specs=[in_v...  5.73 us
  transfers between devices with their start and end apart: 18, of which 1 were waited for; matrix products, arithmetic and copies ran while one was open for 5% of the time, Pallas kernels for 59%

profile of v9, /device:TPU:0, one launch (start us, length us, event | category | flops | bytes accessed | tf_op | source)
XLA Modules:
  0.0 87.4 jit_solution(4985187159237779770)
XLA Ops:
  0.6 1.6 %collective-permute-start = (f32[4,3,4,1024]{3,2,1,0:T(4,128)}, f32[4,3,4,1024]{3,2,1,0:T(4,128)S(1)}, u32[]{:S(2)}, u32[]{:S(2)}) collective-permute-start(f32[4,3,4,1024]{3,2,1,0:T(4,128)} %bitcast.8), channel_id=1, source_target_pairs={{0,8},{8,16},{16,24},{24,32},{32,40},{40,48},{48,56},{56,64},{64,7... | collective-permute-start | bytes 589832 | tf_op jit(solution)/shard_map/ppermute | solution.py:462
  2.3 4.8 %collective-permute-start.1 = (f32[4,3,4,1024]{3,2,1,0:T(4,128)}, f32[4,3,4,1024]{3,2,1,0:T(4,128)S(1)}, u32[]{:S(2)}, u32[]{:S(2)}) collective-permute-start(f32[4,3,4,1024]{3,2,1,0:T(4,128)} %bitcast.9), channel_id=1, source_target_pairs={{8,0},{16,8},{24,16},{32,24},{40,32},{48,40},{56,48},{64,56},{72,6... | collective-permute-start | bytes 589832 | tf_op jit(solution)/shard_map/ppermute | solution.py:462
  7.1 1.1 %fusion.13 = (f32[4,3,3,1024]{3,2,1,0:T(4,128)S(1)}, f32[4,3,3,1024]{3,2,1,0:T(4,128)S(1)}) fusion(f32[4,3,4,1024]{3,2,1,0:T(4,128)} %bitcast.10), kind=kLoop, calls=%fused_computation.43 | loop fusion | bytes 589824 | tf_op jit(solution)/shard_map/slice | solution.py:516
  8.2 2.9 %collective-permute-start.4 = (f32[4,3,3,1024]{3,2,1,0:T(4,128)S(1)}, f32[4,3,3,1024]{3,2,1,0:T(4,128)S(1)}, u32[]{:S(2)}, u32[]{:S(2)}) collective-permute-start(f32[4,3,3,1024]{3,2,1,0:T(4,128)S(1)} %get-tuple-element.32), channel_id=1, source_target_pairs={{1,0},{2,1},{3,2},{4,3},{5,4},{6,5},{7,6},{0,7},{9,8},{10,9},{11,1... | collective-permute-start | bytes 442376 | tf_op jit(solution)/shard_map/ppermute | solution.py:462
  11.2 0.8 copy.21
  12.0 0.8 pad_maximum_fusion.2.own_ref
  12.8 0.7 fusion
  13.5 0.1 fusion.11
  13.7 0.1 pad_maximum_fusion.1
  13.7 0.5 collective-permute-start.5
  14.3 0.1 pad_maximum_fusion
  14.4 0.1 copy.18
  14.5 0.1 reshape.13.near_ref
  14.6 0.1 copy.19
  14.7 0.1 reshape.14.wall_ref
  14.8 0.1 reshape.16.drag_ref
  14.9 2.1 %layer_first.1 = (f32[3,8,256]{2,1,0:T(8,128)S(1)}, bf16[8,192,256]{2,1,0:T(8,128)(2,1)S(1)}, bf16[8,32,256]{2,1,0:T(8,128)(2,1)S(1)}) custom-call(f32[10,8,256]{2,1,0:T(8,128)S(1)} %pad_maximum_fusion.2.own_ref), custom_call_target="tpu_custom_call" | custom-call | flops 524288000 | bytes 1048576 | tf_op jit(solution)/shard_map/layer_first/pallas_call | solution.py:422
  17.0 7.3 %collective-permute-start.17 = (f32[10,8,256]{2,1,0:T(8,128)S(1)}, f32[10,8,256]{2,1,0:T(8,128)S(1)}, u32[]{:S(2)}, u32[]{:S(2)}) collective-permute-start(f32[10,8,256]{2,1,0:T(8,128)S(1)} %pad_maximum_fusion.2.own_ref), channel_id=1, source_target_pairs={{1,0},{2,1},{3,2},{4,3},{5,4},{6,5},{7,6},{8,7},{9,8},{10,9},{11,1... | collective-permute-start | bytes 245768 | tf_op jit(solution)/shard_map/ppermute | solution.py:462
  24.3 37.3 %near.1 = (f32[4,3,4,1024]{3,2,1,0:T(4,128)S(1)}, f32[8,128]{1,0:T(8,128)S(1)}, f32[8,384,128]{2,1,0:T(8,128)S(1)}) custom-call(s32[32]{0:T(128)S(1)} %reshape.13.near_ref, s32[16]{0:T(128)S(1)} %reshape.14.wall_ref, f32[4,3,4,1024]{3,2,1,0:T(4,128)S(1)} %collective-permute-done.below_ref, f32[4,3,4,1024]{3,2,1,0:T(4,128)S(1)} %bitcast.11, ...), custom_call_target="tpu_custom_call" | custom-call | flops 33554432000 | bytes 8388608 | tf_op jit(solution)/shard_map/near/pallas_call | solution.py:231
  61.6 0.1 collective-permute-start.6
  61.7 1.2 %collective-permute-done.6 = f32[8,128]{1,0:T(8,128)S(1)} collective-permute-done((f32[8,128]{1,0:T(8,128)S(1)}, f32[8,128]{1,0:T(8,128)S(1)}, u32[]{:S(2)}, u32[]{:S(2)}) %collective-permute-start.6) | collective-permute-done | bytes 4128 | tf_op jit(solution)/shard_map/ppermute | solution.py:485
  62.9 3.2 %collective-permute-start.9 = (f32[8,128]{1,0:T(8,128)S(1)}, f32[8,128]{1,0:T(8,128)S(1)}, u32[]{:S(2)}, u32[]{:S(2)}) collective-permute-start(f32[8,128]{1,0:T(8,128)S(1)} %max.21), channel_id=1, source_target_pairs={{0,6},{1,7},{2,0},{3,1},{4,2},{5,3},{6,4},{7,5},{8,14},{9,15},{10,... | collective-permute-start | bytes 12296 | tf_op jit(solution)/shard_map/ppermute | solution.py:485
  66.1 6.3 %layer_second.1.layer_ref = f32[3,8,256]{2,1,0:T(8,128)S(1)} custom-call(s32[8,4]{1,0:T(8,128)S(1)} %add_select_fusion.listed_ref, f32[10,8,256]{2,1,0:T(8,128)S(1)} %pad_maximum_fusion.2.own_ref, f32[10,8,256]{2,1,0:T(8,128)S(1)} %collective-permute-done.16.before_ref, f32[10,8,256]{2,1,0:T(8,128)S(1)} %collective-permute-done.17.after_ref, ...), custom_call_target="tpu_custom_call" | custom-call | flops 2097152000 | bytes 1048576 | tf_op jit(solution)/shard_map/layer_second/pallas_call | solution.py:422
  72.5 0.1 collective-permute-start.10
  72.6 1.0 %collective-permute-start.11 = (f32[8,128]{1,0:T(8,128)S(1)}, f32[8,128]{1,0:T(8,128)S(1)}, u32[]{:S(2)}, u32[]{:S(2)}) collective-permute-start(f32[8,128]{1,0:T(8,128)S(1)} %maximum_maximum_fusion.1), channel_id=1, source_target_pairs={{0,16},{8,24},{16,0},{24,8},{32,48},{40,56},{48,32},{56,40},{64,80... | collective-permute-start | bytes 12296 | tf_op jit(solution)/shard_map/ppermute | solution.py:485
  73.6 2.2 %collective-permute-start.12 = (f32[8,128]{1,0:T(8,128)S(1)}, f32[8,128]{1,0:T(8,128)S(1)}, u32[]{:S(2)}, u32[]{:S(2)}) collective-permute-start(f32[8,128]{1,0:T(8,128)S(1)} %maximum_maximum_fusion.1), channel_id=1, source_target_pairs={{0,24},{8,0},{16,8},{24,16},{32,56},{40,32},{48,40},{56,48},{64,88... | collective-permute-start | bytes 12296 | tf_op jit(solution)/shard_map/ppermute | solution.py:485
  75.9 2.6 %wall_0.1.layer_ref = f32[3,8,256]{2,1,0:T(8,128)S(1)} custom-call(f32[8,384,128]{2,1,0:T(8,128)S(1)} %get-tuple-element.23.raw_ref, f32[3,8,256]{2,1,0:T(8,128)S(1)} %bitcast.14, f32[3,8,256]{2,1,0:T(8,128)S(1)} %layer_second.1.layer_ref), custom_call_target="tpu_custom_call" | custom-call | flops 2097152000 | bytes 2097152 | tf_op jit(solution)/shard_map/wall_0/pallas_call | solution.py:280
  78.5 0.7 collective-permute-start.13
  79.2 3.6 %collective-permute-start.14 = (f32[8,128]{1,0:T(8,128)S(1)}, f32[8,128]{1,0:T(8,128)S(1)}, u32[]{:S(2)}, u32[]{:S(2)}) collective-permute-start(f32[8,128]{1,0:T(8,128)S(1)} %maximum_maximum_fusion.refs_0_), channel_id=1, source_target_pairs={{0,64},{8,72},{16,80},{24,88},{32,96},{40,104},{48,112},{56,120},{... | collective-permute-start | bytes 12296 | tf_op jit(solution)/shard_map/ppermute | solution.py:485
  82.8 0.7 collective-permute-start.15
  83.5 3.2 %wall_1.1 = f32[3,8,256]{2,1,0:T(8,128)} custom-call(f32[8,384,128]{2,1,0:T(8,128)S(1)} %get-tuple-element.23.raw_ref, f32[3,8,256]{2,1,0:T(8,128)S(1)} %bitcast.15, f32[3,8,256]{2,1,0:T(8,128)S(1)} %wall_0.1.layer_ref), custom_call_target="tpu_custom_call" | custom-call | flops 2097152000 | bytes 2097152 | tf_op jit(solution)/shard_map/wall_1/pallas_call | solution.py:280
  86.6 0.7 move.1
  (37 shorter events, 0.2 us)
Async XLA Ops:
  0.6 13.7 %copy-start.4 = (s32[8,2]{0,1:T(2,128)S(1)}, s32[8,2]{0,1:T(2,128)}, u32[]{:S(2)}) copy-start(s32[8,2]{0,1:T(2,128)} %param.23) | copy-start | bytes 196
  0.6 14.1 %copy-start.3 = (f32[4,4]{1,0:T(4,128)S(1)}, f32[4,4]{1,0:T(4,128)}, u32[]{:S(2)}) copy-start(f32[4,4]{1,0:T(4,128)} %param.13) | copy-start | bytes 196
  0.6 12.9 %collective-permute-start = (f32[4,3,4,1024]{3,2,1,0:T(4,128)}, f32[4,3,4,1024]{3,2,1,0:T(4,128)S(1)}, u32[]{:S(2)}, u32[]{:S(2)}) collective-permute-start(f32[4,3,4,1024]{3,2,1,0:T(4,128)} %bitcast.8), channel_id=1, source_target_pairs={{0,8},{8,16},{16,24},{24,32},{32,40},{40,48},{48,56},{56,64},{64,7... | collective-permute-start | bytes 589832 | tf_op jit(solution)/shard_map/ppermute | solution.py:462
  2.3 11.2 %collective-permute-start.1 = (f32[4,3,4,1024]{3,2,1,0:T(4,128)}, f32[4,3,4,1024]{3,2,1,0:T(4,128)S(1)}, u32[]{:S(2)}, u32[]{:S(2)}) collective-permute-start(f32[4,3,4,1024]{3,2,1,0:T(4,128)} %bitcast.9), channel_id=1, source_target_pairs={{8,0},{16,8},{24,16},{32,24},{40,32},{48,40},{56,48},{64,56},{72,6... | collective-permute-start | bytes 589832 | tf_op jit(solution)/shard_map/ppermute | solution.py:462
  8.2 8.8 %collective-permute-start.2 = (f32[4,3,3,1024]{3,2,1,0:T(4,128)S(1)}, f32[4,3,3,1024]{3,2,1,0:T(4,128)S(1)}, u32[]{:S(2)}, u32[]{:S(2)}) collective-permute-start(f32[4,3,3,1024]{3,2,1,0:T(4,128)S(1)} %get-tuple-element.33), channel_id=1, source_target_pairs={{0,1},{1,2},{2,3},{3,4},{4,5},{5,6},{6,7},{7,0},{8,9},{9,10},{10,1... | collective-permute-start | bytes 442376 | tf_op jit(solution)/shard_map/ppermute | solution.py:462
  8.2 16.1 %collective-permute-start.4 = (f32[4,3,3,1024]{3,2,1,0:T(4,128)S(1)}, f32[4,3,3,1024]{3,2,1,0:T(4,128)S(1)}, u32[]{:S(2)}, u32[]{:S(2)}) collective-permute-start(f32[4,3,3,1024]{3,2,1,0:T(4,128)S(1)} %get-tuple-element.32), channel_id=1, source_target_pairs={{1,0},{2,1},{3,2},{4,3},{5,4},{6,5},{7,6},{0,7},{9,8},{10,9},{11,1... | collective-permute-start | bytes 442376 | tf_op jit(solution)/shard_map/ppermute | solution.py:462
  13.5 10.8 %copy-start = (f32[4,4,3,1024]{3,1,2,0:T(4,128)S(1)}, f32[4,4,3,1024]{3,1,2,0:T(4,128)}, u32[]{:S(2)}) copy-start(f32[4,4,3,1024]{3,1,2,0:T(4,128)} %param.12) | copy-start | bytes 589828
  13.5 10.8 %copy-start.2 = (f32[1024]{0:T(1024)S(1)}, f32[1024]{0:T(1024)}, u32[]{:S(2)}) copy-start(f32[1024]{0:T(1024)} %param.16) | copy-start | bytes 12292
  13.7 10.6 %collective-permute-start.5 = (f32[6,3,3,1024]{3,2,1,0:T(4,128)S(1)}, f32[6,3,3,1024]{3,2,1,0:T(4,128)S(1)}, u32[]{:S(2)}, u32[]{:S(2)}) collective-permute-start(f32[6,3,3,1024]{3,2,1,0:T(4,128)S(1)} %pad_maximum_fusion.1), channel_id=1, source_target_pairs={{1,0},{2,1},{3,2},{4,3},{5,4},{6,5},{7,6},{0,7},{9,8},{10,9},{11,1... | collective-permute-start | bytes 663560 | tf_op jit(solution)/shard_map/ppermute | solution.py:462
  14.3 10.0 %collective-permute-start.3 = (f32[6,3,3,1024]{3,2,1,0:T(4,128)S(1)}, f32[6,3,3,1024]{3,2,1,0:T(4,128)S(1)}, u32[]{:S(2)}, u32[]{:S(2)}) collective-permute-start(f32[6,3,3,1024]{3,2,1,0:T(4,128)S(1)} %pad_maximum_fusion), channel_id=1, source_target_pairs={{0,1},{1,2},{2,3},{3,4},{4,5},{5,6},{6,7},{7,0},{8,9},{9,10},{10,1... | collective-permute-start | bytes 663560 | tf_op jit(solution)/shard_map/ppermute | solution.py:462
  14.9 51.3 %collective-permute-start.16 = (f32[10,8,256]{2,1,0:T(8,128)S(1)}, f32[10,8,256]{2,1,0:T(8,128)S(1)}, u32[]{:S(2)}, u32[]{:S(2)}) collective-permute-start(f32[10,8,256]{2,1,0:T(8,128)S(1)} %pad_maximum_fusion.2.own_ref), channel_id=1, source_target_pairs={{0,1},{1,2},{2,3},{3,4},{4,5},{5,6},{6,7},{7,8},{8,9},{9,10},{10,1... | collective-permute-start | bytes 245768 | tf_op jit(solution)/shard_map/ppermute | solution.py:462
  17.0 49.1 %collective-permute-start.17 = (f32[10,8,256]{2,1,0:T(8,128)S(1)}, f32[10,8,256]{2,1,0:T(8,128)S(1)}, u32[]{:S(2)}, u32[]{:S(2)}) collective-permute-start(f32[10,8,256]{2,1,0:T(8,128)S(1)} %pad_maximum_fusion.2.own_ref), channel_id=1, source_target_pairs={{1,0},{2,1},{3,2},{4,3},{5,4},{6,5},{7,6},{8,7},{9,8},{10,9},{11,1... | collective-permute-start | bytes 245768 | tf_op jit(solution)/shard_map/ppermute | solution.py:462
  61.6 1.2 %collective-permute-start.6 = (f32[8,128]{1,0:T(8,128)S(1)}, f32[8,128]{1,0:T(8,128)S(1)}, u32[]{:S(2)}, u32[]{:S(2)}) collective-permute-start(f32[8,128]{1,0:T(8,128)S(1)} %get-tuple-element.21), channel_id=1, source_target_pairs={{0,1},{1,0},{2,3},{3,2},{4,5},{5,4},{6,7},{7,6},{8,9},{9,8},{10,11... | collective-permute-start | bytes 12296 | tf_op jit(solution)/shard_map/ppermute | solution.py:485
  62.9 9.6 %collective-permute-start.7 = (f32[8,128]{1,0:T(8,128)S(1)}, f32[8,128]{1,0:T(8,128)S(1)}, u32[]{:S(2)}, u32[]{:S(2)}) collective-permute-start(f32[8,128]{1,0:T(8,128)S(1)} %max.21), channel_id=1, source_target_pairs={{0,2},{1,3},{2,4},{3,5},{4,6},{5,7},{6,0},{7,1},{8,10},{9,11},{10,... | collective-permute-start | bytes 12296 | tf_op jit(solution)/shard_map/ppermute | solution.py:485
  62.9 9.6 %collective-permute-start.8 = (f32[8,128]{1,0:T(8,128)S(1)}, f32[8,128]{1,0:T(8,128)S(1)}, u32[]{:S(2)}, u32[]{:S(2)}) collective-permute-start(f32[8,128]{1,0:T(8,128)S(1)} %max.21), channel_id=1, source_target_pairs={{0,4},{1,5},{2,6},{3,7},{4,0},{5,1},{6,2},{7,3},{8,12},{9,13},{10,... | collective-permute-start | bytes 12296 | tf_op jit(solution)/shard_map/ppermute | solution.py:485
  62.9 9.6 %collective-permute-start.9 = (f32[8,128]{1,0:T(8,128)S(1)}, f32[8,128]{1,0:T(8,128)S(1)}, u32[]{:S(2)}, u32[]{:S(2)}) collective-permute-start(f32[8,128]{1,0:T(8,128)S(1)} %max.21), channel_id=1, source_target_pairs={{0,6},{1,7},{2,0},{3,1},{4,2},{5,3},{6,4},{7,5},{8,14},{9,15},{10,... | collective-permute-start | bytes 12296 | tf_op jit(solution)/shard_map/ppermute | solution.py:485
  66.1 9.7 %copy-start.1 = (f32[8,3,256]{2,0,1:T(8,128)S(1)}, f32[8,3,256]{2,0,1:T(8,128)}, u32[]{:S(2)}) copy-start(f32[8,3,256]{2,0,1:T(8,128)} %param.18) | copy-start | bytes 73732
  72.5 5.9 %collective-permute-start.10 = (f32[8,128]{1,0:T(8,128)S(1)}, f32[8,128]{1,0:T(8,128)S(1)}, u32[]{:S(2)}, u32[]{:S(2)}) collective-permute-start(f32[8,128]{1,0:T(8,128)S(1)} %maximum_maximum_fusion.1), channel_id=1, source_target_pairs={{0,8},{8,16},{16,24},{24,0},{32,40},{40,48},{48,56},{56,32},{64,72... | collective-permute-start | bytes 12296 | tf_op jit(solution)/shard_map/ppermute | solution.py:485
  72.6 5.8 %collective-permute-start.11 = (f32[8,128]{1,0:T(8,128)S(1)}, f32[8,128]{1,0:T(8,128)S(1)}, u32[]{:S(2)}, u32[]{:S(2)}) collective-permute-start(f32[8,128]{1,0:T(8,128)S(1)} %maximum_maximum_fusion.1), channel_id=1, source_target_pairs={{0,16},{8,24},{16,0},{24,8},{32,48},{40,56},{48,32},{56,40},{64,80... | collective-permute-start | bytes 12296 | tf_op jit(solution)/shard_map/ppermute | solution.py:485
  73.6 4.8 %collective-permute-start.12 = (f32[8,128]{1,0:T(8,128)S(1)}, f32[8,128]{1,0:T(8,128)S(1)}, u32[]{:S(2)}, u32[]{:S(2)}) collective-permute-start(f32[8,128]{1,0:T(8,128)S(1)} %maximum_maximum_fusion.1), channel_id=1, source_target_pairs={{0,24},{8,0},{16,8},{24,16},{32,56},{40,32},{48,40},{56,48},{64,88... | collective-permute-start | bytes 12296 | tf_op jit(solution)/shard_map/ppermute | solution.py:485
  78.5 8.2 %collective-permute-start.13 = (f32[8,128]{1,0:T(8,128)S(1)}, f32[8,128]{1,0:T(8,128)S(1)}, u32[]{:S(2)}, u32[]{:S(2)}) collective-permute-start(f32[8,128]{1,0:T(8,128)S(1)} %maximum_maximum_fusion.refs_0_), channel_id=1, source_target_pairs={{0,32},{8,40},{16,48},{24,56},{32,64},{40,72},{48,80},{56,88},{64,... | collective-permute-start | bytes 12296 | tf_op jit(solution)/shard_map/ppermute | solution.py:485
  79.2 7.5 %collective-permute-start.14 = (f32[8,128]{1,0:T(8,128)S(1)}, f32[8,128]{1,0:T(8,128)S(1)}, u32[]{:S(2)}, u32[]{:S(2)}) collective-permute-start(f32[8,128]{1,0:T(8,128)S(1)} %maximum_maximum_fusion.refs_0_), channel_id=1, source_target_pairs={{0,64},{8,72},{16,80},{24,88},{32,96},{40,104},{48,112},{56,120},{... | collective-permute-start | bytes 12296 | tf_op jit(solution)/shard_map/ppermute | solution.py:485
  82.8 3.8 %collective-permute-start.15 = (f32[8,128]{1,0:T(8,128)S(1)}, f32[8,128]{1,0:T(8,128)S(1)}, u32[]{:S(2)}, u32[]{:S(2)}) collective-permute-start(f32[8,128]{1,0:T(8,128)S(1)} %maximum_maximum_fusion.refs_0_), channel_id=1, source_target_pairs={{0,96},{8,104},{16,112},{24,120},{32,0},{40,8},{48,16},{56,24},{64... | collective-permute-start | bytes 12296 | tf_op jit(solution)/shard_map/ppermute | solution.py:485

commit v10 on v9

--- a/solution.py
+++ b/solution.py
@@ -143,16 +143,7 @@
     raw_ref,
     target_ref,
     moment_ref,
-    first_ref,
-    second_ref,
-    sems,
 ):
-    tables = [
-        pltpu.make_async_copy(a, b, sems.at[k])
-        for k, (a, b) in enumerate(((analysis_ref, first_ref), (synthesis_ref, second_ref)))
-    ]
-    for table in tables:
-        table.start()
     rows, _, cols, points = own_ref.shape
     own = rows * cols
     near = near_ref.shape[0]
@@ -179,11 +170,9 @@
     everything = [pos_ref[d] for d in range(3)]
     centred = [v - jnp.sum(v, axis=1, keepdims=True) * (1.0 / points) for v in everything]
     flat = jnp.concatenate(centred, axis=0).astype(BF16)
-    tables[0].wait()
-    coeff = jnp.dot(flat, first_ref[...], preferred_element_type=F32)
+    coeff = jnp.dot(flat, analysis_ref[...], preferred_element_type=F32)
     scaled = (coeff * stiffness_ref[...]).astype(BF16)
-    tables[1].wait()
-    force = -jnp.dot(scaled, second_ref[...], preferred_element_type=F32)
+    force = -jnp.dot(scaled, synthesis_ref[...], preferred_element_type=F32)
     forces = [force[d * slots : (d + 1) * slots] for d in range(3)]
     for g in range((near + wall) // 8):
         a = own + 8 * g
@@ -204,7 +193,7 @@
         put_rows(moment_ref, c, 16, own, moments)
         return carry
 
-    lax.fori_loop(0, own, cell, 0, unroll=2)
+    lax.fori_loop(0, own, cell, 0, unroll=4)
     moments = [get_rows(moment_ref, k * own, own) for k in range(15)]
     own_pos = [v[0:own] for v in everything]
     sums = stokes_finish(own_pos, moments)
@@ -226,11 +215,10 @@
     tiles = points // LANES
     in_vmem = pl.BlockSpec(memory_space=pltpu.VMEM)
     in_smem = pl.BlockSpec(memory_space=pltpu.SMEM)
-    in_hbm = pl.BlockSpec(memory_space=pl.ANY)
     pairs = own * points * (near // own) * points
     return pl.pallas_call(
         near_kernel,
-        in_specs=[in_smem] * 2 + [in_vmem] * 8 + [in_hbm, in_vmem, in_hbm],
+        in_specs=[in_smem] * 2 + [in_vmem] * 11,
         out_specs=[in_vmem] * 3,
         out_shape=[
             jax.ShapeDtypeStruct((rows, 3, cols, points), F32),
@@ -243,11 +231,8 @@
             pltpu.VMEM((tiles, near * STOKES_ROWS, LANES), F32),
             pltpu.VMEM((tiles, own * 8, LANES), F32),
             pltpu.VMEM((tiles, own * 16, LANES), F32),
-            pltpu.VMEM(tables[0].shape, BF16),
-            pltpu.VMEM(tables[2].shape, BF16),
-            pltpu.SemaphoreType.DMA((2,)),
         ],
-        compiler_params=pltpu.CompilerParams(vmem_limit_bytes=50 * 2**20),
+        compiler_params=pltpu.CompilerParams(vmem_limit_bytes=32 * 2**20),
         cost_estimate=pl.CostEstimate(
             flops=1000 * pairs, bytes_accessed=8 * 2**20, transcendentals=pairs
         ),

time: 87.6 us -> 89.1 us (1.017)
  local copies, waits for them, and re-layouts: 2.43 us -> 4.81 us
  Pallas kernels: 52.3 us -> 50.4 us
  other arithmetic: 1.72 us -> 3.17 us
    pallas_call x1, Pallas kernels: 37.3 us -> 35.4 us  [near_part(): pl.pallas_call(near_kernel, in_specs=[in_smem] * 2 + [in_vmem] * 11, out_...]
    unnamed x11 -> x15, local copies, waits for them, and re-layouts: 0.78 us -> 2.37 us
    concatenate x2, other arithmetic: 0.15 us -> 1.6 us  [body(): jnp.concatenate([v[:, :, c:c + HALO] for v in (below[rows - HALO:], above...]
  transfers between devices with their start and end apart: 18 -> 18, of which waited for: 1 -> 1; matrix products, arithmetic and copies ran while one was open for 5% -> 7% of each run, Pallas kernels for 59% -> 56%
where the time goes in v10:
time: 89.1 us; the launch traced here: 88.8 us
  Pallas kernels  50.4 us (57%)
  starting transfers between devices  28.3 us (32%)
  local copies, waits for them, and re-layouts  4.81 us (5%)
  other arithmetic  3.17 us (4%)
  waiting for transfers between devices  1.2 us (1%)
    pallas_call x1, Pallas kernels, near_part(): pl.pallas_call(near_kernel, in_specs=[in_smem] * 2 + [in_vmem] * 11, out_...  35.4 us
    ppermute x8, starting transfers between devices, neighbours(): return (lax.ppermute(high, axis, up), lax.ppermute(low, axis, down))  17.4 us
    ppermute x10, starting transfers between devices, over_all(): lax.ppermute(value, axis, pairs)  10.9 us
    pallas_call x2, Pallas kernels, layer_part(): pl.pallas_call(kernel, in_specs=[in_smem] * len(scalars) + [in_vmem] * le...  8.5 us
    pallas_call x2, Pallas kernels, wall_part(): pl.pallas_call(functools.partial(wall_kernel, stage, per), in_specs=[in_v...  5.74 us
    unnamed x15, local copies, waits for them, and re-layouts  2.37 us
    slice x1, local copies, waits for them, and re-layouts, body(): pos[:, :, :HALO]  1.85 us
  transfers between devices with their start and end apart: 18, of which 1 were waited for; matrix products, arithmetic and copies ran while one was open for 7% of the time, Pallas kernels for 56%

profile of v10, /device:TPU:0, one launch (start us, length us, event | category | flops | bytes accessed | tf_op | source)
XLA Modules:
  0.0 88.8 jit_solution(2565761190520345351)
XLA Ops:
  0.6 1.6 %collective-permute-start = (f32[4,3,4,1024]{3,2,1,0:T(4,128)}, f32[4,3,4,1024]{3,2,1,0:T(4,128)S(1)}, u32[]{:S(2)}, u32[]{:S(2)}) collective-permute-start(f32[4,3,4,1024]{3,2,1,0:T(4,128)} %bitcast.8), channel_id=1, source_target_pairs={{0,8},{8,16},{16,24},{24,32},{32,40},{40,48},{48,56},{56,64},{64,7... | collective-permute-start | bytes 589832 | tf_op jit(solution)/shard_map/ppermute | solution.py:447
  2.3 4.8 %collective-permute-start.1 = (f32[4,3,4,1024]{3,2,1,0:T(4,128)}, f32[4,3,4,1024]{3,2,1,0:T(4,128)S(1)}, u32[]{:S(2)}, u32[]{:S(2)}) collective-permute-start(f32[4,3,4,1024]{3,2,1,0:T(4,128)} %bitcast.9), channel_id=1, source_target_pairs={{8,0},{16,8},{24,16},{32,24},{40,32},{48,40},{56,48},{64,56},{72,6... | collective-permute-start | bytes 589832 | tf_op jit(solution)/shard_map/ppermute | solution.py:447
  7.1 1.8 %fusion.13 = (f32[4,3,3,1024]{3,2,1,0:T(4,128)}, f32[4,3,3,1024]{3,2,1,0:T(4,128)}) fusion(f32[4,3,4,1024]{3,2,1,0:T(4,128)} %bitcast.10), kind=kLoop, calls=%fused_computation.43 | loop fusion | bytes 589824 | tf_op jit(solution)/shard_map/slice | solution.py:501
  9.0 3.0 %collective-permute-start.4 = (f32[4,3,3,1024]{3,2,1,0:T(4,128)}, f32[4,3,3,1024]{3,2,1,0:T(4,128)}, u32[]{:S(2)}, u32[]{:S(2)}) collective-permute-start(f32[4,3,3,1024]{3,2,1,0:T(4,128)} %get-tuple-element.32), channel_id=1, source_target_pairs={{1,0},{2,1},{3,2},{4,3},{5,4},{6,5},{7,6},{0,7},{9,8},{10,9},{11,1... | collective-permute-start | bytes 442376 | tf_op jit(solution)/shard_map/ppermute | solution.py:447
  11.9 0.8 copy.21
  12.7 0.8 pad_maximum_fusion.2.own_ref
  13.5 0.7 fusion
  14.3 0.2 fusion.11
  14.4 0.8 pad_maximum_fusion.1
  15.2 0.2 collective-permute-start.5
  15.4 0.8 pad_maximum_fusion
  16.2 0.3 collective-permute-start.3
  16.6 0.1 copy.18
  16.7 0.1 reshape.13.near_ref
  16.8 0.1 copy.19
  16.9 0.1 reshape.14.wall_ref
  16.9 0.1 reshape.16.drag_ref
  17.0 2.2 %layer_first.1 = (f32[3,8,256]{2,1,0:T(8,128)S(1)}, bf16[8,192,256]{2,1,0:T(8,128)(2,1)S(1)}, bf16[8,32,256]{2,1,0:T(8,128)(2,1)S(1)}) custom-call(f32[10,8,256]{2,1,0:T(8,128)S(1)} %pad_maximum_fusion.2.own_ref), custom_call_target="tpu_custom_call" | custom-call | flops 524288000 | bytes 1048576 | tf_op jit(solution)/shard_map/layer_first/pallas_call | solution.py:407
  19.2 7.4 %collective-permute-start.17 = (f32[10,8,256]{2,1,0:T(8,128)S(1)}, f32[10,8,256]{2,1,0:T(8,128)S(1)}, u32[]{:S(2)}, u32[]{:S(2)}) collective-permute-start(f32[10,8,256]{2,1,0:T(8,128)S(1)} %pad_maximum_fusion.2.own_ref), channel_id=1, source_target_pairs={{1,0},{2,1},{3,2},{4,3},{5,4},{6,5},{7,6},{8,7},{9,8},{10,9},{11,1... | collective-permute-start | bytes 245768 | tf_op jit(solution)/shard_map/ppermute | solution.py:447
  26.7 1.6 %copy-done.3 = bf16[1024,1024]{1,0:T(8,128)(2,1)S(1)} copy-done((bf16[1024,1024]{1,0:T(8,128)(2,1)S(1)}, bf16[1024,1024]{1,0:T(8,128)(2,1)}, u32[]{:S(2)}) %copy-start.3) | copy-done | bytes 2097176
  28.3 35.4 %near.1 = (f32[4,3,4,1024]{3,2,1,0:T(4,128)S(1)}, f32[8,128]{1,0:T(8,128)S(1)}, f32[8,384,128]{2,1,0:T(8,128)S(1)}) custom-call(s32[32]{0:T(128)S(1)} %reshape.13.near_ref, s32[16]{0:T(128)S(1)} %reshape.14.wall_ref, f32[4,3,4,1024]{3,2,1,0:T(4,128)S(1)} %collective-permute-done.below_ref, f32[4,3,4,1024]{3,2,1,0:T(4,128)S(1)} %bitcast.11, ...), custom_call_target="tpu_custom_call" | custom-call | flops 33554432000 | bytes 8388608 | tf_op jit(solution)/shard_map/near/pallas_call | solution.py:219
  63.7 0.1 collective-permute-start.6
  63.8 1.2 %collective-permute-done.6 = f32[8,128]{1,0:T(8,128)S(1)} collective-permute-done((f32[8,128]{1,0:T(8,128)S(1)}, f32[8,128]{1,0:T(8,128)S(1)}, u32[]{:S(2)}, u32[]{:S(2)}) %collective-permute-start.6) | collective-permute-done | bytes 4128 | tf_op jit(solution)/shard_map/ppermute | solution.py:470
  64.9 3.2 %collective-permute-start.9 = (f32[8,128]{1,0:T(8,128)S(1)}, f32[8,128]{1,0:T(8,128)S(1)}, u32[]{:S(2)}, u32[]{:S(2)}) collective-permute-start(f32[8,128]{1,0:T(8,128)S(1)} %max.21), channel_id=1, source_target_pairs={{0,6},{1,7},{2,0},{3,1},{4,2},{5,3},{6,4},{7,5},{8,14},{9,15},{10,... | collective-permute-start | bytes 12296 | tf_op jit(solution)/shard_map/ppermute | solution.py:470
  68.2 6.3 %layer_second.1.layer_ref = f32[3,8,256]{2,1,0:T(8,128)S(1)} custom-call(s32[8,4]{1,0:T(8,128)S(1)} %add_select_fusion.listed_ref, f32[10,8,256]{2,1,0:T(8,128)S(1)} %pad_maximum_fusion.2.own_ref, f32[10,8,256]{2,1,0:T(8,128)S(1)} %collective-permute-done.16.before_ref, f32[10,8,256]{2,1,0:T(8,128)S(1)} %collective-permute-done.17.after_ref, ...), custom_call_target="tpu_custom_call" | custom-call | flops 2097152000 | bytes 1048576 | tf_op jit(solution)/shard_map/layer_second/pallas_call | solution.py:407
  74.7 0.3 collective-permute-start.11
  75.0 2.9 %collective-permute-start.12 = (f32[8,128]{1,0:T(8,128)S(1)}, f32[8,128]{1,0:T(8,128)S(1)}, u32[]{:S(2)}, u32[]{:S(2)}) collective-permute-start(f32[8,128]{1,0:T(8,128)S(1)} %maximum_maximum_fusion.1), channel_id=1, source_target_pairs={{0,24},{8,0},{16,8},{24,16},{32,56},{40,32},{48,40},{56,48},{64,88... | collective-permute-start | bytes 12296 | tf_op jit(solution)/shard_map/ppermute | solution.py:470
  77.9 2.6 %wall_0.1.layer_ref = f32[3,8,256]{2,1,0:T(8,128)S(1)} custom-call(f32[8,384,128]{2,1,0:T(8,128)S(1)} %get-tuple-element.23.raw_ref, f32[3,8,256]{2,1,0:T(8,128)S(1)} %bitcast.14, f32[3,8,256]{2,1,0:T(8,128)S(1)} %layer_second.1.layer_ref), custom_call_target="tpu_custom_call" | custom-call | flops 2097152000 | bytes 2097152 | tf_op jit(solution)/shard_map/wall_0/pallas_call | solution.py:265
  80.6 3.6 %collective-permute-start.14 = (f32[8,128]{1,0:T(8,128)S(1)}, f32[8,128]{1,0:T(8,128)S(1)}, u32[]{:S(2)}, u32[]{:S(2)}) collective-permute-start(f32[8,128]{1,0:T(8,128)S(1)} %maximum_maximum_fusion.refs_0_), channel_id=1, source_target_pairs={{0,64},{8,72},{16,80},{24,88},{32,96},{40,104},{48,112},{56,120},{... | collective-permute-start | bytes 12296 | tf_op jit(solution)/shard_map/ppermute | solution.py:470
  84.2 0.7 collective-permute-start.15
  84.8 3.2 %wall_1.1 = f32[3,8,256]{2,1,0:T(8,128)} custom-call(f32[8,384,128]{2,1,0:T(8,128)S(1)} %get-tuple-element.23.raw_ref, f32[3,8,256]{2,1,0:T(8,128)S(1)} %bitcast.15, f32[3,8,256]{2,1,0:T(8,128)S(1)} %wall_0.1.layer_ref), custom_call_target="tpu_custom_call" | custom-call | flops 2097152000 | bytes 2097152 | tf_op jit(solution)/shard_map/wall_1/pallas_call | solution.py:265
  88.0 0.7 move.1
  (41 shorter events, 0.3 us)
Async XLA Ops:
  0.6 15.9 %copy-start.6 = (s32[8,2]{0,1:T(2,128)S(1)}, s32[8,2]{0,1:T(2,128)}, u32[]{:S(2)}) copy-start(s32[8,2]{0,1:T(2,128)} %param.23) | copy-start | bytes 196
  0.6 16.3 %copy-start.5 = (f32[4,4]{1,0:T(4,128)S(1)}, f32[4,4]{1,0:T(4,128)}, u32[]{:S(2)}) copy-start(f32[4,4]{1,0:T(4,128)} %param.13) | copy-start | bytes 196
  0.6 13.6 %collective-permute-start = (f32[4,3,4,1024]{3,2,1,0:T(4,128)}, f32[4,3,4,1024]{3,2,1,0:T(4,128)S(1)}, u32[]{:S(2)}, u32[]{:S(2)}) collective-permute-start(f32[4,3,4,1024]{3,2,1,0:T(4,128)} %bitcast.8), channel_id=1, source_target_pairs={{0,8},{8,16},{16,24},{24,32},{32,40},{40,48},{48,56},{56,64},{64,7... | collective-permute-start | bytes 589832 | tf_op jit(solution)/shard_map/ppermute | solution.py:447
  2.3 12.0 %collective-permute-start.1 = (f32[4,3,4,1024]{3,2,1,0:T(4,128)}, f32[4,3,4,1024]{3,2,1,0:T(4,128)S(1)}, u32[]{:S(2)}, u32[]{:S(2)}) collective-permute-start(f32[4,3,4,1024]{3,2,1,0:T(4,128)} %bitcast.9), channel_id=1, source_target_pairs={{8,0},{16,8},{24,16},{32,24},{40,32},{48,40},{56,48},{64,56},{72,6... | collective-permute-start | bytes 589832 | tf_op jit(solution)/shard_map/ppermute | solution.py:447
  9.0 10.2 %collective-permute-start.2 = (f32[4,3,3,1024]{3,2,1,0:T(4,128)}, f32[4,3,3,1024]{3,2,1,0:T(4,128)}, u32[]{:S(2)}, u32[]{:S(2)}) collective-permute-start(f32[4,3,3,1024]{3,2,1,0:T(4,128)} %get-tuple-element.33), channel_id=1, source_target_pairs={{0,1},{1,2},{2,3},{3,4},{4,5},{5,6},{6,7},{7,0},{8,9},{9,10},{10,1... | collective-permute-start | bytes 442376 | tf_op jit(solution)/shard_map/ppermute | solution.py:447
  9.0 17.6 %collective-permute-start.4 = (f32[4,3,3,1024]{3,2,1,0:T(4,128)}, f32[4,3,3,1024]{3,2,1,0:T(4,128)}, u32[]{:S(2)}, u32[]{:S(2)}) collective-permute-start(f32[4,3,3,1024]{3,2,1,0:T(4,128)} %get-tuple-element.32), channel_id=1, source_target_pairs={{1,0},{2,1},{3,2},{4,3},{5,4},{6,5},{7,6},{0,7},{9,8},{10,9},{11,1... | collective-permute-start | bytes 442376 | tf_op jit(solution)/shard_map/ppermute | solution.py:447
  14.2 12.4 %copy-start = (f32[4,4,3,1024]{3,1,2,0:T(4,128)S(1)}, f32[4,4,3,1024]{3,1,2,0:T(4,128)}, u32[]{:S(2)}) copy-start(f32[4,4,3,1024]{3,1,2,0:T(4,128)} %param.12) | copy-start | bytes 589828
  14.2 12.4 %copy-start.2 = (bf16[1024,1024]{1,0:T(8,128)(2,1)S(1)}, bf16[1024,1024]{1,0:T(8,128)(2,1)}, u32[]{:S(2)}) copy-start(bf16[1024,1024]{1,0:T(8,128)(2,1)} %analysis_ref.1) | copy-start | bytes 6291460
  14.2 12.4 %copy-start.4 = (f32[1024]{0:T(1024)S(1)}, f32[1024]{0:T(1024)}, u32[]{:S(2)}) copy-start(f32[1024]{0:T(1024)} %param.16) | copy-start | bytes 12292
  15.2 11.4 %collective-permute-start.5 = (f32[6,3,3,1024]{3,2,1,0:T(4,128)}, f32[6,3,3,1024]{3,2,1,0:T(4,128)S(1)}, u32[]{:S(2)}, u32[]{:S(2)}) collective-permute-start(f32[6,3,3,1024]{3,2,1,0:T(4,128)} %pad_maximum_fusion.1), channel_id=1, source_target_pairs={{1,0},{2,1},{3,2},{4,3},{5,4},{6,5},{7,6},{0,7},{9,8},{10,9},{11,1... | collective-permute-start | bytes 663560 | tf_op jit(solution)/shard_map/ppermute | solution.py:447
  16.2 10.4 %collective-permute-start.3 = (f32[6,3,3,1024]{3,2,1,0:T(4,128)}, f32[6,3,3,1024]{3,2,1,0:T(4,128)S(1)}, u32[]{:S(2)}, u32[]{:S(2)}) collective-permute-start(f32[6,3,3,1024]{3,2,1,0:T(4,128)} %pad_maximum_fusion), channel_id=1, source_target_pairs={{0,1},{1,2},{2,3},{3,4},{4,5},{5,6},{6,7},{7,0},{8,9},{9,10},{10,1... | collective-permute-start | bytes 663560 | tf_op jit(solution)/shard_map/ppermute | solution.py:447
  17.0 51.2 %collective-permute-start.16 = (f32[10,8,256]{2,1,0:T(8,128)S(1)}, f32[10,8,256]{2,1,0:T(8,128)S(1)}, u32[]{:S(2)}, u32[]{:S(2)}) collective-permute-start(f32[10,8,256]{2,1,0:T(8,128)S(1)} %pad_maximum_fusion.2.own_ref), channel_id=1, source_target_pairs={{0,1},{1,2},{2,3},{3,4},{4,5},{5,6},{6,7},{7,8},{8,9},{9,10},{10,1... | collective-permute-start | bytes 245768 | tf_op jit(solution)/shard_map/ppermute | solution.py:447
  19.2 49.0 %collective-permute-start.17 = (f32[10,8,256]{2,1,0:T(8,128)S(1)}, f32[10,8,256]{2,1,0:T(8,128)S(1)}, u32[]{:S(2)}, u32[]{:S(2)}) collective-permute-start(f32[10,8,256]{2,1,0:T(8,128)S(1)} %pad_maximum_fusion.2.own_ref), channel_id=1, source_target_pairs={{1,0},{2,1},{3,2},{4,3},{5,4},{6,5},{7,6},{8,7},{9,8},{10,9},{11,1... | collective-permute-start | bytes 245768 | tf_op jit(solution)/shard_map/ppermute | solution.py:447
  26.7 1.6 %copy-start.3 = (bf16[1024,1024]{1,0:T(8,128)(2,1)S(1)}, bf16[1024,1024]{1,0:T(8,128)(2,1)}, u32[]{:S(2)}) copy-start(bf16[1024,1024]{1,0:T(8,128)(2,1)} %synthesis_ref.1) | copy-start | bytes 6291460
  63.7 1.2 %collective-permute-start.6 = (f32[8,128]{1,0:T(8,128)S(1)}, f32[8,128]{1,0:T(8,128)S(1)}, u32[]{:S(2)}, u32[]{:S(2)}) collective-permute-start(f32[8,128]{1,0:T(8,128)S(1)} %get-tuple-element.21), channel_id=1, source_target_pairs={{0,1},{1,0},{2,3},{3,2},{4,5},{5,4},{6,7},{7,6},{8,9},{9,8},{10,11... | collective-permute-start | bytes 12296 | tf_op jit(solution)/shard_map/ppermute | solution.py:470
  64.9 9.6 %collective-permute-start.7 = (f32[8,128]{1,0:T(8,128)S(1)}, f32[8,128]{1,0:T(8,128)S(1)}, u32[]{:S(2)}, u32[]{:S(2)}) collective-permute-start(f32[8,128]{1,0:T(8,128)S(1)} %max.21), channel_id=1, source_target_pairs={{0,2},{1,3},{2,4},{3,5},{4,6},{5,7},{6,0},{7,1},{8,10},{9,11},{10,... | collective-permute-start | bytes 12296 | tf_op jit(solution)/shard_map/ppermute | solution.py:470
  64.9 9.6 %collective-permute-start.8 = (f32[8,128]{1,0:T(8,128)S(1)}, f32[8,128]{1,0:T(8,128)S(1)}, u32[]{:S(2)}, u32[]{:S(2)}) collective-permute-start(f32[8,128]{1,0:T(8,128)S(1)} %max.21), channel_id=1, source_target_pairs={{0,4},{1,5},{2,6},{3,7},{4,0},{5,1},{6,2},{7,3},{8,12},{9,13},{10,... | collective-permute-start | bytes 12296 | tf_op jit(solution)/shard_map/ppermute | solution.py:470
  64.9 9.6 %collective-permute-start.9 = (f32[8,128]{1,0:T(8,128)S(1)}, f32[8,128]{1,0:T(8,128)S(1)}, u32[]{:S(2)}, u32[]{:S(2)}) collective-permute-start(f32[8,128]{1,0:T(8,128)S(1)} %max.21), channel_id=1, source_target_pairs={{0,6},{1,7},{2,0},{3,1},{4,2},{5,3},{6,4},{7,5},{8,14},{9,15},{10,... | collective-permute-start | bytes 12296 | tf_op jit(solution)/shard_map/ppermute | solution.py:470
  68.2 9.7 %copy-start.1 = (f32[8,3,256]{2,0,1:T(8,128)S(1)}, f32[8,3,256]{2,0,1:T(8,128)}, u32[]{:S(2)}) copy-start(f32[8,3,256]{2,0,1:T(8,128)} %param.18) | copy-start | bytes 73732
  74.6 5.9 %collective-permute-start.10 = (f32[8,128]{1,0:T(8,128)S(1)}, f32[8,128]{1,0:T(8,128)S(1)}, u32[]{:S(2)}, u32[]{:S(2)}) collective-permute-start(f32[8,128]{1,0:T(8,128)S(1)} %maximum_maximum_fusion.1), channel_id=1, source_target_pairs={{0,8},{8,16},{16,24},{24,0},{32,40},{40,48},{48,56},{56,32},{64,72... | collective-permute-start | bytes 12296 | tf_op jit(solution)/shard_map/ppermute | solution.py:470
  74.7 5.8 %collective-permute-start.11 = (f32[8,128]{1,0:T(8,128)S(1)}, f32[8,128]{1,0:T(8,128)S(1)}, u32[]{:S(2)}, u32[]{:S(2)}) collective-permute-start(f32[8,128]{1,0:T(8,128)S(1)} %maximum_maximum_fusion.1), channel_id=1, source_target_pairs={{0,16},{8,24},{16,0},{24,8},{32,48},{40,56},{48,32},{56,40},{64,80... | collective-permute-start | bytes 12296 | tf_op jit(solution)/shard_map/ppermute | solution.py:470
  75.0 5.5 %collective-permute-start.12 = (f32[8,128]{1,0:T(8,128)S(1)}, f32[8,128]{1,0:T(8,128)S(1)}, u32[]{:S(2)}, u32[]{:S(2)}) collective-permute-start(f32[8,128]{1,0:T(8,128)S(1)} %maximum_maximum_fusion.1), channel_id=1, source_target_pairs={{0,24},{8,0},{16,8},{24,16},{32,56},{40,32},{48,40},{56,48},{64,88... | collective-permute-start | bytes 12296 | tf_op jit(solution)/shard_map/ppermute | solution.py:470
  80.5 7.5 %collective-permute-start.13 = (f32[8,128]{1,0:T(8,128)S(1)}, f32[8,128]{1,0:T(8,128)S(1)}, u32[]{:S(2)}, u32[]{:S(2)}) collective-permute-start(f32[8,128]{1,0:T(8,128)S(1)} %maximum_maximum_fusion.refs_0_), channel_id=1, source_target_pairs={{0,32},{8,40},{16,48},{24,56},{32,64},{40,72},{48,80},{56,88},{64,... | collective-permute-start | bytes 12296 | tf_op jit(solution)/shard_map/ppermute | solution.py:470
  80.6 7.4 %collective-permute-start.14 = (f32[8,128]{1,0:T(8,128)S(1)}, f32[8,128]{1,0:T(8,128)S(1)}, u32[]{:S(2)}, u32[]{:S(2)}) collective-permute-start(f32[8,128]{1,0:T(8,128)S(1)} %maximum_maximum_fusion.refs_0_), channel_id=1, source_target_pairs={{0,64},{8,72},{16,80},{24,88},{32,96},{40,104},{48,112},{56,120},{... | collective-permute-start | bytes 12296 | tf_op jit(solution)/shard_map/ppermute | solution.py:470
  84.2 3.8 %collective-permute-start.15 = (f32[8,128]{1,0:T(8,128)S(1)}, f32[8,128]{1,0:T(8,128)S(1)}, u32[]{:S(2)}, u32[]{:S(2)}) collective-permute-start(f32[8,128]{1,0:T(8,128)S(1)} %maximum_maximum_fusion.refs_0_), channel_id=1, source_target_pairs={{0,96},{8,104},{16,112},{24,120},{32,0},{40,8},{48,16},{56,24},{64... | collective-permute-start | bytes 12296 | tf_op jit(solution)/shard_map/ppermute | solution.py:470

commit v11 on v9

--- a/solution.py
+++ b/solution.py
@@ -204,7 +204,7 @@
         put_rows(moment_ref, c, 16, own, moments)
         return carry
 
-    lax.fori_loop(0, own, cell, 0, unroll=2)
+    lax.fori_loop(0, own, cell, 0, unroll=4)
     moments = [get_rows(moment_ref, k * own, own) for k in range(15)]
     own_pos = [v[0:own] for v in everything]
     sums = stokes_finish(own_pos, moments)
@@ -355,7 +355,7 @@
             feature_ref[first + i] = jnp.concatenate(split, axis=0).astype(BF16)
             return carry
 
-        lax.fori_loop(0, patches, prepare, 0, unroll=4)
+        lax.fori_loop(0, patches, prepare, 0, unroll=True)
 
 
 def layer_first(own_ref, out_ref, left_ref, feature_ref, raw_ref, target_ref, moment_ref):

time: 87.6 us -> 87.1 us (level)
  no operation moved by 1% of the time
where the time goes in v11:
time: 87.1 us; the launch traced here: 86.9 us
  Pallas kernels  51.7 us (59%)
  starting transfers between devices  28.9 us (33%)
  local copies, waits for them, and re-layouts  2.43 us (3%)
  other arithmetic  1.72 us (2%)
  waiting for transfers between devices  1.2 us (1%)
  between operations  0.9 us (1%)
    pallas_call x1, Pallas kernels, near_part(): pl.pallas_call(near_kernel, in_specs=[in_smem] * 2 + [in_vmem] * 8 + [in_...  36.8 us
    ppermute x8, starting transfers between devices, neighbours(): return (lax.ppermute(high, axis, up), lax.ppermute(low, axis, down))  17.4 us
    ppermute x10, starting transfers between devices, over_all(): lax.ppermute(value, axis, pairs)  11.5 us
    pallas_call x2, Pallas kernels, layer_part(): pl.pallas_call(kernel, in_specs=[in_smem] * len(scalars) + [in_vmem] * le...  8.37 us
    pallas_call x2, Pallas kernels, wall_part(): pl.pallas_call(functools.partial(wall_kernel, stage, per), in_specs=[in_v...  5.73 us
  transfers between devices with their start and end apart: 18, of which 1 were waited for; matrix products, arithmetic and copies ran while one was open for 5% of the time, Pallas kernels for 59%

profile of v11, /device:TPU:0, one launch (start us, length us, event | category | flops | bytes accessed | tf_op | source)
XLA Modules:
  0.0 86.9 jit_solution(12222080644423027311)
XLA Ops:
  0.6 1.6 %collective-permute-start = (f32[4,3,4,1024]{3,2,1,0:T(4,128)}, f32[4,3,4,1024]{3,2,1,0:T(4,128)S(1)}, u32[]{:S(2)}, u32[]{:S(2)}) collective-permute-start(f32[4,3,4,1024]{3,2,1,0:T(4,128)} %bitcast.8), channel_id=1, source_target_pairs={{0,8},{8,16},{16,24},{24,32},{32,40},{40,48},{48,56},{56,64},{64,7... | collective-permute-start | bytes 589832 | tf_op jit(solution)/shard_map/ppermute | solution.py:462
  2.3 4.8 %collective-permute-start.1 = (f32[4,3,4,1024]{3,2,1,0:T(4,128)}, f32[4,3,4,1024]{3,2,1,0:T(4,128)S(1)}, u32[]{:S(2)}, u32[]{:S(2)}) collective-permute-start(f32[4,3,4,1024]{3,2,1,0:T(4,128)} %bitcast.9), channel_id=1, source_target_pairs={{8,0},{16,8},{24,16},{32,24},{40,32},{48,40},{56,48},{64,56},{72,6... | collective-permute-start | bytes 589832 | tf_op jit(solution)/shard_map/ppermute | solution.py:462
  7.1 1.1 %fusion.13 = (f32[4,3,3,1024]{3,2,1,0:T(4,128)S(1)}, f32[4,3,3,1024]{3,2,1,0:T(4,128)S(1)}) fusion(f32[4,3,4,1024]{3,2,1,0:T(4,128)} %bitcast.10), kind=kLoop, calls=%fused_computation.43 | loop fusion | bytes 589824 | tf_op jit(solution)/shard_map/slice | solution.py:516
  8.2 2.9 %collective-permute-start.4 = (f32[4,3,3,1024]{3,2,1,0:T(4,128)S(1)}, f32[4,3,3,1024]{3,2,1,0:T(4,128)S(1)}, u32[]{:S(2)}, u32[]{:S(2)}) collective-permute-start(f32[4,3,3,1024]{3,2,1,0:T(4,128)S(1)} %get-tuple-element.32), channel_id=1, source_target_pairs={{1,0},{2,1},{3,2},{4,3},{5,4},{6,5},{7,6},{0,7},{9,8},{10,9},{11,1... | collective-permute-start | bytes 442376 | tf_op jit(solution)/shard_map/ppermute | solution.py:462
  11.2 0.8 copy.21
  12.0 0.8 pad_maximum_fusion.2.own_ref
  12.8 0.7 fusion
  13.5 0.1 fusion.11
  13.7 0.1 pad_maximum_fusion.1
  13.7 0.5 collective-permute-start.5
  14.3 0.1 pad_maximum_fusion
  14.4 0.1 copy.18
  14.5 0.1 reshape.13.near_ref
  14.6 0.1 copy.19
  14.7 0.1 reshape.14.wall_ref
  14.8 0.1 reshape.16.drag_ref
  14.9 2.1 %layer_first.1 = (f32[3,8,256]{2,1,0:T(8,128)S(1)}, bf16[8,192,256]{2,1,0:T(8,128)(2,1)S(1)}, bf16[8,32,256]{2,1,0:T(8,128)(2,1)S(1)}) custom-call(f32[10,8,256]{2,1,0:T(8,128)S(1)} %pad_maximum_fusion.2.own_ref), custom_call_target="tpu_custom_call" | custom-call | flops 524288000 | bytes 1048576 | tf_op jit(solution)/shard_map/layer_first/pallas_call | solution.py:422
  16.9 7.4 %collective-permute-start.17 = (f32[10,8,256]{2,1,0:T(8,128)S(1)}, f32[10,8,256]{2,1,0:T(8,128)S(1)}, u32[]{:S(2)}, u32[]{:S(2)}) collective-permute-start(f32[10,8,256]{2,1,0:T(8,128)S(1)} %pad_maximum_fusion.2.own_ref), channel_id=1, source_target_pairs={{1,0},{2,1},{3,2},{4,3},{5,4},{6,5},{7,6},{8,7},{9,8},{10,9},{11,1... | collective-permute-start | bytes 245768 | tf_op jit(solution)/shard_map/ppermute | solution.py:462
  24.4 36.8 %near.1 = (f32[4,3,4,1024]{3,2,1,0:T(4,128)S(1)}, f32[8,128]{1,0:T(8,128)S(1)}, f32[8,384,128]{2,1,0:T(8,128)S(1)}) custom-call(s32[32]{0:T(128)S(1)} %reshape.13.near_ref, s32[16]{0:T(128)S(1)} %reshape.14.wall_ref, f32[4,3,4,1024]{3,2,1,0:T(4,128)S(1)} %collective-permute-done.below_ref, f32[4,3,4,1024]{3,2,1,0:T(4,128)S(1)} %bitcast.11, ...), custom_call_target="tpu_custom_call" | custom-call | flops 33554432000 | bytes 8388608 | tf_op jit(solution)/shard_map/near/pallas_call | solution.py:231
  61.2 0.1 collective-permute-start.6
  61.3 1.2 %collective-permute-done.6 = f32[8,128]{1,0:T(8,128)S(1)} collective-permute-done((f32[8,128]{1,0:T(8,128)S(1)}, f32[8,128]{1,0:T(8,128)S(1)}, u32[]{:S(2)}, u32[]{:S(2)}) %collective-permute-start.6) | collective-permute-done | bytes 4128 | tf_op jit(solution)/shard_map/ppermute | solution.py:485
  62.5 3.2 %collective-permute-start.9 = (f32[8,128]{1,0:T(8,128)S(1)}, f32[8,128]{1,0:T(8,128)S(1)}, u32[]{:S(2)}, u32[]{:S(2)}) collective-permute-start(f32[8,128]{1,0:T(8,128)S(1)} %max.21), channel_id=1, source_target_pairs={{0,6},{1,7},{2,0},{3,1},{4,2},{5,3},{6,4},{7,5},{8,14},{9,15},{10,... | collective-permute-start | bytes 12296 | tf_op jit(solution)/shard_map/ppermute | solution.py:485
  65.7 6.3 %layer_second.1.layer_ref = f32[3,8,256]{2,1,0:T(8,128)S(1)} custom-call(s32[8,4]{1,0:T(8,128)S(1)} %add_select_fusion.listed_ref, f32[10,8,256]{2,1,0:T(8,128)S(1)} %pad_maximum_fusion.2.own_ref, f32[10,8,256]{2,1,0:T(8,128)S(1)} %collective-permute-done.16.before_ref, f32[10,8,256]{2,1,0:T(8,128)S(1)} %collective-permute-done.17.after_ref, ...), custom_call_target="tpu_custom_call" | custom-call | flops 2097152000 | bytes 1048576 | tf_op jit(solution)/shard_map/layer_second/pallas_call | solution.py:422
  72.1 0.1 collective-permute-start.10
  72.2 0.9 %collective-permute-start.11 = (f32[8,128]{1,0:T(8,128)S(1)}, f32[8,128]{1,0:T(8,128)S(1)}, u32[]{:S(2)}, u32[]{:S(2)}) collective-permute-start(f32[8,128]{1,0:T(8,128)S(1)} %maximum_maximum_fusion.1), channel_id=1, source_target_pairs={{0,16},{8,24},{16,0},{24,8},{32,48},{40,56},{48,32},{56,40},{64,80... | collective-permute-start | bytes 12296 | tf_op jit(solution)/shard_map/ppermute | solution.py:485
  73.1 2.3 %collective-permute-start.12 = (f32[8,128]{1,0:T(8,128)S(1)}, f32[8,128]{1,0:T(8,128)S(1)}, u32[]{:S(2)}, u32[]{:S(2)}) collective-permute-start(f32[8,128]{1,0:T(8,128)S(1)} %maximum_maximum_fusion.1), channel_id=1, source_target_pairs={{0,24},{8,0},{16,8},{24,16},{32,56},{40,32},{48,40},{56,48},{64,88... | collective-permute-start | bytes 12296 | tf_op jit(solution)/shard_map/ppermute | solution.py:485
  75.4 2.6 %wall_0.1.layer_ref = f32[3,8,256]{2,1,0:T(8,128)S(1)} custom-call(f32[8,384,128]{2,1,0:T(8,128)S(1)} %get-tuple-element.23.raw_ref, f32[3,8,256]{2,1,0:T(8,128)S(1)} %bitcast.14, f32[3,8,256]{2,1,0:T(8,128)S(1)} %layer_second.1.layer_ref), custom_call_target="tpu_custom_call" | custom-call | flops 2097152000 | bytes 2097152 | tf_op jit(solution)/shard_map/wall_0/pallas_call | solution.py:280
  78.0 0.6 collective-permute-start.13
  78.6 3.6 %collective-permute-start.14 = (f32[8,128]{1,0:T(8,128)S(1)}, f32[8,128]{1,0:T(8,128)S(1)}, u32[]{:S(2)}, u32[]{:S(2)}) collective-permute-start(f32[8,128]{1,0:T(8,128)S(1)} %maximum_maximum_fusion.refs_0_), channel_id=1, source_target_pairs={{0,64},{8,72},{16,80},{24,88},{32,96},{40,104},{48,112},{56,120},{... | collective-permute-start | bytes 12296 | tf_op jit(solution)/shard_map/ppermute | solution.py:485
  82.3 0.7 collective-permute-start.15
  82.9 3.2 %wall_1.1 = f32[3,8,256]{2,1,0:T(8,128)} custom-call(f32[8,384,128]{2,1,0:T(8,128)S(1)} %get-tuple-element.23.raw_ref, f32[3,8,256]{2,1,0:T(8,128)S(1)} %bitcast.15, f32[3,8,256]{2,1,0:T(8,128)S(1)} %wall_0.1.layer_ref), custom_call_target="tpu_custom_call" | custom-call | flops 2097152000 | bytes 2097152 | tf_op jit(solution)/shard_map/wall_1/pallas_call | solution.py:280
  86.1 0.7 move.1
  (37 shorter events, 0.2 us)
Async XLA Ops:
  0.6 13.7 %copy-start.4 = (s32[8,2]{0,1:T(2,128)S(1)}, s32[8,2]{0,1:T(2,128)}, u32[]{:S(2)}) copy-start(s32[8,2]{0,1:T(2,128)} %param.23) | copy-start | bytes 196
  0.6 14.1 %copy-start.3 = (f32[4,4]{1,0:T(4,128)S(1)}, f32[4,4]{1,0:T(4,128)}, u32[]{:S(2)}) copy-start(f32[4,4]{1,0:T(4,128)} %param.13) | copy-start | bytes 196
  0.6 12.9 %collective-permute-start = (f32[4,3,4,1024]{3,2,1,0:T(4,128)}, f32[4,3,4,1024]{3,2,1,0:T(4,128)S(1)}, u32[]{:S(2)}, u32[]{:S(2)}) collective-permute-start(f32[4,3,4,1024]{3,2,1,0:T(4,128)} %bitcast.8), channel_id=1, source_target_pairs={{0,8},{8,16},{16,24},{24,32},{32,40},{40,48},{48,56},{56,64},{64,7... | collective-permute-start | bytes 589832 | tf_op jit(solution)/shard_map/ppermute | solution.py:462
  2.3 11.2 %collective-permute-start.1 = (f32[4,3,4,1024]{3,2,1,0:T(4,128)}, f32[4,3,4,1024]{3,2,1,0:T(4,128)S(1)}, u32[]{:S(2)}, u32[]{:S(2)}) collective-permute-start(f32[4,3,4,1024]{3,2,1,0:T(4,128)} %bitcast.9), channel_id=1, source_target_pairs={{8,0},{16,8},{24,16},{32,24},{40,32},{48,40},{56,48},{64,56},{72,6... | collective-permute-start | bytes 589832 | tf_op jit(solution)/shard_map/ppermute | solution.py:462
  8.2 8.7 %collective-permute-start.2 = (f32[4,3,3,1024]{3,2,1,0:T(4,128)S(1)}, f32[4,3,3,1024]{3,2,1,0:T(4,128)S(1)}, u32[]{:S(2)}, u32[]{:S(2)}) collective-permute-start(f32[4,3,3,1024]{3,2,1,0:T(4,128)S(1)} %get-tuple-element.33), channel_id=1, source_target_pairs={{0,1},{1,2},{2,3},{3,4},{4,5},{5,6},{6,7},{7,0},{8,9},{9,10},{10,1... | collective-permute-start | bytes 442376 | tf_op jit(solution)/shard_map/ppermute | solution.py:462
  8.2 16.1 %collective-permute-start.4 = (f32[4,3,3,1024]{3,2,1,0:T(4,128)S(1)}, f32[4,3,3,1024]{3,2,1,0:T(4,128)S(1)}, u32[]{:S(2)}, u32[]{:S(2)}) collective-permute-start(f32[4,3,3,1024]{3,2,1,0:T(4,128)S(1)} %get-tuple-element.32), channel_id=1, source_target_pairs={{1,0},{2,1},{3,2},{4,3},{5,4},{6,5},{7,6},{0,7},{9,8},{10,9},{11,1... | collective-permute-start | bytes 442376 | tf_op jit(solution)/shard_map/ppermute | solution.py:462
  13.5 10.9 %copy-start = (f32[4,4,3,1024]{3,1,2,0:T(4,128)S(1)}, f32[4,4,3,1024]{3,1,2,0:T(4,128)}, u32[]{:S(2)}) copy-start(f32[4,4,3,1024]{3,1,2,0:T(4,128)} %param.12) | copy-start | bytes 589828
  13.5 10.9 %copy-start.2 = (f32[1024]{0:T(1024)S(1)}, f32[1024]{0:T(1024)}, u32[]{:S(2)}) copy-start(f32[1024]{0:T(1024)} %param.16) | copy-start | bytes 12292
  13.7 10.7 %collective-permute-start.5 = (f32[6,3,3,1024]{3,2,1,0:T(4,128)S(1)}, f32[6,3,3,1024]{3,2,1,0:T(4,128)S(1)}, u32[]{:S(2)}, u32[]{:S(2)}) collective-permute-start(f32[6,3,3,1024]{3,2,1,0:T(4,128)S(1)} %pad_maximum_fusion.1), channel_id=1, source_target_pairs={{1,0},{2,1},{3,2},{4,3},{5,4},{6,5},{7,6},{0,7},{9,8},{10,9},{11,1... | collective-permute-start | bytes 663560 | tf_op jit(solution)/shard_map/ppermute | solution.py:462
  14.3 10.0 %collective-permute-start.3 = (f32[6,3,3,1024]{3,2,1,0:T(4,128)S(1)}, f32[6,3,3,1024]{3,2,1,0:T(4,128)S(1)}, u32[]{:S(2)}, u32[]{:S(2)}) collective-permute-start(f32[6,3,3,1024]{3,2,1,0:T(4,128)S(1)} %pad_maximum_fusion), channel_id=1, source_target_pairs={{0,1},{1,2},{2,3},{3,4},{4,5},{5,6},{6,7},{7,0},{8,9},{9,10},{10,1... | collective-permute-start | bytes 663560 | tf_op jit(solution)/shard_map/ppermute | solution.py:462
  14.9 50.9 %collective-permute-start.16 = (f32[10,8,256]{2,1,0:T(8,128)S(1)}, f32[10,8,256]{2,1,0:T(8,128)S(1)}, u32[]{:S(2)}, u32[]{:S(2)}) collective-permute-start(f32[10,8,256]{2,1,0:T(8,128)S(1)} %pad_maximum_fusion.2.own_ref), channel_id=1, source_target_pairs={{0,1},{1,2},{2,3},{3,4},{4,5},{5,6},{6,7},{7,8},{8,9},{9,10},{10,1... | collective-permute-start | bytes 245768 | tf_op jit(solution)/shard_map/ppermute | solution.py:462
  16.9 48.8 %collective-permute-start.17 = (f32[10,8,256]{2,1,0:T(8,128)S(1)}, f32[10,8,256]{2,1,0:T(8,128)S(1)}, u32[]{:S(2)}, u32[]{:S(2)}) collective-permute-start(f32[10,8,256]{2,1,0:T(8,128)S(1)} %pad_maximum_fusion.2.own_ref), channel_id=1, source_target_pairs={{1,0},{2,1},{3,2},{4,3},{5,4},{6,5},{7,6},{8,7},{9,8},{10,9},{11,1... | collective-permute-start | bytes 245768 | tf_op jit(solution)/shard_map/ppermute | solution.py:462
  61.2 1.2 %collective-permute-start.6 = (f32[8,128]{1,0:T(8,128)S(1)}, f32[8,128]{1,0:T(8,128)S(1)}, u32[]{:S(2)}, u32[]{:S(2)}) collective-permute-start(f32[8,128]{1,0:T(8,128)S(1)} %get-tuple-element.21), channel_id=1, source_target_pairs={{0,1},{1,0},{2,3},{3,2},{4,5},{5,4},{6,7},{7,6},{8,9},{9,8},{10,11... | collective-permute-start | bytes 12296 | tf_op jit(solution)/shard_map/ppermute | solution.py:485
  62.5 9.6 %collective-permute-start.7 = (f32[8,128]{1,0:T(8,128)S(1)}, f32[8,128]{1,0:T(8,128)S(1)}, u32[]{:S(2)}, u32[]{:S(2)}) collective-permute-start(f32[8,128]{1,0:T(8,128)S(1)} %max.21), channel_id=1, source_target_pairs={{0,2},{1,3},{2,4},{3,5},{4,6},{5,7},{6,0},{7,1},{8,10},{9,11},{10,... | collective-permute-start | bytes 12296 | tf_op jit(solution)/shard_map/ppermute | solution.py:485
  62.5 9.6 %collective-permute-start.8 = (f32[8,128]{1,0:T(8,128)S(1)}, f32[8,128]{1,0:T(8,128)S(1)}, u32[]{:S(2)}, u32[]{:S(2)}) collective-permute-start(f32[8,128]{1,0:T(8,128)S(1)} %max.21), channel_id=1, source_target_pairs={{0,4},{1,5},{2,6},{3,7},{4,0},{5,1},{6,2},{7,3},{8,12},{9,13},{10,... | collective-permute-start | bytes 12296 | tf_op jit(solution)/shard_map/ppermute | solution.py:485
  62.5 9.6 %collective-permute-start.9 = (f32[8,128]{1,0:T(8,128)S(1)}, f32[8,128]{1,0:T(8,128)S(1)}, u32[]{:S(2)}, u32[]{:S(2)}) collective-permute-start(f32[8,128]{1,0:T(8,128)S(1)} %max.21), channel_id=1, source_target_pairs={{0,6},{1,7},{2,0},{3,1},{4,2},{5,3},{6,4},{7,5},{8,14},{9,15},{10,... | collective-permute-start | bytes 12296 | tf_op jit(solution)/shard_map/ppermute | solution.py:485
  65.7 9.7 %copy-start.1 = (f32[8,3,256]{2,0,1:T(8,128)S(1)}, f32[8,3,256]{2,0,1:T(8,128)}, u32[]{:S(2)}) copy-start(f32[8,3,256]{2,0,1:T(8,128)} %param.18) | copy-start | bytes 73732
  72.1 5.9 %collective-permute-start.10 = (f32[8,128]{1,0:T(8,128)S(1)}, f32[8,128]{1,0:T(8,128)S(1)}, u32[]{:S(2)}, u32[]{:S(2)}) collective-permute-start(f32[8,128]{1,0:T(8,128)S(1)} %maximum_maximum_fusion.1), channel_id=1, source_target_pairs={{0,8},{8,16},{16,24},{24,0},{32,40},{40,48},{48,56},{56,32},{64,72... | collective-permute-start | bytes 12296 | tf_op jit(solution)/shard_map/ppermute | solution.py:485
  72.2 5.8 %collective-permute-start.11 = (f32[8,128]{1,0:T(8,128)S(1)}, f32[8,128]{1,0:T(8,128)S(1)}, u32[]{:S(2)}, u32[]{:S(2)}) collective-permute-start(f32[8,128]{1,0:T(8,128)S(1)} %maximum_maximum_fusion.1), channel_id=1, source_target_pairs={{0,16},{8,24},{16,0},{24,8},{32,48},{40,56},{48,32},{56,40},{64,80... | collective-permute-start | bytes 12296 | tf_op jit(solution)/shard_map/ppermute | solution.py:485
  73.1 4.9 %collective-permute-start.12 = (f32[8,128]{1,0:T(8,128)S(1)}, f32[8,128]{1,0:T(8,128)S(1)}, u32[]{:S(2)}, u32[]{:S(2)}) collective-permute-start(f32[8,128]{1,0:T(8,128)S(1)} %maximum_maximum_fusion.1), channel_id=1, source_target_pairs={{0,24},{8,0},{16,8},{24,16},{32,56},{40,32},{48,40},{56,48},{64,88... | collective-permute-start | bytes 12296 | tf_op jit(solution)/shard_map/ppermute | solution.py:485
  78.0 8.1 %collective-permute-start.13 = (f32[8,128]{1,0:T(8,128)S(1)}, f32[8,128]{1,0:T(8,128)S(1)}, u32[]{:S(2)}, u32[]{:S(2)}) collective-permute-start(f32[8,128]{1,0:T(8,128)S(1)} %maximum_maximum_fusion.refs_0_), channel_id=1, source_target_pairs={{0,32},{8,40},{16,48},{24,56},{32,64},{40,72},{48,80},{56,88},{64,... | collective-permute-start | bytes 12296 | tf_op jit(solution)/shard_map/ppermute | solution.py:485
  78.6 7.5 %collective-permute-start.14 = (f32[8,128]{1,0:T(8,128)S(1)}, f32[8,128]{1,0:T(8,128)S(1)}, u32[]{:S(2)}, u32[]{:S(2)}) collective-permute-start(f32[8,128]{1,0:T(8,128)S(1)} %maximum_maximum_fusion.refs_0_), channel_id=1, source_target_pairs={{0,64},{8,72},{16,80},{24,88},{32,96},{40,104},{48,112},{56,120},{... | collective-permute-start | bytes 12296 | tf_op jit(solution)/shard_map/ppermute | solution.py:485
  82.3 3.8 %collective-permute-start.15 = (f32[8,128]{1,0:T(8,128)S(1)}, f32[8,128]{1,0:T(8,128)S(1)}, u32[]{:S(2)}, u32[]{:S(2)}) collective-permute-start(f32[8,128]{1,0:T(8,128)S(1)} %maximum_maximum_fusion.refs_0_), channel_id=1, source_target_pairs={{0,96},{8,104},{16,112},{24,120},{32,0},{40,8},{48,16},{56,24},{64... | collective-permute-start | bytes 12296 | tf_op jit(solution)/shard_map/ppermute | solution.py:485
